TPU v7x, 256 devices: a whole 4x4x8 slice. The times are simulated.
256 devices in a mesh: pair: 32 (over z, x), aux: 8 (over y, core).
Axes of the slice: x: 4, y: 4, z: 8, core: 2. Of those that a mesh axis runs over, the one named last changes fastest.
Arguments:
- amplitudes: bfloat16 [128, 128, 128], P('pair'), may hold values from -0.59765625 to 0.59765625
- coefficients: bfloat16 [128, 512, 128], P('pair'), may hold values from -0.375 to 0.375
- energies: float32 [128, 128], P('pair'), may hold values from 0.2 to 3
- pair_shift: float32 [128], P('pair'), may hold values from -3 to -1
- pno_count: int32 [128], P('pair'), may hold values from 64 to 128
- coupled_pairs: int32 [128, 16], P('pair'), may hold values from 0 to 127, as said below
- coupling_weight: float32 [128, 16], P('pair'), may hold values from -1.5 to 1.5
- slab_one: bfloat16 [128, 24576, 128], P('pair', 'aux'), may hold values from -0.47851562 to 0.47851562
- slab_two: bfloat16 [128, 24576, 128], P('pair', 'aux'), may hold values from -0.47851562 to 0.47851562
Outputs:
- residual: float32 [128, 128, 128], P('pair')
Inputs may be any that keep to these rules, and one draw needn't show every extreme that they name: `coupled_pairs`: pair q is owned by index q // 4 of the pair axis. Among the 64 couplings of one owner's pairs, at most 3 name pairs of any one owner, and in every draw exactly 3 of each owner's couplings name pairs of some one owner (two of them may name the same pair).
All inputs are finite; a program needn't handle non-finite values.
Results may differ from a plain program's by a relative error of at most 0.003.
Values may be sent and summed in bfloat16 or wider, within the bound.
No kernel may reach another device: no remote copies, remote signals or barrier semaphores. Data moves between devices by JAX's collectives and lax.ppermute only.
A program may use at most 128 MiB of HBM per device.

v0:
```python
import jax
import jax.numpy as jnp
from jax import lax
from jax.sharding import PartitionSpec as P


def project(own_coef, far_coef, far_amplitude):
    intersection = jnp.einsum(
        "...nv,...nw->...vw", own_coef, far_coef, preferred_element_type=jnp.float32
    ).astype(jnp.bfloat16)
    half_way = jnp.einsum(
        "...ac,...cd->...ad", intersection, far_amplitude, preferred_element_type=jnp.float32
    ).astype(jnp.bfloat16)
    return jnp.einsum(
        "...ad,...bd->...ab", half_way, intersection, preferred_element_type=jnp.float32
    ).astype(jnp.bfloat16)


def slot_layout(link_ids, pair_local, owner_count, slot_width):
    target_owner = link_ids // pair_local
    remote_slot = link_ids % pair_local
    owner_match = (
        target_owner[:, None] == jnp.arange(owner_count, dtype=jnp.int32)[None, :]
    ).astype(jnp.int32)
    earlier = jnp.cumsum(owner_match, axis=0) - owner_match
    position = jnp.sum(earlier * owner_match, axis=1)
    placement_index = target_owner * slot_width + position
    requests = (
        jnp.zeros((owner_count * slot_width,), jnp.int32).at[placement_index].set(remote_slot)
    )
    return (placement_index, requests.reshape(owner_count, slot_width))


def shards(
    amplitudes,
    coefficients,
    energies,
    pair_shift,
    pno_count,
    coupled_pairs,
    coupling_weight,
    slab_one,
    slab_two,
):
    pair_local = amplitudes.shape[0]
    pno_width = amplitudes.shape[1]
    link_count = coupled_pairs.shape[1]
    owner_count = lax.axis_size("pair")
    capacity = max(2, (4 * pair_local * link_count + 3 * owner_count - 1) // (3 * owner_count))
    flat_ids = coupled_pairs.reshape(-1)
    first_copy = (lax.axis_index("aux") == 0).astype(jnp.float32)
    placement_index, requests = slot_layout(flat_ids, pair_local, owner_count, capacity)
    asked_slots = lax.all_to_all(requests, "pair", split_axis=0, concat_axis=0, tiled=True)
    back_amp, back_coef = (
        lax.all_to_all(amplitudes[asked_slots], "pair", split_axis=0, concat_axis=0, tiled=True),
        lax.all_to_all(coefficients[asked_slots], "pair", split_axis=0, concat_axis=0, tiled=True),
    )
    far_amplitude = back_amp.reshape(owner_count * capacity, pno_width, pno_width)[placement_index]
    far_amplitude = far_amplitude.reshape(pair_local, link_count, pno_width, pno_width)
    far_coef = back_coef.reshape(owner_count * capacity, back_coef.shape[2], pno_width)[
        placement_index
    ]
    far_coef = far_coef.reshape(pair_local, link_count, back_coef.shape[2], pno_width)
    own_coef = jnp.broadcast_to(coefficients[:, None], far_coef.shape)
    projected = project(own_coef, far_coef, far_amplitude)
    coupling = jnp.sum(coupling_weight[:, :, None, None] * projected.astype(jnp.float32), axis=1)
    coupling_share = coupling * first_copy
    partial_exchange = jnp.einsum(
        "pqa,pqb->pab", slab_one, slab_two, preferred_element_type=jnp.float32
    )
    amp_float = amplitudes.astype(jnp.float32)
    weighted_one = jnp.einsum(
        "pqc,pca->pqa", slab_one, amplitudes, preferred_element_type=jnp.float32
    )
    weighted_two = jnp.einsum(
        "pqc,pca->pqa", slab_two, amplitudes, preferred_element_type=jnp.float32
    )
    partial_quadratic = jnp.einsum(
        "pqa,pqb->pab", weighted_one, weighted_two, precision=lax.Precision.HIGHEST
    )
    exchange, remainder = lax.psum((partial_exchange, partial_quadratic - coupling_share), "aux")
    diagonal = (energies[:, :, None] + energies[:, None, :] - pair_shift[:, None, None]) * amp_float
    summed = exchange + diagonal + remainder
    inside = jnp.arange(pno_width, dtype=jnp.int32)[None, :] < pno_count[:, None]
    return jnp.where(inside[:, :, None] & inside[:, None, :], summed, jnp.float32(0.0))


def solution(mesh):
    placed = (
        P("pair", None, None),
        P("pair", None, None),
        P("pair", None),
        P("pair"),
        P("pair"),
        P("pair", None),
        P("pair", None),
        P("pair", "aux", None),
        P("pair", "aux", None),
    )
    return jax.shard_map(
        shards, mesh=mesh, in_specs=placed, out_specs=P("pair", None, None), check_vma=False
    )
```

profile of v0, /device:TPU:1, one launch (start us, length us, event | category | flops | bytes accessed | tf_op | source)
XLA Modules:
  0.0 511.0 jit_solution(2344479295162340179)
XLA Ops:
  6.5 0.0 copy-start
  6.5 0.9 reshape.189
  7.5 0.8 reshape.188
  8.3 0.1 fusion.14
  8.3 0.1 reduce_window_sum.11
  8.4 0.2 select_reduce_fusion
  8.6 0.8 scatter_custom_fusion
  9.4 0.1 all_to_all.14
  9.5 20.2 %all_to_all.22 = s32[32,1,3]{2,1,0:T(1,128)S(1)} all-to-all(s32[32,1,3]{2,1,0:T(1,128)S(1)} %bitcast.33), channel_id=1, replica_groups=mesh['pair'=32,'aux'=8] {'pair'}, dimensions={0} | all-to-all | bytes 768 | tf_op jit(solution)/shard_map/all_to_all | solution.py:53
  29.8 0.1 copy.20
  29.9 0.1 copy.21
  30.0 0.1 reshape.196
  30.1 3.6 gather_fusion.2
  33.7 4.8 all-to-all-start.2
  38.5 7.8 %gather_fusion = bf16[96,512,128]{2,1,0:T(8,128)(2,1)} fusion(bf16[4,512,128]{2,1,0:T(8,128)(2,1)} %param.10, s32[1024]{0:T(1024)S(1)} %pad_clamp_fusion.1), kind=kCustom, calls=%fused_computation | custom fusion | bytes 25166208 | tf_op jit(solution)/shard_map/gather | solution.py:56
  46.3 62.3 %all-to-all-done.2 = bf16[32,3,128,128]{3,2,1,0:T(8,128)(2,1)} async-done(((bf16[32,3,128,128]{3,2,1,0:T(8,128)(2,1)}), bf16[32,3,128,128]{3,2,1,0:T(8,128)(2,1)}, u32[]{:S(2)}, u32[]{:S(2)}) %all-to-all-start.2) | async-done | bytes 3145760 | tf_op jit(solution)/shard_map/all_to_all | solution.py:55
  108.6 6.6 %all-to-all-start.1 = ((bf16[32,3,512,128]{3,2,1,0:T(8,128)(2,1)}), bf16[32,3,512,128]{3,2,1,0:T(8,128)(2,1)}, u32[]{:S(2)}, u32[]{:S(2)}) async-start(bf16[32,3,512,128]{3,2,1,0:T(8,128)(2,1)} %bitcast.29), calls=%async_computation.1 | async-start | bytes 25165824 | tf_op jit(solution)/shard_map/all_to_all | solution.py:56
  115.2 0.0 all-reduce.3.cloned.1.call-start
  115.3 0.0 copy-done
  115.3 0.0 copy-start.1
  115.3 3.7 fusion.18
  119.0 0.0 copy-done.1
  119.0 0.0 copy-start.2
  119.0 3.7 fusion.19
  122.7 0.0 copy-done.2
  122.7 3.7 fusion.20
  126.4 4.1 gather_fusion.3
  130.4 260.7 %all-to-all-done.1 = bf16[32,3,512,128]{3,2,1,0:T(8,128)(2,1)} async-done(((bf16[32,3,512,128]{3,2,1,0:T(8,128)(2,1)}), bf16[32,3,512,128]{3,2,1,0:T(8,128)(2,1)}, u32[]{:S(2)}, u32[]{:S(2)}) %all-to-all-start.1) | async-done | bytes 12582944 | tf_op jit(solution)/shard_map/all_to_all | solution.py:56
  391.1 10.3 %gather_fusion.1 = bf16[64,512,128]{2,1,0:T(8,128)(2,1)} fusion(bf16[96,512,128]{2,1,0:T(8,128)(2,1)} %bitcast.5, s32[1024]{0:T(1024)S(1)} %pad_clamp_fusion), kind=kCustom, calls=%fused_computation.1 | custom fusion | bytes 16777472 | tf_op jit(solution)/shard_map/gather | solution.py:60
  401.4 0.0 copy-start.5
  401.4 7.3 %fusion = bf16[4,16,128,128]{3,2,1,0:T(8,128)(2,1)} fusion(bf16[4,16,512,128]{3,2,1,0:T(8,128)(2,1)} %bitcast.31, bf16[4,512,128]{2,1,0:T(8,128)(2,1)} %param.10), kind=kOutput, calls=%fused_computation.6 | convolution fusion | flops 1073741824 | bytes 11010048 | tf_op jit(solution)/shard_map/...nv,...nw->...vw/dot_general | solution.py:8
  408.7 0.0 copy-done.5
  408.7 4.3 multiply_reduce_fusion
  412.9 0.0 copy-start.6
  413.0 0.0 copy-start.3
  413.0 0.0 copy-start.4
  413.0 11.5 %convolution_subtract_fusion = f32[4,128,128]{2,1,0:T(8,128)} fusion(f32[4,3072,128]{1,2,0:T(8,128)} %fusion.19, f32[4,3072,128]{2,1,0:T(8,128)} %fusion.20, f32[4,128,128]{2,1,0:T(8,128)S(1)} %multiply_reduce_fusion, f32[]{:T(128)S(6)} %convert_element_type.28), kind=kOutput, calls=%fused_computation.12 | convolution fusion | flops 2416050176 | bytes 13107204 | tf_op jit(solution)/shard_map/pqa,pqb->pab/dot_general | solution.py:78
  424.5 0.0 all-reduce.3.cloned.1.call-update
  424.5 0.0 copy-done.6
  424.5 0.1 iota_compare_fusion.1
  424.6 77.7 %all-reduce.3.cloned.1.call-done = (f32[4,128,128]{2,1,0:T(8,128)}, f32[4,128,128]{2,1,0:T(8,128)}) async-done(((f32[4,128,128]{2,1,0:T(8,128)}, f32[4,128,128]{2,1,0:T(8,128)}), (f32[4,128,128]{2,1,0:T(8,128)}, f32[4,128,128]{2,1,0:T(8,128)})) %all-reduce.3.cloned.1.call-update) | async-done | bytes 524304 | tf_op jit(solution)/shard_map/psum | solution.py:81
  502.3 0.0 copy-done.3
  502.3 0.0 copy-done.4
  502.3 1.9 add_select_fusion
  (5 shorter events, 0.0 us)
Async XLA Ops:
  6.5 108.8 %copy-start = (bf16[4,3072,128]{2,1,0:T(8,128)(2,1)S(1)}, bf16[4,3072,128]{2,1,0:T(8,128)(2,1)}, u32[]{:S(2)}) copy-start(bf16[4,3072,128]{2,1,0:T(8,128)(2,1)} %param.16) | copy-start | bytes 9437188
  33.7 74.9 %all-to-all-start.2 = ((bf16[32,3,128,128]{3,2,1,0:T(8,128)(2,1)}), bf16[32,3,128,128]{3,2,1,0:T(8,128)(2,1)}, u32[]{:S(2)}, u32[]{:S(2)}) async-start(bf16[32,3,128,128]{3,2,1,0:T(8,128)(2,1)} %bitcast.30), calls=%async_computation.2 | async-start | bytes 6291456 | tf_op jit(solution)/shard_map/all_to_all | solution.py:55
  108.6 282.5 %all-to-all-start.1 = ((bf16[32,3,512,128]{3,2,1,0:T(8,128)(2,1)}), bf16[32,3,512,128]{3,2,1,0:T(8,128)(2,1)}, u32[]{:S(2)}, u32[]{:S(2)}) async-start(bf16[32,3,512,128]{3,2,1,0:T(8,128)(2,1)} %bitcast.29), calls=%async_computation.1 | async-start | bytes 25165824 | tf_op jit(solution)/shard_map/all_to_all | solution.py:56
  115.2 387.0 %all-reduce.3.cloned.1.call-start = ((), (), s32[]{:S(2)}) async-start(), calls=%async_computation.3 | async-start | bytes 1048576 | tf_op jit(solution)/shard_map/psum | solution.py:81
  115.3 3.7 copy-start.1
  119.0 3.7 copy-start.2
  401.4 7.3 %copy-start.5 = (f32[4,16]{1,0:T(4,128)S(1)}, f32[4,16]{1,0:T(4,128)}, u32[]{:S(2)}) copy-start(f32[4,16]{1,0:T(4,128)} %param.15) | copy-start | bytes 772
  412.9 11.5 %copy-start.6 = (s32[4]{0:T(128)S(1)}, s32[4]{0:T(128)}, u32[]{:S(2)}) copy-start(s32[4]{0:T(128)} %param.13) | copy-start | bytes 52
  413.0 89.3 %copy-start.3 = (f32[4,128]{1,0:T(4,128)S(1)}, f32[4,128]{1,0:T(4,128)}, u32[]{:S(2)}) copy-start(f32[4,128]{1,0:T(4,128)} %param.11) | copy-start | bytes 6148
  413.0 89.3 %copy-start.4 = (f32[4]{0:T(128)S(1)}, f32[4]{0:T(128)}, u32[]{:S(2)}) copy-start(f32[4]{0:T(128)} %param.12) | copy-start | bytes 52
Sparse Core Ops, SparseCore 0:
  424.6 77.5 all-reduce.2
where the time goes:
time: 513 us; the launch traced here: 511 us
  waiting for transfers between devices  401 us (78%)
  matrix products  34.1 us (7%)
  local copies, waits for them, and re-layouts  28.6 us (6%)
  blocking collectives  20.2 us (4%)
  between operations  13.5 us (3%)
  starting transfers between devices  11.5 us (2%)
    all_to_all x1, waiting for transfers between devices, shards(): lax.all_to_all(coefficients[asked_slots], 'pair', split_axis=0, concat_ax...  261 us
    psum x1, waiting for transfers between devices, shards(): lax.psum((partial_exchange, partial_quadratic - coupling_share), 'aux')  77.7 us
    all_to_all x1, waiting for transfers between devices, shards(): lax.all_to_all(amplitudes[asked_slots], 'pair', split_axis=0, concat_axis...  62.3 us
    all_to_all x1, blocking collectives, shards(): lax.all_to_all(requests, 'pair', split_axis=0, concat_axis=0, tiled=True)  20.2 us
    dot_general x1, matrix products, shards(): jnp.einsum('pqa,pqb->pab', weighted_one, weighted_two, precision=lax.Prec...  11.5 us
    gather x1, local copies, waits for them, and re-layouts, shards(): back_coef.reshape(owner_count * capacity, back_coef.shape[2], pno_width)  10.3 us
  transfers between devices with their start and end apart: 3, of which 3 were waited for; matrix products, arithmetic and copies ran while one was open for 4% of the time, Pallas kernels for 0%

commit v1 on v0

v1 whole, which is shorter than its diff:
```python
import jax
import jax.numpy as jnp
from jax import lax
from jax.experimental import pallas as pl
from jax.experimental.pallas import tpu as pltpu
from jax.sharding import Mesh
from jax.sharding import PartitionSpec as P

NX, NY, NC = 4, 4, 2
ROWS = 16


def ring(size, step):
    return [(i, (i + step) % size) for i in range(size)]


def prepare_kernel(where, coef, amp, meta, z_out, x_out):
    y, c = where[2], where[3]
    nz = z_out.shape[0]
    half = coef.shape[1] // NC
    amp_half = amp.shape[1] // NC
    v = amp.shape[2]
    coef_part = coef[y, pl.ds(pl.multiple_of(c * half, half), half), :]
    amp_part = amp[y, pl.ds(pl.multiple_of(c * amp_half, amp_half), amp_half), :]
    for d in range(nz):
        z_out[d, :half, :] = coef_part
        z_out[d, half:, :] = amp_part
    for s in range(2):
        x_out[s * v : (s + 1) * v, :] = coef[2 * c + s].T
    x_out[2 * v : 2 * v + ROWS, :] = jnp.zeros((ROWS, x_out.shape[1]), x_out.dtype)
    x_out[2 * v : 2 * v + ROWS, :v] = meta[...]


def couple_kernel(
    where, p0, p1, p2, p3, q_mine, q_other, own, away, meta_f, meta_i, sm_f, sm_i, pick, acc, amp_q, sem
):
    x, y, c = where[1], where[2], where[3]
    v = q_mine.shape[2]
    half = p0.shape[1] // NC
    amp_half = v // NC
    parts = (p0, p1, p2, p3)
    for r, ref in enumerate(parts):
        rows = ref[2 * v : 2 * v + ROWS, :v].astype(jnp.float32)[:8]
        meta_f[r] = rows
        meta_i[r] = rows.astype(jnp.int32)
    copy_f = pltpu.make_async_copy(meta_f, sm_f, sem.at[0])
    copy_i = pltpu.make_async_copy(meta_i, sm_i, sem.at[1])
    copy_f.start()
    copy_i.start()
    acc[...] = jnp.zeros_like(acc)
    copy_f.wait()
    copy_i.wait()
    for r in range(NX):
        for s in range(2):

            def scan(k, found):
                pair_id = sm_i[r, c, s * 64 + k]
                owner = pair_id // 4
                hit = (pair_id % 4 == y) & (owner % NX == x)
                pick[0, found] = k
                pick[1, found] = owner // NX
                return found + hit.astype(jnp.int32)

            found = lax.fori_loop(0, 16, scan, 0)

            def one(j, carry):
                k = pick[0, j]
                zq = pick[1, j]
                base = s * 64 + 16 + k
                weight = sm_f[r, c, base] + sm_f[r, c, base + 16] + sm_f[r, c, base + 32]
                left = parts[r]
                mine_at = pl.multiple_of(c * half, half)
                other_at = pl.multiple_of((1 - c) * half, half)
                inter = jnp.dot(
                    left[s * v : (s + 1) * v, pl.ds(mine_at, half)],
                    q_mine[zq, :half, :],
                    preferred_element_type=jnp.float32,
                )
                inter += jnp.dot(
                    left[s * v : (s + 1) * v, pl.ds(other_at, half)],
                    q_other[zq, :half, :],
                    preferred_element_type=jnp.float32,
                )
                inter = inter.astype(jnp.bfloat16)
                amp_q[pl.ds(pl.multiple_of(c * amp_half, amp_half), amp_half), :] = q_mine[zq, half:, :]
                amp_q[pl.ds(pl.multiple_of((1 - c) * amp_half, amp_half), amp_half), :] = q_other[
                    zq, half:, :
                ]
                mid = jnp.dot(inter, amp_q[...], preferred_element_type=jnp.float32)
                mid = mid.astype(jnp.bfloat16)
                proj = lax.dot_general(
                    mid, inter, (((1,), (1,)), ((), ())), preferred_element_type=jnp.float32
                )
                acc[r, s] += weight * proj.astype(jnp.bfloat16).astype(jnp.float32)
                return carry

            lax.fori_loop(0, found, one, 0)
    own[...] = acc[0]
    for r in range(1, NX):
        away[r - 1] = acc[r].astype(jnp.bfloat16)


def split_weight(weight):
    first = lax.reduce_precision(weight, 8, 7)
    second = lax.reduce_precision(weight - first, 8, 7)
    third = lax.reduce_precision(weight - first - second, 8, 7)
    return first, second, third


def shards(
    amplitudes,
    coefficients,
    energies,
    pair_shift,
    pno_count,
    coupled_pairs,
    coupling_weight,
    slab_one,
    slab_two,
):
    pairs, v, _ = amplitudes.shape
    nv = coefficients.shape[1]
    nz = lax.axis_size("z")
    where = jnp.stack([lax.axis_index(a) for a in ("z", "x", "y", "c")]).astype(jnp.int32)
    c = where[3]
    smem = pl.BlockSpec(memory_space=pltpu.SMEM)
    vmem = pl.BlockSpec(memory_space=pltpu.VMEM)

    meta = jnp.concatenate(
        [coupled_pairs.astype(jnp.float32), *split_weight(coupling_weight)], axis=1
    ).astype(jnp.bfloat16)
    meta = jnp.pad(meta.reshape(2, 2 * meta.shape[1]), ((0, ROWS - 2), (0, 0)))
    z_block, x_block = pl.pallas_call(
        prepare_kernel,
        out_shape=(
            jax.ShapeDtypeStruct((nz, (nv + v) // NC, v), jnp.bfloat16),
            jax.ShapeDtypeStruct((2 * v + ROWS, nv), jnp.bfloat16),
        ),
        in_specs=[smem, vmem, vmem, vmem],
        out_specs=(vmem, vmem),
        name="prepare",
    )(where, coefficients, amplitudes, meta)
    x_parts = [x_block] + [lax.ppermute(x_block, "x", ring(NX, k)) for k in (1, 2, 3)]
    q_mine = lax.all_to_all(z_block, "z", split_axis=0, concat_axis=0, tiled=True)
    q_other = lax.ppermute(q_mine, "c", ring(NC, 1))

    exchange = jnp.einsum("pqa,pqb->pab", slab_one, slab_two, preferred_element_type=jnp.float32)
    gone = lax.dynamic_slice_in_dim(exchange, 2 * (1 - c), 2, 0)
    kept = lax.dynamic_slice_in_dim(exchange, 2 * c, 2, 0)
    kept = kept + lax.ppermute(gone, "c", ring(NC, 1))
    amp_float = amplitudes.astype(jnp.float32)
    amp_kept = lax.dynamic_slice_in_dim(amp_float, 2 * c, 2, 0)
    right = jnp.einsum("pab,pbc->pac", kept, amp_kept, precision=lax.Precision.HIGHEST)
    quadratic = jnp.einsum("pba,pbc->pac", amp_kept, right, precision=lax.Precision.HIGHEST)
    local = kept + quadratic

    own, away = pl.pallas_call(
        couple_kernel,
        out_shape=(
            jax.ShapeDtypeStruct((2, v, v), jnp.float32),
            jax.ShapeDtypeStruct((NX - 1, 2, v, v), jnp.bfloat16),
        ),
        in_specs=[smem] + [vmem] * 6,
        out_specs=(vmem, vmem),
        scratch_shapes=[
            pltpu.VMEM((NX, 8, v), jnp.float32),
            pltpu.VMEM((NX, 8, v), jnp.int32),
            pltpu.SMEM((NX, 8, v), jnp.float32),
            pltpu.SMEM((NX, 8, v), jnp.int32),
            pltpu.SMEM((2, 24), jnp.int32),
            pltpu.VMEM((NX, 2, v, v), jnp.float32),
            pltpu.VMEM((v, v), jnp.bfloat16),
            pltpu.SemaphoreType.DMA((2,)),
        ],
        compiler_params=pltpu.CompilerParams(vmem_limit_bytes=32 * 1024 * 1024),
        name="couple",
    )(where, *x_parts, q_mine, q_other)
    back = [lax.ppermute(away[k - 1], "x", ring(NX, NX - k)) for k in (1, 2, 3)]
    share = local - (own + sum(b.astype(jnp.float32) for b in back))
    y1, y2, y3 = (lax.ppermute(share, "y", ring(NY, k)) for k in (1, 2, 3))
    mine = (share + y2) + (y1 + y3)
    other = lax.ppermute(mine, "c", ring(NC, 1))
    total = jnp.where(
        c == 0, jnp.concatenate([mine, other], axis=0), jnp.concatenate([other, mine], axis=0)
    )
    diagonal = (energies[:, :, None] + energies[:, None, :] - pair_shift[:, None, None]) * amp_float
    inside = jnp.arange(v, dtype=jnp.int32)[None, :] < pno_count[:, None]
    return jnp.where(inside[:, :, None] & inside[:, None, :], total + diagonal, jnp.float32(0.0))


def solution(mesh):
    owners = mesh.devices.shape[0]
    fine = Mesh(mesh.devices.reshape(owners // NX, NX, NY, NC), ("z", "x", "y", "c"))
    pair, aux = ("z", "x"), ("y", "c")
    placed = (
        P(pair, None, None),
        P(pair, None, None),
        P(pair, None),
        P(pair),
        P(pair),
        P(pair, None),
        P(pair, None),
        P(pair, aux, None),
        P(pair, aux, None),
    )
    return jax.shard_map(
        shards, mesh=fine, in_specs=placed, out_specs=P(pair, None, None), check_vma=False
    )
```

time: 513 us -> 89 us (0.17)
  waiting for transfers between devices: 401 us -> 16.3 us
  matrix products: 34.1 us -> 5.98 us
  local copies, waits for them, and re-layouts: 28.6 us -> 2.34 us
  between operations: 13.5 us -> 0.08 us
  Pallas kernels: 0 us -> 9.72 us
  starting transfers between devices: 11.5 us -> 20.2 us
  blocking collectives: 20.2 us -> 28.3 us
    all_to_all x2 -> x0, waiting for transfers between devices: 323 us -> none  [the longest x1 261 us: shards(): lax.all_to_all(coefficients[asked_slots], 'pair', split_axis=0, concat_ax...]
    psum x1 -> x0, waiting for transfers between devices: 77.7 us -> none  [shards(): lax.psum((partial_exchange, partial_quadratic - coupling_share), 'aux')]
    dot_general x5 -> x2, matrix products: 30.4 us -> 2.34 us  [the longest x1 1.17 us: shards(): jnp.einsum('pab,pbc->pac', kept, amp_kept, precision=lax.Precision.HIGHEST)]
    gather x4 -> x0, local copies, waits for them, and re-layouts: 25.7 us -> none  [the longest x1 10.3 us: shards(): back_coef.reshape(owner_count * capacity, back_coef.shape[2], pno_width)]
    ppermute x0 -> x12, starting transfers between devices: none -> 20.2 us  [the longest x3 5.08 us: shards(): back = [lax.ppermute(away[k - 1], 'x', ring(NX, NX - k)) for k in (1, 2, 3)]]
    ppermute x0 -> x12, waiting for transfers between devices: none -> 16.3 us  [the longest x3 5.86 us: shards(): y1, y2, y3 = (lax.ppermute(share, 'y', ring(NY, k)) for k in (1, 2, 3))]
    all_to_all x2 -> x0, starting transfers between devices: 11.5 us -> none  [the longest x1 6.64 us: shards(): lax.all_to_all(coefficients[asked_slots], 'pair', split_axis=0, concat_ax...]
    pallas_call x0 -> x2, Pallas kernels: none -> 9.72 us  [the longest x1 7.53 us: shards(): pl.pallas_call(couple_kernel, out_shape=(jax.ShapeDtypeStruct((2, v, v),...]
  transfers between devices with their start and end apart: 3 -> 12, of which waited for: 3 -> 7; matrix products, arithmetic and copies ran while one was open for 4% -> 7% of each run, Pallas kernels for 0% -> 9%
where the time goes in v1:
time: 89 us; the launch traced here: 88.1 us
  blocking collectives  28.3 us (32%)
  starting transfers between devices  20.2 us (23%)
  waiting for transfers between devices  16.3 us (18%)
  Pallas kernels  9.72 us (11%)
  matrix products  5.98 us (7%)
  other arithmetic  5.2 us (6%)
  local copies, waits for them, and re-layouts  2.34 us (3%)
    all_to_all x1, blocking collectives, shards(): lax.all_to_all(z_block, 'z', split_axis=0, concat_axis=0, tiled=True)  28.3 us
    pallas_call x1, Pallas kernels, shards(): pl.pallas_call(couple_kernel, out_shape=(jax.ShapeDtypeStruct((2, v, v),...  7.53 us
    ppermute x3, waiting for transfers between devices, shards(): y1, y2, y3 = (lax.ppermute(share, 'y', ring(NY, k)) for k in (1, 2, 3))  5.86 us
    ppermute x3, waiting for transfers between devices, shards(): lax.ppermute(x_block, 'x', ring(NX, k))  5.7 us
    ppermute x3, starting transfers between devices, shards(): back = [lax.ppermute(away[k - 1], 'x', ring(NX, NX - k)) for k in (1, 2, 3)]  5.08 us
    ppermute x3, starting transfers between devices, shards(): lax.ppermute(x_block, 'x', ring(NX, k))  4.81 us
    ppermute x1, starting transfers between devices, shards(): other = lax.ppermute(mine, 'c', ring(NC, 1))  4.19 us
    ppermute x3, waiting for transfers between devices, shards(): back = [lax.ppermute(away[k - 1], 'x', ring(NX, NX - k)) for k in (1, 2, 3)]  3.8 us
  transfers between devices with their start and end apart: 12, of which 7 were waited for; matrix products, arithmetic and copies ran while one was open for 7% of the time, Pallas kernels for 9%

profile of v1, /device:TPU:1, one launch (start us, length us, event | category | flops | bytes accessed | tf_op | source)
XLA Modules:
  0.0 88.1 jit_solution(16321418292101161118)
XLA Ops:
  0.0 0.0 copy-start
  0.0 0.8 reduce-precision_convert_fusion.1
  0.8 0.8 convert_convert_fusion
  1.6 0.1 pad_maximum_fusion
  1.7 0.1 convert_element_type.23
  1.8 0.6 pad.4.meta
  2.4 0.7 pad_add_fusion.where
  3.1 2.2 %prepare.1 = (bf16[8,320,128]{2,1,0:T(8,128)(2,1)}, bf16[272,512]{1,0:T(8,128)(2,1)}) custom-call(s32[4]{0:T(128)} %pad_add_fusion.where, bf16[4,512,128]{2,1,0:T(8,128)(2,1)} %coef.1, bf16[4,128,128]{2,1,0:T(8,128)(2,1)} %amp.1, bf16[16,128]{1,0:T(8,128)(2,1)} %pad.4.meta), custom_call_target="tpu_custom_call" | custom-call | tf_op jit(solution)/shard_map/prepare/pallas_call | solution.py:133
  5.3 28.3 %all_to_all.5.q_mine = bf16[8,320,128]{2,1,0:T(8,128)(2,1)} all-to-all(bf16[8,320,128]{2,1,0:T(8,128)(2,1)} %get-tuple-element.10), channel_id=1, replica_groups=mesh['z'=8,'x'=4,'y'=4,'c'=2] {'z'}, dimensions={0} | all-to-all | bytes 1310720 | tf_op jit(solution)/shard_map/all_to_all | solution.py:144
  33.5 2.1 %collective-permute-start.4 = (bf16[8,320,128]{2,1,0:T(8,128)(2,1)}, bf16[8,320,128]{2,1,0:T(8,128)(2,1)}, u32[]{:S(2)}, u32[]{:S(2)}) collective-permute-start(bf16[8,320,128]{2,1,0:T(8,128)(2,1)} %all_to_all.5.q_mine), channel_id=1, source_target_pairs={{0,1},{1,0},{2,3},{3,2},{4,5},{5,4},{6,7},{7,6},{8,9},{9,8},{10,11... | collective-permute-start | bytes 1966088 | tf_op jit(solution)/shard_map/ppermute | solution.py:145
  35.6 0.0 copy-start.1
  35.6 0.0 copy-start.2
  35.6 1.2 %collective-permute-start.1 = (bf16[272,512]{1,0:T(8,128)(2,1)}, bf16[272,512]{1,0:T(8,128)(2,1)}, u32[]{:S(2)}, u32[]{:S(2)}) collective-permute-start(bf16[272,512]{1,0:T(8,128)(2,1)} %get-tuple-element.9.p0), channel_id=1, source_target_pairs={{0,8},{8,16},{16,24},{24,0},{1,9},{9,17},{17,25},{25,1},{2,10},{10... | collective-permute-start | bytes 835592 | tf_op jit(solution)/shard_map/ppermute | solution.py:143
  36.8 2.5 %collective-permute-start.2 = (bf16[272,512]{1,0:T(8,128)(2,1)}, bf16[272,512]{1,0:T(8,128)(2,1)}, u32[]{:S(2)}, u32[]{:S(2)}) collective-permute-start(bf16[272,512]{1,0:T(8,128)(2,1)} %get-tuple-element.9.p0), channel_id=1, source_target_pairs={{0,16},{8,24},{16,0},{24,8},{1,17},{9,25},{17,1},{25,9},{2,18},{10... | collective-permute-start | bytes 835592 | tf_op jit(solution)/shard_map/ppermute | solution.py:143
  39.3 1.2 %collective-permute-start.3 = (bf16[272,512]{1,0:T(8,128)(2,1)}, bf16[272,512]{1,0:T(8,128)(2,1)}, u32[]{:S(2)}, u32[]{:S(2)}) collective-permute-start(bf16[272,512]{1,0:T(8,128)(2,1)} %get-tuple-element.9.p0), channel_id=1, source_target_pairs={{0,24},{8,0},{16,8},{24,16},{1,25},{9,1},{17,9},{25,17},{2,26},{10... | collective-permute-start | bytes 835592 | tf_op jit(solution)/shard_map/ppermute | solution.py:143
  40.5 0.0 copy-done
  40.5 3.6 %fusion.10 = f32[4,128,128]{2,1,0:T(8,128)} fusion(bf16[4,3072,128]{2,1,0:T(8,128)(2,1)S(1)} %copy-done, bf16[4,3072,128]{2,1,0:T(8,128)(2,1)} %param.17), kind=kOutput, calls=%fused_computation.26 | convolution fusion | flops 402653184 | bytes 6553600 | tf_op jit(solution)/shard_map/pqa,pqb->pab/dot_general | solution.py:147
  44.1 0.0 copy-start.7
  44.1 0.0 copy-start.5
  44.1 0.0 copy-start.6
  44.1 1.6 %constant_dynamic-slice_fusion = f32[2,128,128]{2,1,0:T(8,128)} fusion(f32[4,128,128]{2,1,0:T(8,128)} %fusion.10, s32[]{:T(128)S(6)} %select_n.21), kind=kLoop, calls=%fused_computation.23 | loop fusion | bytes 262148 | tf_op jit(solution)/shard_map/dynamic_slice | solution.py:148
  45.7 0.9 %collective-permute-start = (f32[2,128,128]{2,1,0:T(8,128)}, f32[2,128,128]{2,1,0:T(8,128)}, u32[]{:S(2)}, u32[]{:S(2)}) collective-permute-start(f32[2,128,128]{2,1,0:T(8,128)} %constant_dynamic-slice_fusion), channel_id=1, source_target_pairs={{0,1},{1,0},{2,3},{3,2},{4,5},{5,4},{6,7},{7,6},{8,9},{9,8},{10,11... | collective-permute-start | bytes 393224 | tf_op jit(solution)/shard_map/ppermute | solution.py:150
  46.6 0.0 copy-start.3
  46.6 0.0 copy-start.4
  46.6 0.0 collective-permute-done.1.p1
  46.6 5.7 %collective-permute-done.2.p2 = bf16[272,512]{1,0:T(8,128)(2,1)} collective-permute-done((bf16[272,512]{1,0:T(8,128)(2,1)}, bf16[272,512]{1,0:T(8,128)(2,1)}, u32[]{:S(2)}, u32[]{:S(2)}) %collective-permute-start.2) | collective-permute-done | bytes 278560 | tf_op jit(solution)/shard_map/ppermute | solution.py:143
  52.3 0.0 collective-permute-done.3.p3
  52.3 0.0 collective-permute-done.4.q_other
  52.3 0.0 copy-done.1
  52.3 0.0 copy-done.2
  52.3 7.5 %couple.1 = (f32[2,128,128]{2,1,0:T(8,128)S(1)}, bf16[3,2,128,128]{3,2,1,0:T(8,128)(2,1)S(1)}) custom-call(s32[4]{0:T(128)S(1)} %copy-done.2, bf16[272,512]{1,0:T(8,128)(2,1)S(1)} %copy-done.1, bf16[272,512]{1,0:T(8,128)(2,1)} %collective-permute-done.1.p1, bf16[272,512]{1,0:T(8,128)(2,1)} %collective-permute-done.2.p2, ...), custom_call_target="tpu_custom_call" | custom-call | tf_op jit(solution)/shard_map/couple/pallas_call | solution.py:157
  59.9 4.1 %collective-permute-start.5 = (bf16[2,128,128]{2,1,0:T(8,128)(2,1)S(1)}, bf16[2,128,128]{2,1,0:T(8,128)(2,1)S(1)}, u32[]{:S(2)}, u32[]{:S(2)}) collective-permute-start(bf16[2,128,128]{2,1,0:T(8,128)(2,1)S(1)} %get-tuple-element.13), channel_id=1, source_target_pairs={{0,24},{8,0},{16,8},{24,16},{1,25},{9,1},{17,9},{25,17},{2,26},{10... | collective-permute-start | bytes 196616 | tf_op jit(solution)/shard_map/ppermute | solution.py:178
  64.0 0.2 collective-permute-start.6
  64.2 0.8 collective-permute-start.7
  65.0 0.0 collective-permute-done
  65.0 1.2 %fusion.3 = f32[2,128,128]{2,1,0:T(8,128)S(1)} fusion(bf16[4,128,128]{2,1,0:T(8,128)(2,1)} %amp.1, s32[]{:T(128)S(6)} %select_n.20, f32[2,128,128]{2,1,0:T(8,128)} %collective-permute-done, f32[4,128,128]{2,1,0:T(8,128)} %fusion.10), kind=kOutput, calls=%fused_computation.10 | convolution fusion | flops 50364416 | bytes 459776 | tf_op jit(solution)/shard_map/pab,pbc->pac/dot_general | solution.py:153
  66.2 0.0 collective-permute-done.5
  66.2 3.2 %collective-permute-done.6 = bf16[2,128,128]{2,1,0:T(8,128)(2,1)S(1)} collective-permute-done((bf16[2,128,128]{2,1,0:T(8,128)(2,1)S(1)}, bf16[2,128,128]{2,1,0:T(8,128)(2,1)S(1)}, u32[]{:S(2)}, u32[]{:S(2)}) %collective-permute-start.6) | collective-permute-done | bytes 65568 | tf_op jit(solution)/shard_map/ppermute | solution.py:178
  69.3 0.6 collective-permute-done.7
  70.0 0.0 copy-done.3
  70.0 0.0 copy-done.4
  70.0 1.2 %fusion = f32[2,128,128]{2,1,0:T(8,128)S(1)} fusion(f32[2,128,128]{2,1,0:T(8,128)S(1)} %fusion.3, f32[2,128,128]{2,1,0:T(8,128)S(1)} %get-tuple-element.11, bf16[2,128,128]{2,1,0:T(8,128)(2,1)S(1)} %collective-permute-done.7, bf16[2,128,128]{2,1,0:T(8,128)(2,1)S(1)} %collective-permute-done.6, bf16[2,128,128]{2,1,0:T(8,128)(2,1)S(1)} %collective-permute-done.5, ...), kind=kOutput, calls=%fused_computation.1 | convolution fusion | flops 50626560 | bytes 918528 | tf_op jit(solution)/shard_map/pba,pbc->pac/dot_general | solution.py:154
  71.2 2.4 %collective-permute-start.10 = (f32[2,128,128]{2,1,0:T(8,128)S(1)}, f32[2,128,128]{2,1,0:T(8,128)S(1)}, u32[]{:S(2)}, u32[]{:S(2)}) collective-permute-start(f32[2,128,128]{2,1,0:T(8,128)S(1)} %fusion), channel_id=1, source_target_pairs={{0,6},{2,0},{4,2},{6,4},{1,7},{3,1},{5,3},{7,5},{8,14},{10,8},{12,... | collective-permute-start | bytes 393224 | tf_op jit(solution)/shard_map/ppermute | solution.py:180
  73.6 0.0 collective-permute-start.8
  73.6 0.7 collective-permute-start.9
  74.3 2.6 %collective-permute-done.10 = f32[2,128,128]{2,1,0:T(8,128)S(1)} collective-permute-done((f32[2,128,128]{2,1,0:T(8,128)S(1)}, f32[2,128,128]{2,1,0:T(8,128)S(1)}, u32[]{:S(2)}, u32[]{:S(2)}) %collective-permute-start.10) | collective-permute-done | bytes 131104 | tf_op jit(solution)/shard_map/ppermute | solution.py:180
  76.9 2.1 %collective-permute-done.8 = f32[2,128,128]{2,1,0:T(8,128)S(1)} collective-permute-done((f32[2,128,128]{2,1,0:T(8,128)S(1)}, f32[2,128,128]{2,1,0:T(8,128)S(1)}, u32[]{:S(2)}, u32[]{:S(2)}) %collective-permute-start.8) | collective-permute-done | bytes 131104 | tf_op jit(solution)/shard_map/ppermute | solution.py:180
  79.0 1.1 %collective-permute-done.9 = f32[2,128,128]{2,1,0:T(8,128)} collective-permute-done((f32[2,128,128]{2,1,0:T(8,128)S(1)}, f32[2,128,128]{2,1,0:T(8,128)}, u32[]{:S(2)}, u32[]{:S(2)}) %collective-permute-start.9) | collective-permute-done | bytes 131104 | tf_op jit(solution)/shard_map/ppermute | solution.py:180
  80.1 0.9 %add_add_fusion = f32[2,128,128]{2,1,0:T(8,128)S(1)} fusion(f32[2,128,128]{2,1,0:T(8,128)} %collective-permute-done.9, f32[2,128,128]{2,1,0:T(8,128)S(1)} %collective-permute-done.10, f32[2,128,128]{2,1,0:T(8,128)S(1)} %fusion, f32[2,128,128]{2,1,0:T(8,128)S(1)} %collective-permute-done.8), kind=kLoop, calls=%fused_computation.5 | loop fusion | flops 98304 | bytes 655360 | tf_op jit(solution)/shard_map/add | solution.py:181
  81.1 4.2 %collective-permute-start.11 = (f32[2,128,128]{2,1,0:T(8,128)S(1)}, f32[2,128,128]{2,1,0:T(8,128)S(1)}, u32[]{:S(2)}, u32[]{:S(2)}) collective-permute-start(f32[2,128,128]{2,1,0:T(8,128)S(1)} %add_add_fusion), channel_id=1, source_target_pairs={{0,1},{1,0},{2,3},{3,2},{4,5},{5,4},{6,7},{7,6},{8,9},{9,8},{10,11... | collective-permute-start | bytes 393224 | tf_op jit(solution)/shard_map/ppermute | solution.py:182
  85.3 0.0 copy-done.7
  85.3 0.1 iota_compare_fusion
  85.3 0.9 %collective-permute-done.11 = f32[2,128,128]{2,1,0:T(8,128)S(1)} collective-permute-done((f32[2,128,128]{2,1,0:T(8,128)S(1)}, f32[2,128,128]{2,1,0:T(8,128)S(1)}, u32[]{:S(2)}, u32[]{:S(2)}) %collective-permute-start.11) | collective-permute-done | bytes 131104 | tf_op jit(solution)/shard_map/ppermute | solution.py:182
  86.3 0.0 copy-done.5
  86.3 0.0 copy-done.6
  86.3 1.8 %fusion.2 = f32[4,128,128]{2,1,0:T(8,128)} fusion(f32[2,128,128]{2,1,0:T(8,128)S(1)} %collective-permute-done.11, f32[2,128,128]{2,1,0:T(8,128)S(1)} %add_add_fusion, bf16[4,128,128]{2,1,0:T(8,128)(2,1)} %amp.1, f32[4]{0:T(128)S(1)} %copy-done.6, f32[4,128]{1,0:T(4,128)S(1)} %copy-done.5, pred[]{:T(512)S(6)} %eq.3, pred[4,128]{1,0:T(4,128)(4,1)S(1)} %iota_compare_fusion), kind=kLoop, calls=%fused_computation.4 | loop fusion | flops 655360 | bytes 657937 | tf_op jit(solution)/shard_map/jit(_where)/select_n | solution.py:188
  (1 shorter events, 0.0 us)
Async XLA Ops:
  0.0 40.5 %copy-start = (bf16[4,3072,128]{2,1,0:T(8,128)(2,1)S(1)}, bf16[4,3072,128]{2,1,0:T(8,128)(2,1)}, u32[]{:S(2)}) copy-start(bf16[4,3072,128]{2,1,0:T(8,128)(2,1)} %param.16) | copy-start | bytes 9437188
  33.5 18.8 %collective-permute-start.4 = (bf16[8,320,128]{2,1,0:T(8,128)(2,1)}, bf16[8,320,128]{2,1,0:T(8,128)(2,1)}, u32[]{:S(2)}, u32[]{:S(2)}) collective-permute-start(bf16[8,320,128]{2,1,0:T(8,128)(2,1)} %all_to_all.5.q_mine), channel_id=1, source_target_pairs={{0,1},{1,0},{2,3},{3,2},{4,5},{5,4},{6,7},{7,6},{8,9},{9,8},{10,11... | collective-permute-start | bytes 1966088 | tf_op jit(solution)/shard_map/ppermute | solution.py:145
  35.6 16.7 %copy-start.1 = (bf16[272,512]{1,0:T(8,128)(2,1)S(1)}, bf16[272,512]{1,0:T(8,128)(2,1)}, u32[]{:S(2)}) copy-start(bf16[272,512]{1,0:T(8,128)(2,1)} %get-tuple-element.9.p0) | copy-start | bytes 835588
  35.6 16.7 %copy-start.2 = (s32[4]{0:T(128)S(1)}, s32[4]{0:T(128)}, u32[]{:S(2)}) copy-start(s32[4]{0:T(128)} %pad_add_fusion.where) | copy-start | bytes 52
  35.6 11.0 %collective-permute-start.1 = (bf16[272,512]{1,0:T(8,128)(2,1)}, bf16[272,512]{1,0:T(8,128)(2,1)}, u32[]{:S(2)}, u32[]{:S(2)}) collective-permute-start(bf16[272,512]{1,0:T(8,128)(2,1)} %get-tuple-element.9.p0), channel_id=1, source_target_pairs={{0,8},{8,16},{16,24},{24,0},{1,9},{9,17},{17,25},{25,1},{2,10},{10... | collective-permute-start | bytes 835592 | tf_op jit(solution)/shard_map/ppermute | solution.py:143
  36.8 15.5 %collective-permute-start.2 = (bf16[272,512]{1,0:T(8,128)(2,1)}, bf16[272,512]{1,0:T(8,128)(2,1)}, u32[]{:S(2)}, u32[]{:S(2)}) collective-permute-start(bf16[272,512]{1,0:T(8,128)(2,1)} %get-tuple-element.9.p0), channel_id=1, source_target_pairs={{0,16},{8,24},{16,0},{24,8},{1,17},{9,25},{17,1},{25,9},{2,18},{10... | collective-permute-start | bytes 835592 | tf_op jit(solution)/shard_map/ppermute | solution.py:143
  39.3 13.0 %collective-permute-start.3 = (bf16[272,512]{1,0:T(8,128)(2,1)}, bf16[272,512]{1,0:T(8,128)(2,1)}, u32[]{:S(2)}, u32[]{:S(2)}) collective-permute-start(bf16[272,512]{1,0:T(8,128)(2,1)} %get-tuple-element.9.p0), channel_id=1, source_target_pairs={{0,24},{8,0},{16,8},{24,16},{1,25},{9,1},{17,9},{25,17},{2,26},{10... | collective-permute-start | bytes 835592 | tf_op jit(solution)/shard_map/ppermute | solution.py:143
  44.1 41.2 %copy-start.7 = (s32[4]{0:T(128)S(1)}, s32[4]{0:T(128)}, u32[]{:S(2)}) copy-start(s32[4]{0:T(128)} %param.13) | copy-start | bytes 52
  44.1 42.2 %copy-start.5 = (f32[4,128]{1,0:T(4,128)S(1)}, f32[4,128]{1,0:T(4,128)}, u32[]{:S(2)}) copy-start(f32[4,128]{1,0:T(4,128)} %param.11) | copy-start | bytes 6148
  44.1 42.2 %copy-start.6 = (f32[4]{0:T(128)S(1)}, f32[4]{0:T(128)}, u32[]{:S(2)}) copy-start(f32[4]{0:T(128)} %param.12) | copy-start | bytes 52
  45.7 19.3 %collective-permute-start = (f32[2,128,128]{2,1,0:T(8,128)}, f32[2,128,128]{2,1,0:T(8,128)}, u32[]{:S(2)}, u32[]{:S(2)}) collective-permute-start(f32[2,128,128]{2,1,0:T(8,128)} %constant_dynamic-slice_fusion), channel_id=1, source_target_pairs={{0,1},{1,0},{2,3},{3,2},{4,5},{5,4},{6,7},{7,6},{8,9},{9,8},{10,11... | collective-permute-start | bytes 393224 | tf_op jit(solution)/shard_map/ppermute | solution.py:150
  46.6 23.4 %copy-start.3 = (f32[4,128,128]{2,1,0:T(8,128)S(1)}, f32[4,128,128]{2,1,0:T(8,128)}, u32[]{:S(2)}) copy-start(f32[4,128,128]{2,1,0:T(8,128)} %fusion.10) | copy-start | bytes 786436
  46.6 23.4 %copy-start.4 = (bf16[4,128,128]{2,1,0:T(8,128)(2,1)S(1)}, bf16[4,128,128]{2,1,0:T(8,128)(2,1)}, u32[]{:S(2)}) copy-start(bf16[4,128,128]{2,1,0:T(8,128)(2,1)} %amp.1) | copy-start | bytes 393220
  59.9 6.3 %collective-permute-start.5 = (bf16[2,128,128]{2,1,0:T(8,128)(2,1)S(1)}, bf16[2,128,128]{2,1,0:T(8,128)(2,1)S(1)}, u32[]{:S(2)}, u32[]{:S(2)}) collective-permute-start(bf16[2,128,128]{2,1,0:T(8,128)(2,1)S(1)} %get-tuple-element.13), channel_id=1, source_target_pairs={{0,24},{8,0},{16,8},{24,16},{1,25},{9,1},{17,9},{25,17},{2,26},{10... | collective-permute-start | bytes 196616 | tf_op jit(solution)/shard_map/ppermute | solution.py:178
  64.0 5.3 %collective-permute-start.6 = (bf16[2,128,128]{2,1,0:T(8,128)(2,1)S(1)}, bf16[2,128,128]{2,1,0:T(8,128)(2,1)S(1)}, u32[]{:S(2)}, u32[]{:S(2)}) collective-permute-start(bf16[2,128,128]{2,1,0:T(8,128)(2,1)S(1)} %get-tuple-element.15), channel_id=1, source_target_pairs={{0,16},{8,24},{16,0},{24,8},{1,17},{9,25},{17,1},{25,9},{2,18},{10... | collective-permute-start | bytes 196616 | tf_op jit(solution)/shard_map/ppermute | solution.py:178
  64.2 5.8 %collective-permute-start.7 = (bf16[2,128,128]{2,1,0:T(8,128)(2,1)S(1)}, bf16[2,128,128]{2,1,0:T(8,128)(2,1)S(1)}, u32[]{:S(2)}, u32[]{:S(2)}) collective-permute-start(bf16[2,128,128]{2,1,0:T(8,128)(2,1)S(1)} %get-tuple-element.14), channel_id=1, source_target_pairs={{0,8},{8,16},{16,24},{24,0},{1,9},{9,17},{17,25},{25,1},{2,10},{10... | collective-permute-start | bytes 196616 | tf_op jit(solution)/shard_map/ppermute | solution.py:178
  71.2 5.8 %collective-permute-start.10 = (f32[2,128,128]{2,1,0:T(8,128)S(1)}, f32[2,128,128]{2,1,0:T(8,128)S(1)}, u32[]{:S(2)}, u32[]{:S(2)}) collective-permute-start(f32[2,128,128]{2,1,0:T(8,128)S(1)} %fusion), channel_id=1, source_target_pairs={{0,6},{2,0},{4,2},{6,4},{1,7},{3,1},{5,3},{7,5},{8,14},{10,8},{12,... | collective-permute-start | bytes 393224 | tf_op jit(solution)/shard_map/ppermute | solution.py:180
  73.6 5.4 %collective-permute-start.8 = (f32[2,128,128]{2,1,0:T(8,128)S(1)}, f32[2,128,128]{2,1,0:T(8,128)S(1)}, u32[]{:S(2)}, u32[]{:S(2)}) collective-permute-start(f32[2,128,128]{2,1,0:T(8,128)S(1)} %fusion), channel_id=1, source_target_pairs={{0,4},{2,6},{4,0},{6,2},{1,5},{3,7},{5,1},{7,3},{8,12},{10,14},{12... | collective-permute-start | bytes 393224 | tf_op jit(solution)/shard_map/ppermute | solution.py:180
  73.6 6.5 %collective-permute-start.9 = (f32[2,128,128]{2,1,0:T(8,128)S(1)}, f32[2,128,128]{2,1,0:T(8,128)}, u32[]{:S(2)}, u32[]{:S(2)}) collective-permute-start(f32[2,128,128]{2,1,0:T(8,128)S(1)} %fusion), channel_id=1, source_target_pairs={{0,2},{2,4},{4,6},{6,0},{1,3},{3,5},{5,7},{7,1},{8,10},{10,12},{12... | collective-permute-start | bytes 393224 | tf_op jit(solution)/shard_map/ppermute | solution.py:180
  81.1 5.2 %collective-permute-start.11 = (f32[2,128,128]{2,1,0:T(8,128)S(1)}, f32[2,128,128]{2,1,0:T(8,128)S(1)}, u32[]{:S(2)}, u32[]{:S(2)}) collective-permute-start(f32[2,128,128]{2,1,0:T(8,128)S(1)} %add_add_fusion), channel_id=1, source_target_pairs={{0,1},{1,0},{2,3},{3,2},{4,5},{5,4},{6,7},{7,6},{8,9},{9,8},{10,11... | collective-permute-start | bytes 393224 | tf_op jit(solution)/shard_map/ppermute | solution.py:182

commit v2 on v0

v2 whole, which is shorter than its diff:
```python
import jax
import jax.numpy as jnp
from jax import lax
from jax.experimental import pallas as pl
from jax.experimental.pallas import tpu as pltpu
from jax.sharding import Mesh
from jax.sharding import PartitionSpec as P

NX, NY, NC = 4, 4, 2
META = 16
STEP = 4


def opposite(size, step):
    up = [(i * NC, ((i + step) % size) * NC) for i in range(size)]
    down = [(i * NC + 1, ((i - step) % size) * NC + 1) for i in range(size)]
    return up + down


def ring(size, step):
    return [(i, (i + step) % size) for i in range(size)]


def partners(turn):
    table = ([1, 0, 3, 2], [3, 2, 1, 0])
    return [
        (y * NC + c, table[(turn + c) % 2][y] * NC + c) for y in range(NY) for c in range(NC)
    ]


def prepare_kernel(where, pairs, weights, coef, amp, z_full, x_all, x_own, sem):
    y, c = where[2], where[3]
    _, nv, v = coef.shape
    copies = []

    def fetch(src, dst):
        copy = pltpu.make_async_copy(src, dst, sem.at[len(copies)])
        copy.start()
        copies.append(copy)

    fetch(coef.at[y], z_full.at[pl.ds(0, nv)])
    fetch(amp.at[y], z_full.at[pl.ds(nv, v)])
    for s in range(4):
        fetch(coef.at[s], x_all.at[pl.ds(s * nv, nv)])
    for s in range(2):
        fetch(coef.at[2 * c + s], x_own.at[pl.ds(s * nv, nv)])
    weight = weights[...]
    first = weight.astype(jnp.bfloat16).astype(jnp.float32)
    second = (weight - first).astype(jnp.bfloat16).astype(jnp.float32)
    third = weight - first - second
    meta = jnp.concatenate([pairs[...].astype(jnp.float32), first, second, third], axis=0)
    meta = meta.astype(jnp.bfloat16)
    for ref, start in ((x_all, 4 * nv), (x_own, 2 * nv)):
        ref[start : start + META, :] = jnp.zeros((META, v), jnp.bfloat16)
        ref[start : start + META, : meta.shape[1]] = meta
    for copy in copies:
        copy.wait()


def pack_kernel(where, first, second, after, packed):
    c = where[3]
    rows, v = first.shape
    nv = rows - v
    half, amp_half = nv // NC, v // NC
    packed[:rows, :] = first[...]
    packed[rows : rows + half, :] = second[pl.ds(pl.multiple_of(c * half, half), half), :]
    packed[rows + half :, :] = second[
        pl.ds(pl.multiple_of(nv + c * amp_half, amp_half), amp_half), :
    ]


def turn_kernel(near, own, turned):
    nv = turned.shape[1]
    v = near.shape[1]
    at = 0
    for ref, slots in ((near, 4), (own, 2)):
        for s in range(slots):
            turned[at * v : (at + 1) * v, :] = ref[s * nv : (s + 1) * nv, :].T
            at += 1


def couple_kernel(where, turned, x_near, x_far, x_own, z_full, *refs):
    z, x, y, c = where[0], where[1], where[2], where[3]
    mine, other = refs[:3], refs[3:6]
    near, far, own, left, right, q, acc, meta, meta_f, meta_i, sm_f, sm_i, picks, factors, sem = refs[6:]
    nz, rows, v = q.shape
    nv = rows - v
    half, amp_half = nv // NC, v // NC
    copies = []

    def fetch(src, dst):
        copy = pltpu.make_async_copy(src, dst, sem.at[len(copies)])
        copy.start()
        copies.append(copy)

    fetch(x_near.at[pl.ds(4 * nv, META)], meta.at[0])
    fetch(x_own.at[pl.ds(2 * nv, META)], meta.at[1])
    fetch(x_far, right)
    early = list(copies)
    fetch(turned, left.at[pl.ds(0, 6 * v)])
    fetch(z_full, q.at[z])
    sign = 1 - 2 * c
    across = lax.rem(z + 4, nz)
    for refs_from, away, part in ((mine, -sign, c), (other, sign, 1 - c)):
        for k in range(1, 4):
            src = refs_from[k - 1].at[pl.ds(0, rows)] if k == 3 else refs_from[k - 1]
            fetch(src, q.at[lax.rem(z + away * k + nz, nz)])
        fetch(
            refs_from[2].at[pl.ds(rows, half)],
            q.at[across, pl.ds(pl.multiple_of(part * half, half), half)],
        )
        fetch(
            refs_from[2].at[pl.ds(rows + half, amp_half)],
            q.at[across, pl.ds(pl.multiple_of(nv + part * amp_half, amp_half), amp_half)],
        )
    for copy in early:
        copy.wait()
    for i, block in enumerate((meta[0], meta[1], right[2 * nv :, :])):
        block = block.astype(jnp.float32)
        meta_i[i, :4] = block[:4].astype(jnp.int32)
        meta_f[i, :4] = block[4:8] + block[8:12] + block[12:16]
    copy_f = pltpu.make_async_copy(meta_f, sm_f, sem.at[0])
    copy_i = pltpu.make_async_copy(meta_i, sm_i, sem.at[1])
    copy_f.start()
    copy_i.start()
    for s in range(2):
        left[(6 + s) * v : (7 + s) * v, :] = right[s * nv : (s + 1) * nv, :].T
    copy_f.wait()
    copy_i.wait()
    found = 0
    wanted = x * 4 + y
    for p in range(8):
        source = 0 if p < 4 else 1 if p < 6 else 2
        slot = p if p < 4 else 2 * c + p % 2
        for k in range(16):
            pair_id = sm_i[source, slot, k]
            picks[found] = pair_id * 8 + p
            factors[found] = sm_f[source, slot, k]
            found += (pair_id % 16 == wanted).astype(jnp.int32)
    for j in range(STEP):
        picks[found + j] = 0
        factors[found + j] = 0.0
    acc[...] = jnp.zeros_like(acc)
    for copy in copies[len(early) :]:
        copy.wait()

    def several(i, carry):
        at = [i * STEP + j for j in range(STEP)]
        ps = [picks[a] % 8 for a in at]
        zs = [picks[a] // (8 * 4 * NX) for a in at]
        inter = [
            jnp.dot(
                left[pl.ds(pl.multiple_of(p * v, v), v), :],
                q[zq, :nv, :],
                preferred_element_type=jnp.float32,
            ).astype(jnp.bfloat16)
            for p, zq in zip(ps, zs)
        ]
        mid = [
            jnp.dot(a, q[zq, nv:, :], preferred_element_type=jnp.float32).astype(jnp.bfloat16)
            for a, zq in zip(inter, zs)
        ]
        proj = [
            lax.dot_general(m, a, (((1,), (1,)), ((), ())), preferred_element_type=jnp.float32)
            .astype(jnp.bfloat16)
            .astype(jnp.float32)
            for m, a in zip(mid, inter)
        ]
        for a, p, value in zip(at, ps, proj):
            acc[p] += factors[a] * value
        return carry

    lax.fori_loop(0, (found + STEP - 1) // STEP, several, 0)
    near[...] = acc[:4].astype(jnp.bfloat16)
    own[...] = acc[4:6]
    far[...] = acc[6:8].astype(jnp.bfloat16)


def settle_kernel(where, local, near, far, own, kept, gone):
    c = where[3]
    for s in range(2):
        gone[s] = local[2 * (1 - c) + s] - near[2 * (1 - c) + s].astype(jnp.float32)
        kept[s] = local[2 * c + s] - near[2 * c + s].astype(jnp.float32) - (
            own[s] + far[s].astype(jnp.float32)
        )


def shards(
    amplitudes,
    coefficients,
    energies,
    pair_shift,
    pno_count,
    coupled_pairs,
    coupling_weight,
    slab_one,
    slab_two,
):
    pairs, v, _ = amplitudes.shape
    nv = coefficients.shape[1]
    nz = lax.axis_size("z")
    where = jnp.stack([lax.axis_index(a) for a in ("z", "x", "y", "c")]).astype(jnp.int32)
    c = where[3]
    smem = pl.BlockSpec(memory_space=pltpu.SMEM)
    vmem = pl.BlockSpec(memory_space=pltpu.VMEM)
    anywhere = pl.BlockSpec(memory_space=pl.ANY)
    bf16, f32, i32 = jnp.bfloat16, jnp.float32, jnp.int32

    z_full, x_all, x_own = pl.pallas_call(
        prepare_kernel,
        out_shape=(
            jax.ShapeDtypeStruct((nv + v, v), bf16),
            jax.ShapeDtypeStruct((4 * nv + META, v), bf16),
            jax.ShapeDtypeStruct((2 * nv + META, v), bf16),
        ),
        in_specs=[smem, vmem, vmem, anywhere, anywhere],
        out_specs=(vmem,) * 3,
        scratch_shapes=[pltpu.SemaphoreType.DMA((8,))],
        compiler_params=pltpu.CompilerParams(vmem_limit_bytes=4 * 1024 * 1024),
        name="prepare",
    )(where, coupled_pairs, coupling_weight, coefficients, amplitudes)

    swap = ring(NC, 1)
    z_one = lax.ppermute(z_full, ("z", "c"), opposite(nz, 1))
    z_two = lax.ppermute(z_full, ("z", "c"), opposite(nz, 2))
    x_near = lax.ppermute(x_all, ("x", "c"), opposite(NX, 1))
    x_far = lax.ppermute(x_own, "x", ring(NX, 2))
    exchange = jnp.einsum("pqa,pqb->pab", slab_one, slab_two, preferred_element_type=f32)
    amp_float = amplitudes.astype(f32)
    right = jnp.einsum("pab,pbc->pac", exchange, amp_float, precision=lax.Precision.HIGHEST)
    quadratic = jnp.einsum("pba,pbc->pac", amp_float, right, precision=lax.Precision.HIGHEST)
    local = exchange + quadratic

    z_rest = pl.pallas_call(
        pack_kernel,
        out_shape=jax.ShapeDtypeStruct((nv + v + (nv + v) // NC, v), bf16),
        in_specs=[smem, vmem, vmem, anywhere],
        out_specs=vmem,
        compiler_params=pltpu.CompilerParams(vmem_limit_bytes=4 * 1024 * 1024),
        name="pack",
    )(where, z_one, z_two, exchange)
    z_rest = lax.ppermute(z_rest, ("z", "c"), opposite(nz, 2))
    z_mine = [z_one, z_two, z_rest]
    z_other = [lax.ppermute(b, "c", swap) for b in z_mine]

    turned = pl.pallas_call(
        turn_kernel,
        out_shape=jax.ShapeDtypeStruct((6 * v, nv), bf16),
        in_specs=[vmem, vmem],
        out_specs=vmem,
        compiler_params=pltpu.CompilerParams(vmem_limit_bytes=6 * 1024 * 1024),
        cost_estimate=pl.CostEstimate(flops=0, bytes_accessed=12_000_000, transcendentals=0),
        name="turn",
    )(x_near, x_own)
    near, far, own = pl.pallas_call(
        couple_kernel,
        out_shape=(
            jax.ShapeDtypeStruct((4, v, v), bf16),
            jax.ShapeDtypeStruct((2, v, v), bf16),
            jax.ShapeDtypeStruct((2, v, v), f32),
        ),
        in_specs=[smem] + [anywhere] * 11,
        out_specs=(vmem, vmem, vmem),
        scratch_shapes=[
            pltpu.VMEM((8 * v, nv), bf16),
            pltpu.VMEM((2 * nv + META, v), bf16),
            pltpu.VMEM((nz, nv + v, v), bf16),
            pltpu.VMEM((8, v, v), f32),
            pltpu.VMEM((2, META, v), bf16),
            pltpu.VMEM((3, 8, v), f32),
            pltpu.VMEM((3, 8, v), i32),
            pltpu.SMEM((3, 8, v), f32),
            pltpu.SMEM((3, 8, v), i32),
            pltpu.SMEM((128 + STEP,), i32),
            pltpu.SMEM((128 + STEP,), f32),
            pltpu.SemaphoreType.DMA((16,)),
        ],
        compiler_params=pltpu.CompilerParams(vmem_limit_bytes=8 * 1024 * 1024),
        cost_estimate=pl.CostEstimate(flops=0, bytes_accessed=12_000_000, transcendentals=0),
        name="couple",
    )(where, turned, x_near, x_far, x_own, z_full, *z_mine, *z_other)

    near_back = lax.ppermute(near, ("x", "c"), opposite(NX, NX - 1))
    far_back = lax.ppermute(far, "x", ring(NX, 2))
    kept, gone = pl.pallas_call(
        settle_kernel,
        out_shape=(jax.ShapeDtypeStruct((2, v, v), f32),) * 2,
        in_specs=[smem] + [vmem] * 4,
        out_specs=(vmem, vmem),
        compiler_params=pltpu.CompilerParams(vmem_limit_bytes=4 * 1024 * 1024),
        name="settle",
    )(where, local, near_back, far_back, own)
    share = kept + lax.ppermute(gone, "c", swap)
    share = share + lax.ppermute(share, ("y", "c"), partners(0))
    share = share + lax.ppermute(share, ("y", "c"), partners(1))
    other = lax.ppermute(share, "c", swap)
    total = jnp.where(
        c == 0, jnp.concatenate([share, other], axis=0), jnp.concatenate([other, share], axis=0)
    )
    diagonal = (energies[:, :, None] + energies[:, None, :] - pair_shift[:, None, None]) * amp_float
    inside = jnp.arange(v, dtype=i32)[None, :] < pno_count[:, None]
    return jnp.where(inside[:, :, None] & inside[:, None, :], total + diagonal, f32(0.0))


def solution(mesh):
    owners = mesh.devices.shape[0]
    fine = Mesh(mesh.devices.reshape(owners // NX, NX, NY, NC), ("z", "x", "y", "c"))
    pair, aux = ("z", "x"), ("y", "c")
    placed = (
        P(pair, None, None),
        P(pair, None, None),
        P(pair, None),
        P(pair),
        P(pair),
        P(pair, None),
        P(pair, None),
        P(pair, aux, None),
        P(pair, aux, None),
    )
    return jax.shard_map(
        shards, mesh=fine, in_specs=placed, out_specs=P(pair, None, None), check_vma=False
    )
```

time: 513 us -> 61 us (0.12)
  waiting for transfers between devices: 401 us -> 14 us
  matrix products: 34.1 us -> 3.81 us
  local copies, waits for them, and re-layouts: 28.6 us -> 3.49 us
  blocking collectives: 20.2 us -> 0 us
  starting transfers between devices: 11.5 us -> 29.7 us
  between operations: 13.5 us -> 0.12 us
  Pallas kernels: 0 us -> 8.57 us
    all_to_all x2 -> x0, waiting for transfers between devices: 323 us -> none  [the longest x1 261 us: shards(): lax.all_to_all(coefficients[asked_slots], 'pair', split_axis=0, concat_ax...]
    psum x1 -> x0, waiting for transfers between devices: 77.7 us -> none  [shards(): lax.psum((partial_exchange, partial_quadratic - coupling_share), 'aux')]
    dot_general x6 -> x3, matrix products: 34.1 us -> 3.81 us  [the longest x1 2.96 us: shards(): jnp.einsum('pqa,pqb->pab', slab_one, slab_two, preferred_element_type=f32)]
    ppermute x0 -> x14, starting transfers between devices: none -> 29.7 us  [the longest x1 6.48 us: shards(): z_one = lax.ppermute(z_full, ('z', 'c'), opposite(nz, 1))]
    gather x4 -> x0, local copies, waits for them, and re-layouts: 25.7 us -> none  [the longest x1 10.3 us: shards(): back_coef.reshape(owner_count * capacity, back_coef.shape[2], pno_width)]
    all_to_all x1 -> x0, blocking collectives: 20.2 us -> none  [shards(): lax.all_to_all(requests, 'pair', split_axis=0, concat_axis=0, tiled=True)]
    ppermute x0 -> x14, waiting for transfers between devices: none -> 14 us  [the longest x1 3.03 us: shards(): z_rest = lax.ppermute(z_rest, ('z', 'c'), opposite(nz, 2))]
    all_to_all x2 -> x0, starting transfers between devices: 11.5 us -> none  [the longest x1 6.64 us: shards(): lax.all_to_all(coefficients[asked_slots], 'pair', split_axis=0, concat_ax...]
  transfers between devices with their start and end apart: 3 -> 14, of which waited for: 3 -> 7; matrix products, arithmetic and copies ran while one was open for 4% -> 6% of each run, Pallas kernels for 0% -> 1%
where the time goes in v2:
time: 61 us; the launch traced here: 60.8 us
  starting transfers between devices  29.7 us (49%)
  waiting for transfers between devices  14 us (23%)
  Pallas kernels  8.57 us (14%)
  matrix products  3.81 us (6%)
  local copies, waits for them, and re-layouts  3.49 us (6%)
  other arithmetic  1.11 us (2%)
    ppermute x1, starting transfers between devices, shards(): z_one = lax.ppermute(z_full, ('z', 'c'), opposite(nz, 1))  6.48 us
    pallas_call x1, Pallas kernels, shards(): pl.pallas_call(couple_kernel, out_shape=(jax.ShapeDtypeStruct((4, v, v),...  5.32 us
    unnamed x18, local copies, waits for them, and re-layouts  3.49 us
    ppermute x1, starting transfers between devices, shards(): z_rest = lax.ppermute(z_rest, ('z', 'c'), opposite(nz, 2))  3.22 us
    ppermute x1, waiting for transfers between devices, shards(): z_rest = lax.ppermute(z_rest, ('z', 'c'), opposite(nz, 2))  3.03 us
    dot_general x1, matrix products, shards(): jnp.einsum('pqa,pqb->pab', slab_one, slab_two, preferred_element_type=f32)  2.96 us
    ppermute x1, waiting for transfers between devices, shards(): share = share + lax.ppermute(share, ('y', 'c'), partners(0))  2.84 us
    ppermute x1, waiting for transfers between devices, shards(): share = share + lax.ppermute(share, ('y', 'c'), partners(1))  2.81 us
  transfers between devices with their start and end apart: 14, of which 7 were waited for; matrix products, arithmetic and copies ran while one was open for 6% of the time, Pallas kernels for 1%

profile of v2, /device:TPU:1, one launch (start us, length us, event | category | flops | bytes accessed | tf_op | source)
XLA Modules:
  0.0 60.8 jit_solution(7939351024850979288)
XLA Ops:
  0.0 0.0 copy-start
  0.0 0.1 pad_add_fusion.where
  0.1 0.0 copy-start.1
  0.1 1.1 %copy-done.1 = bf16[4,128,128]{2,1,0:T(8,128)(2,1)S(1)} copy-done((bf16[4,128,128]{2,1,0:T(8,128)(2,1)S(1)}, bf16[4,128,128]{2,1,0:T(8,128)(2,1)}, u32[]{:S(2)}) %copy-start.1) | copy-done | bytes 131096
  1.1 0.0 copy-start.3
  1.1 1.0 %copy-done.3 = bf16[4,512,128]{2,1,0:T(8,128)(2,1)S(1)} copy-done((bf16[4,512,128]{2,1,0:T(8,128)(2,1)S(1)}, bf16[4,512,128]{2,1,0:T(8,128)(2,1)}, u32[]{:S(2)}) %copy-start.3) | copy-done | bytes 524312
  2.2 0.0 copy-start.4
  2.2 0.7 %copy-done.4 = s32[4,16]{1,0:T(4,128)S(1)} copy-done((s32[4,16]{1,0:T(4,128)S(1)}, s32[4,16]{1,0:T(4,128)}, u32[]{:S(2)}) %copy-start.4) | copy-done | bytes 280
  2.9 0.0 copy-start.5
  2.9 0.7 %copy-done.5 = f32[4,16]{1,0:T(4,128)S(1)} copy-done((f32[4,16]{1,0:T(4,128)S(1)}, f32[4,16]{1,0:T(4,128)}, u32[]{:S(2)}) %copy-start.5) | copy-done | bytes 280
  3.5 1.9 %prepare.1 = (bf16[640,128]{1,0:T(8,128)(2,1)S(1)}, bf16[2064,128]{1,0:T(8,128)(2,1)S(1)}, bf16[1040,128]{1,0:T(8,128)(2,1)S(1)}) custom-call(s32[4]{0:T(128)S(1)} %pad_add_fusion.where, s32[4,16]{1,0:T(4,128)S(1)} %copy-done.4, f32[4,16]{1,0:T(4,128)S(1)} %copy-done.5, bf16[4,512,128]{2,1,0:T(8,128)(2,1)S(1)} %copy-done.3, bf16[4,128,128]{2,1,0:T(8,128)(2,1)S(1)} %copy-done.1), custom_call_target="tpu_custom_call" | custom-call | tf_op jit(solution)/shard_map/prepare/pallas_call | solution.py:209
  5.4 6.5 %collective-permute-start.2 = (bf16[640,128]{1,0:T(8,128)(2,1)S(1)}, bf16[640,128]{1,0:T(8,128)(2,1)S(1)}, u32[]{:S(2)}, u32[]{:S(2)}) collective-permute-start(bf16[640,128]{1,0:T(8,128)(2,1)S(1)} %get-tuple-element.15.z_full), channel_id=1, source_target_pairs={{0,32},{32,64},{64,96},{96,128},{128,160},{160,192},{192,224},{224... | collective-permute-start | bytes 491528 | tf_op jit(solution)/shard_map/ppermute | solution.py:224
  11.9 1.2 %collective-permute-start.3 = (bf16[640,128]{1,0:T(8,128)(2,1)S(1)}, bf16[640,128]{1,0:T(8,128)(2,1)S(1)}, u32[]{:S(2)}, u32[]{:S(2)}) collective-permute-start(bf16[640,128]{1,0:T(8,128)(2,1)S(1)} %get-tuple-element.15.z_full), channel_id=1, source_target_pairs={{0,64},{32,96},{64,128},{96,160},{128,192},{160,224},{192,0},{224,... | collective-permute-start | bytes 491528 | tf_op jit(solution)/shard_map/ppermute | solution.py:225
  13.1 0.0 copy-start.2
  13.1 2.5 %collective-permute-start = (bf16[2064,128]{1,0:T(8,128)(2,1)S(1)}, bf16[2064,128]{1,0:T(8,128)(2,1)S(1)}, u32[]{:S(2)}, u32[]{:S(2)}) collective-permute-start(bf16[2064,128]{1,0:T(8,128)(2,1)S(1)} %get-tuple-element.13), channel_id=1, source_target_pairs={{0,8},{8,16},{16,24},{24,0},{1,25},{9,1},{17,9},{25,17},{2,10},{10... | collective-permute-start | bytes 1585160 | tf_op jit(solution)/shard_map/ppermute | solution.py:226
  15.5 0.0 copy-done
  15.6 3.0 %fusion.3.after = f32[4,128,128]{2,1,0:T(8,128)S(1)} fusion(bf16[4,3072,128]{2,1,0:T(8,128)(2,1)S(1)} %copy-done, bf16[4,3072,128]{2,1,0:T(8,128)(2,1)} %param.17), kind=kOutput, calls=%fused_computation.7 | convolution fusion | flops 402653184 | bytes 6553600 | tf_op jit(solution)/shard_map/pqa,pqb->pab/dot_general | solution.py:228
  18.5 0.0 collective-permute-done.2.first.refs_0_
  18.5 0.0 collective-permute-done.3.second.refs_1_
  18.5 0.6 pack.1
  19.1 3.2 %collective-permute-start.4 = (bf16[960,128]{1,0:T(8,128)(2,1)S(1)}, bf16[960,128]{1,0:T(8,128)(2,1)S(1)}, u32[]{:S(2)}, u32[]{:S(2)}) collective-permute-start(bf16[960,128]{1,0:T(8,128)(2,1)S(1)} %pack.1), channel_id=1, source_target_pairs={{0,64},{32,96},{64,128},{96,160},{128,192},{160,224},{192,0},{224,... | collective-permute-start | bytes 737288 | tf_op jit(solution)/shard_map/ppermute | solution.py:242
  22.3 2.7 %collective-permute-start.1 = (bf16[1040,128]{1,0:T(8,128)(2,1)S(1)}, bf16[1040,128]{1,0:T(8,128)(2,1)S(1)}, u32[]{:S(2)}, u32[]{:S(2)}) collective-permute-start(bf16[1040,128]{1,0:T(8,128)(2,1)S(1)} %get-tuple-element.14.own.x_own), channel_id=1, source_target_pairs={{0,16},{8,24},{16,0},{24,8},{1,17},{9,25},{17,1},{25,9},{2,18},{10... | collective-permute-start | bytes 798728 | tf_op jit(solution)/shard_map/ppermute | solution.py:227
  25.1 3.0 %collective-permute-done.4.refs_2_ = bf16[960,128]{1,0:T(8,128)(2,1)S(1)} collective-permute-done((bf16[960,128]{1,0:T(8,128)(2,1)S(1)}, bf16[960,128]{1,0:T(8,128)(2,1)S(1)}, u32[]{:S(2)}, u32[]{:S(2)}) %collective-permute-start.4) | collective-permute-done | bytes 245792 | tf_op jit(solution)/shard_map/ppermute | solution.py:242
  28.1 0.9 %collective-permute-start.7 = (bf16[960,128]{1,0:T(8,128)(2,1)S(1)}, bf16[960,128]{1,0:T(8,128)(2,1)S(1)}, u32[]{:S(2)}, u32[]{:S(2)}) collective-permute-start(bf16[960,128]{1,0:T(8,128)(2,1)S(1)} %collective-permute-done.4.refs_2_), channel_id=1, source_target_pairs={{0,1},{1,0},{2,3},{3,2},{4,5},{5,4},{6,7},{7,6},{8,9},{9,8},{10,11... | collective-permute-start | bytes 737288 | tf_op jit(solution)/shard_map/ppermute | solution.py:244
  29.0 0.0 collective-permute-start.5
  29.0 0.5 collective-permute-start.6
  29.5 0.0 copy-done.2
  29.5 0.4 fusion.4
  29.9 0.0 collective-permute-done.near.x_near
  29.9 0.3 turn.1.turned
  30.2 0.0 copy-start.8
  30.2 0.0 copy-start.6
  30.2 0.0 copy-start.7
  30.2 0.9 %collective-permute-done.1.x_far = bf16[1040,128]{1,0:T(8,128)(2,1)S(1)} collective-permute-done((bf16[1040,128]{1,0:T(8,128)(2,1)S(1)}, bf16[1040,128]{1,0:T(8,128)(2,1)S(1)}, u32[]{:S(2)}, u32[]{:S(2)}) %collective-permute-start.1) | collective-permute-done | bytes 266272 | tf_op jit(solution)/shard_map/ppermute | solution.py:227
  31.1 0.0 collective-permute-done.5.refs_3_
  31.1 0.0 collective-permute-done.6.refs_4_
  31.1 0.0 collective-permute-done.7.refs_5_
  31.1 5.3 %couple.1 = (bf16[4,128,128]{2,1,0:T(8,128)(2,1)S(1)}, bf16[2,128,128]{2,1,0:T(8,128)(2,1)S(1)}, f32[2,128,128]{2,1,0:T(8,128)S(1)}) custom-call(s32[4]{0:T(128)S(1)} %pad_add_fusion.where, bf16[768,512]{1,0:T(8,128)(2,1)S(1)} %turn.1.turned, bf16[2064,128]{1,0:T(8,128)(2,1)S(1)} %collective-permute-done.near.x_near, ...), custom_call_target="tpu_custom_call" | custom-call | bytes 12000000 | tf_op jit(solution)/shard_map/couple/pallas_call | solution.py:255
  36.4 1.8 %collective-permute-start.8 = (bf16[4,128,128]{2,1,0:T(8,128)(2,1)S(1)}, bf16[4,128,128]{2,1,0:T(8,128)(2,1)S(1)}, u32[]{:S(2)}, u32[]{:S(2)}) collective-permute-start(bf16[4,128,128]{2,1,0:T(8,128)(2,1)S(1)} %get-tuple-element.16), channel_id=1, source_target_pairs={{0,24},{8,0},{16,8},{24,16},{1,9},{9,17},{17,25},{25,1},{2,26},{10... | collective-permute-start | bytes 393224 | tf_op jit(solution)/shard_map/ppermute | solution.py:283
  38.3 2.2 %collective-permute-start.9 = (bf16[2,128,128]{2,1,0:T(8,128)(2,1)S(1)}, bf16[2,128,128]{2,1,0:T(8,128)(2,1)S(1)}, u32[]{:S(2)}, u32[]{:S(2)}) collective-permute-start(bf16[2,128,128]{2,1,0:T(8,128)(2,1)S(1)} %get-tuple-element.17), channel_id=1, source_target_pairs={{0,16},{8,24},{16,0},{24,8},{1,17},{9,25},{17,1},{25,9},{2,18},{10... | collective-permute-start | bytes 196616 | tf_op jit(solution)/shard_map/ppermute | solution.py:284
  40.4 0.4 fusion.local
  40.9 2.5 %collective-permute-done.9.far = bf16[2,128,128]{2,1,0:T(8,128)(2,1)S(1)} collective-permute-done((bf16[2,128,128]{2,1,0:T(8,128)(2,1)S(1)}, bf16[2,128,128]{2,1,0:T(8,128)(2,1)S(1)}, u32[]{:S(2)}, u32[]{:S(2)}) %collective-permute-start.9) | collective-permute-done | bytes 65568 | tf_op jit(solution)/shard_map/ppermute | solution.py:284
  43.4 0.0 collective-permute-done.8.near
  43.4 0.6 settle.1
  44.0 2.1 %collective-permute-start.10 = (f32[2,128,128]{2,1,0:T(8,128)S(1)}, f32[2,128,128]{2,1,0:T(8,128)S(1)}, u32[]{:S(2)}, u32[]{:S(2)}) collective-permute-start(f32[2,128,128]{2,1,0:T(8,128)S(1)} %get-tuple-element.20), channel_id=1, source_target_pairs={{0,1},{1,0},{2,3},{3,2},{4,5},{5,4},{6,7},{7,6},{8,9},{9,8},{10,11... | collective-permute-start | bytes 393224 | tf_op jit(solution)/shard_map/ppermute | solution.py:293
  46.1 1.0 %collective-permute-done.10 = f32[2,128,128]{2,1,0:T(8,128)S(1)} collective-permute-done((f32[2,128,128]{2,1,0:T(8,128)S(1)}, f32[2,128,128]{2,1,0:T(8,128)S(1)}, u32[]{:S(2)}, u32[]{:S(2)}) %collective-permute-start.10) | collective-permute-done | bytes 131104 | tf_op jit(solution)/shard_map/ppermute | solution.py:293
  47.1 2.3 %collective-permute-start.11 = (f32[2,128,128]{2,1,0:T(8,128)S(1)}, f32[2,128,128]{2,1,0:T(8,128)S(1)}, u32[]{:S(2)}, u32[]{:S(2)}) collective-permute-start(f32[2,128,128]{2,1,0:T(8,128)S(1)} %add.29), channel_id=1, source_target_pairs={{0,2},{1,7},{2,0},{3,5},{4,6},{5,3},{6,4},{7,1},{8,10},{9,15},{10,... | collective-permute-start | bytes 393224 | tf_op jit(solution)/shard_map/ppermute | solution.py:294
  49.4 2.8 %collective-permute-done.11 = f32[2,128,128]{2,1,0:T(8,128)S(1)} collective-permute-done((f32[2,128,128]{2,1,0:T(8,128)S(1)}, f32[2,128,128]{2,1,0:T(8,128)S(1)}, u32[]{:S(2)}, u32[]{:S(2)}) %collective-permute-start.11) | collective-permute-done | bytes 131104 | tf_op jit(solution)/shard_map/ppermute | solution.py:294
  52.2 1.1 %collective-permute-start.12 = (f32[2,128,128]{2,1,0:T(8,128)S(1)}, f32[2,128,128]{2,1,0:T(8,128)S(1)}, u32[]{:S(2)}, u32[]{:S(2)}) collective-permute-start(f32[2,128,128]{2,1,0:T(8,128)S(1)} %add.30), channel_id=1, source_target_pairs={{0,6},{1,3},{2,4},{3,1},{4,2},{5,7},{6,0},{7,5},{8,14},{9,11},{10,... | collective-permute-start | bytes 393224 | tf_op jit(solution)/shard_map/ppermute | solution.py:295
  53.3 2.8 %collective-permute-done.12 = f32[2,128,128]{2,1,0:T(8,128)S(1)} collective-permute-done((f32[2,128,128]{2,1,0:T(8,128)S(1)}, f32[2,128,128]{2,1,0:T(8,128)S(1)}, u32[]{:S(2)}, u32[]{:S(2)}) %collective-permute-start.12) | collective-permute-done | bytes 131104 | tf_op jit(solution)/shard_map/ppermute | solution.py:295
  56.2 2.7 %collective-permute-start.13 = (f32[2,128,128]{2,1,0:T(8,128)S(1)}, f32[2,128,128]{2,1,0:T(8,128)S(1)}, u32[]{:S(2)}, u32[]{:S(2)}) collective-permute-start(f32[2,128,128]{2,1,0:T(8,128)S(1)} %add.31), channel_id=1, source_target_pairs={{0,1},{1,0},{2,3},{3,2},{4,5},{5,4},{6,7},{7,6},{8,9},{9,8},{10,11... | collective-permute-start | bytes 393224 | tf_op jit(solution)/shard_map/ppermute | solution.py:296
  58.9 0.0 copy-done.8
  58.9 0.1 iota_compare_fusion
  59.0 0.9 %collective-permute-done.13 = f32[2,128,128]{2,1,0:T(8,128)S(1)} collective-permute-done((f32[2,128,128]{2,1,0:T(8,128)S(1)}, f32[2,128,128]{2,1,0:T(8,128)S(1)}, u32[]{:S(2)}, u32[]{:S(2)}) %collective-permute-start.13) | collective-permute-done | bytes 131104 | tf_op jit(solution)/shard_map/ppermute | solution.py:296
  59.9 0.0 copy-done.6
  59.9 0.0 copy-done.7
  59.9 0.9 %fusion.2 = f32[4,128,128]{2,1,0:T(8,128)} fusion(f32[2,128,128]{2,1,0:T(8,128)S(1)} %collective-permute-done.13, f32[2,128,128]{2,1,0:T(8,128)S(1)} %add.31, bf16[4,128,128]{2,1,0:T(8,128)(2,1)S(1)} %copy-done.2, f32[4]{0:T(128)S(1)} %copy-done.7, f32[4,128]{1,0:T(4,128)S(1)} %copy-done.6, pred[]{:T(512)S(6)} %eq.3, pred[4,128]{1,0:T(4,128)(4,1)S(1)} %iota_compare_fusion), kind=kLoop, calls=%fused_computation.4 | loop fusion | flops 655360 | bytes 657937 | tf_op jit(solution)/shard_map/jit(_where)/select_n | solution.py:302
  (3 shorter events, 0.0 us)
Async XLA Ops:
  0.0 15.5 %copy-start = (bf16[4,3072,128]{2,1,0:T(8,128)(2,1)S(1)}, bf16[4,3072,128]{2,1,0:T(8,128)(2,1)}, u32[]{:S(2)}) copy-start(bf16[4,3072,128]{2,1,0:T(8,128)(2,1)} %param.16) | copy-start | bytes 9437188
  0.1 1.1 %copy-start.1 = (bf16[4,128,128]{2,1,0:T(8,128)(2,1)S(1)}, bf16[4,128,128]{2,1,0:T(8,128)(2,1)}, u32[]{:S(2)}) copy-start(bf16[4,128,128]{2,1,0:T(8,128)(2,1)} %amp.1) | copy-start | bytes 393220
  1.1 1.0 %copy-start.3 = (bf16[4,512,128]{2,1,0:T(8,128)(2,1)S(1)}, bf16[4,512,128]{2,1,0:T(8,128)(2,1)}, u32[]{:S(2)}) copy-start(bf16[4,512,128]{2,1,0:T(8,128)(2,1)} %coef.1) | copy-start | bytes 1572868
  2.2 0.7 %copy-start.4 = (s32[4,16]{1,0:T(4,128)S(1)}, s32[4,16]{1,0:T(4,128)}, u32[]{:S(2)}) copy-start(s32[4,16]{1,0:T(4,128)} %pairs.1) | copy-start | bytes 772
  2.9 0.7 %copy-start.5 = (f32[4,16]{1,0:T(4,128)S(1)}, f32[4,16]{1,0:T(4,128)}, u32[]{:S(2)}) copy-start(f32[4,16]{1,0:T(4,128)} %weights.1) | copy-start | bytes 772
  5.4 13.1 %collective-permute-start.2 = (bf16[640,128]{1,0:T(8,128)(2,1)S(1)}, bf16[640,128]{1,0:T(8,128)(2,1)S(1)}, u32[]{:S(2)}, u32[]{:S(2)}) collective-permute-start(bf16[640,128]{1,0:T(8,128)(2,1)S(1)} %get-tuple-element.15.z_full), channel_id=1, source_target_pairs={{0,32},{32,64},{64,96},{96,128},{128,160},{160,192},{192,224},{224... | collective-permute-start | bytes 491528 | tf_op jit(solution)/shard_map/ppermute | solution.py:224
  11.9 6.6 %collective-permute-start.3 = (bf16[640,128]{1,0:T(8,128)(2,1)S(1)}, bf16[640,128]{1,0:T(8,128)(2,1)S(1)}, u32[]{:S(2)}, u32[]{:S(2)}) collective-permute-start(bf16[640,128]{1,0:T(8,128)(2,1)S(1)} %get-tuple-element.15.z_full), channel_id=1, source_target_pairs={{0,64},{32,96},{64,128},{96,160},{128,192},{160,224},{192,0},{224,... | collective-permute-start | bytes 491528 | tf_op jit(solution)/shard_map/ppermute | solution.py:225
  13.1 16.4 %copy-start.2 = (bf16[4,128,128]{2,1,0:T(8,128)(2,1)S(1)}, bf16[4,128,128]{2,1,0:T(8,128)(2,1)}, u32[]{:S(2)}) copy-start(bf16[4,128,128]{2,1,0:T(8,128)(2,1)} %amp.1) | copy-start | bytes 393220
  13.1 16.8 %collective-permute-start = (bf16[2064,128]{1,0:T(8,128)(2,1)S(1)}, bf16[2064,128]{1,0:T(8,128)(2,1)S(1)}, u32[]{:S(2)}, u32[]{:S(2)}) collective-permute-start(bf16[2064,128]{1,0:T(8,128)(2,1)S(1)} %get-tuple-element.13), channel_id=1, source_target_pairs={{0,8},{8,16},{16,24},{24,0},{1,25},{9,1},{17,9},{25,17},{2,10},{10... | collective-permute-start | bytes 1585160 | tf_op jit(solution)/shard_map/ppermute | solution.py:226
  19.1 9.0 %collective-permute-start.4 = (bf16[960,128]{1,0:T(8,128)(2,1)S(1)}, bf16[960,128]{1,0:T(8,128)(2,1)S(1)}, u32[]{:S(2)}, u32[]{:S(2)}) collective-permute-start(bf16[960,128]{1,0:T(8,128)(2,1)S(1)} %pack.1), channel_id=1, source_target_pairs={{0,64},{32,96},{64,128},{96,160},{128,192},{160,224},{192,0},{224,... | collective-permute-start | bytes 737288 | tf_op jit(solution)/shard_map/ppermute | solution.py:242
  22.3 8.8 %collective-permute-start.1 = (bf16[1040,128]{1,0:T(8,128)(2,1)S(1)}, bf16[1040,128]{1,0:T(8,128)(2,1)S(1)}, u32[]{:S(2)}, u32[]{:S(2)}) collective-permute-start(bf16[1040,128]{1,0:T(8,128)(2,1)S(1)} %get-tuple-element.14.own.x_own), channel_id=1, source_target_pairs={{0,16},{8,24},{16,0},{24,8},{1,17},{9,25},{17,1},{25,9},{2,18},{10... | collective-permute-start | bytes 798728 | tf_op jit(solution)/shard_map/ppermute | solution.py:227
  28.1 3.0 %collective-permute-start.7 = (bf16[960,128]{1,0:T(8,128)(2,1)S(1)}, bf16[960,128]{1,0:T(8,128)(2,1)S(1)}, u32[]{:S(2)}, u32[]{:S(2)}) collective-permute-start(bf16[960,128]{1,0:T(8,128)(2,1)S(1)} %collective-permute-done.4.refs_2_), channel_id=1, source_target_pairs={{0,1},{1,0},{2,3},{3,2},{4,5},{5,4},{6,7},{7,6},{8,9},{9,8},{10,11... | collective-permute-start | bytes 737288 | tf_op jit(solution)/shard_map/ppermute | solution.py:244
  29.0 2.1 %collective-permute-start.5 = (bf16[640,128]{1,0:T(8,128)(2,1)S(1)}, bf16[640,128]{1,0:T(8,128)(2,1)S(1)}, u32[]{:S(2)}, u32[]{:S(2)}) collective-permute-start(bf16[640,128]{1,0:T(8,128)(2,1)S(1)} %collective-permute-done.2.first.refs_0_), channel_id=1, source_target_pairs={{0,1},{1,0},{2,3},{3,2},{4,5},{5,4},{6,7},{7,6},{8,9},{9,8},{10,11... | collective-permute-start | bytes 491528 | tf_op jit(solution)/shard_map/ppermute | solution.py:244
  29.0 2.1 %collective-permute-start.6 = (bf16[640,128]{1,0:T(8,128)(2,1)S(1)}, bf16[640,128]{1,0:T(8,128)(2,1)S(1)}, u32[]{:S(2)}, u32[]{:S(2)}) collective-permute-start(bf16[640,128]{1,0:T(8,128)(2,1)S(1)} %collective-permute-done.3.second.refs_1_), channel_id=1, source_target_pairs={{0,1},{1,0},{2,3},{3,2},{4,5},{5,4},{6,7},{7,6},{8,9},{9,8},{10,11... | collective-permute-start | bytes 491528 | tf_op jit(solution)/shard_map/ppermute | solution.py:244
  30.2 28.8 %copy-start.8 = (s32[4]{0:T(128)S(1)}, s32[4]{0:T(128)}, u32[]{:S(2)}) copy-start(s32[4]{0:T(128)} %param.13) | copy-start | bytes 52
  30.2 29.7 %copy-start.6 = (f32[4,128]{1,0:T(4,128)S(1)}, f32[4,128]{1,0:T(4,128)}, u32[]{:S(2)}) copy-start(f32[4,128]{1,0:T(4,128)} %param.11) | copy-start | bytes 6148
  30.2 29.7 %copy-start.7 = (f32[4]{0:T(128)S(1)}, f32[4]{0:T(128)}, u32[]{:S(2)}) copy-start(f32[4]{0:T(128)} %param.12) | copy-start | bytes 52
  36.4 7.0 %collective-permute-start.8 = (bf16[4,128,128]{2,1,0:T(8,128)(2,1)S(1)}, bf16[4,128,128]{2,1,0:T(8,128)(2,1)S(1)}, u32[]{:S(2)}, u32[]{:S(2)}) collective-permute-start(bf16[4,128,128]{2,1,0:T(8,128)(2,1)S(1)} %get-tuple-element.16), channel_id=1, source_target_pairs={{0,24},{8,0},{16,8},{24,16},{1,9},{9,17},{17,25},{25,1},{2,26},{10... | collective-permute-start | bytes 393224 | tf_op jit(solution)/shard_map/ppermute | solution.py:283
  38.3 5.1 %collective-permute-start.9 = (bf16[2,128,128]{2,1,0:T(8,128)(2,1)S(1)}, bf16[2,128,128]{2,1,0:T(8,128)(2,1)S(1)}, u32[]{:S(2)}, u32[]{:S(2)}) collective-permute-start(bf16[2,128,128]{2,1,0:T(8,128)(2,1)S(1)} %get-tuple-element.17), channel_id=1, source_target_pairs={{0,16},{8,24},{16,0},{24,8},{1,17},{9,25},{17,1},{25,9},{2,18},{10... | collective-permute-start | bytes 196616 | tf_op jit(solution)/shard_map/ppermute | solution.py:284
  44.0 3.1 %collective-permute-start.10 = (f32[2,128,128]{2,1,0:T(8,128)S(1)}, f32[2,128,128]{2,1,0:T(8,128)S(1)}, u32[]{:S(2)}, u32[]{:S(2)}) collective-permute-start(f32[2,128,128]{2,1,0:T(8,128)S(1)} %get-tuple-element.20), channel_id=1, source_target_pairs={{0,1},{1,0},{2,3},{3,2},{4,5},{5,4},{6,7},{7,6},{8,9},{9,8},{10,11... | collective-permute-start | bytes 393224 | tf_op jit(solution)/shard_map/ppermute | solution.py:293
  47.1 5.1 %collective-permute-start.11 = (f32[2,128,128]{2,1,0:T(8,128)S(1)}, f32[2,128,128]{2,1,0:T(8,128)S(1)}, u32[]{:S(2)}, u32[]{:S(2)}) collective-permute-start(f32[2,128,128]{2,1,0:T(8,128)S(1)} %add.29), channel_id=1, source_target_pairs={{0,2},{1,7},{2,0},{3,5},{4,6},{5,3},{6,4},{7,1},{8,10},{9,15},{10,... | collective-permute-start | bytes 393224 | tf_op jit(solution)/shard_map/ppermute | solution.py:294
  52.2 3.9 %collective-permute-start.12 = (f32[2,128,128]{2,1,0:T(8,128)S(1)}, f32[2,128,128]{2,1,0:T(8,128)S(1)}, u32[]{:S(2)}, u32[]{:S(2)}) collective-permute-start(f32[2,128,128]{2,1,0:T(8,128)S(1)} %add.30), channel_id=1, source_target_pairs={{0,6},{1,3},{2,4},{3,1},{4,2},{5,7},{6,0},{7,5},{8,14},{9,11},{10,... | collective-permute-start | bytes 393224 | tf_op jit(solution)/shard_map/ppermute | solution.py:295
  56.2 3.7 %collective-permute-start.13 = (f32[2,128,128]{2,1,0:T(8,128)S(1)}, f32[2,128,128]{2,1,0:T(8,128)S(1)}, u32[]{:S(2)}, u32[]{:S(2)}) collective-permute-start(f32[2,128,128]{2,1,0:T(8,128)S(1)} %add.31), channel_id=1, source_target_pairs={{0,1},{1,0},{2,3},{3,2},{4,5},{5,4},{6,7},{7,6},{8,9},{9,8},{10,11... | collective-permute-start | bytes 393224 | tf_op jit(solution)/shard_map/ppermute | solution.py:296

commit v3 on v2

v3 whole, which is shorter than its diff:
```python
import jax
import jax.numpy as jnp
from jax import lax
from jax.experimental import pallas as pl
from jax.experimental.pallas import tpu as pltpu
from jax.sharding import Mesh
from jax.sharding import PartitionSpec as P

NX, NY, NC = 4, 4, 2
META = 16
STEP = 4


def opposite(size, step):
    up = [(i * NC, ((i + step) % size) * NC) for i in range(size)]
    down = [(i * NC + 1, ((i - step) % size) * NC + 1) for i in range(size)]
    return up + down


def ring(size, step):
    return [(i, (i + step) % size) for i in range(size)]


def partners(turn):
    table = ([1, 0, 3, 2], [3, 2, 1, 0])
    return [
        (y * NC + c, table[(turn + c) % 2][y] * NC + c) for y in range(NY) for c in range(NC)
    ]


def prepare_kernel(pairs, weights, coef, amp, z_full, x_all, x_own, pairs_v, weights_v, sem):
    y, c = lax.axis_index("y"), lax.axis_index("c")
    _, nv, v = coef.shape
    copies = []

    def fetch(src, dst):
        copy = pltpu.make_async_copy(src, dst, sem.at[len(copies)])
        copy.start()
        copies.append(copy)

    fetch(pairs, pairs_v)
    fetch(weights, weights_v)
    at = 0
    for part in range(NC):
        for ref, size in ((coef, nv // NC), (amp, v // NC)):
            fetch(ref.at[y, pl.ds(part * size, size)], z_full.at[pl.ds(at, size)])
            at += size
    for s in range(4):
        fetch(coef.at[s], x_all.at[pl.ds(s * nv, nv)])
    for s in range(2):
        fetch(coef.at[2 * c + s], x_own.at[pl.ds(s * nv, nv)])
    copies[0].wait()
    copies[1].wait()
    weight = weights_v[...]
    first = weight.astype(jnp.bfloat16).astype(jnp.float32)
    second = (weight - first).astype(jnp.bfloat16).astype(jnp.float32)
    third = weight - first - second
    meta = jnp.concatenate([pairs_v[...].astype(jnp.float32), first, second, third], axis=0)
    meta = meta.astype(jnp.bfloat16)
    for ref, start in ((x_all, 4 * nv), (x_own, 2 * nv)):
        ref[start : start + META, :] = jnp.zeros((META, v), jnp.bfloat16)
        ref[start : start + META, : meta.shape[1]] = meta
    for copy in copies[2:]:
        copy.wait()


def couple_kernel(where, x_near, x_own, x_far, z_full, *refs):
    z, x, y, c = where[0], where[1], where[2], where[3]
    mine, other = refs[:4], refs[4:8]
    near, far, own, left, q, acc, meta_f, meta_i, sm_f, sm_i, codes, sem = refs[8:]
    nz, rows, v = q.shape
    nv = rows - v
    half, amp_half = nv // NC, v // NC
    sources = ((x_near, 4), (x_own, 2), (x_far, 2))
    for i, (ref, slots) in enumerate(sources):
        block = ref[slots * nv : slots * nv + META, :].astype(jnp.float32)
        meta_i[4 * i : 4 * i + 4, :] = block[:4].astype(jnp.int32)
        meta_f[4 * i : 4 * i + 4, :] = block[4:8] + block[8:12] + block[12:16]
    copy_i = pltpu.make_async_copy(meta_i, sm_i, sem.at[0])
    copy_f = pltpu.make_async_copy(meta_f, sm_f, sem.at[1])
    copy_i.start()
    copy_f.start()
    at = 0
    for ref, slots in sources:
        for s in range(slots):
            left[at * v : (at + 1) * v, :] = ref[s * nv : (s + 1) * nv, :].T
            at += 1
    acc[...] = jnp.zeros_like(acc)
    sign = 1 - 2 * c
    across = lax.rem(z + 4, nz)
    step = half + amp_half

    def place(at, part, block):
        q[at, pl.ds(pl.multiple_of(part * half, half), half), :] = block[:half]
        q[at, pl.ds(pl.multiple_of(nv + part * amp_half, amp_half), amp_half), :] = block[half:]

    for part in range(NC):
        lower = slice(part * step, (part + 1) * step)
        place(z, part, z_full[lower, :])
        for blocks, away in ((mine, -sign), (other, sign)):
            for k in range(1, 4):
                place(lax.rem(z + away * k + nz, nz), part, blocks[k - 1][lower, :])
    place(across, c, mine[3][...])
    place(across, 1 - c, other[3][...])
    copy_i.wait()
    copy_f.wait()
    found = 0
    wanted = x * 4 + y
    for p in range(8):
        row = p if p < 4 else 4 * (p // 2 - 1) + 2 * c + p % 2
        base = row * 128 + p * 16
        ids = [sm_i[row, k] for k in range(16)]
        values = [
            lax.shift_left(lax.shift_right_logical(n, 4), 11) + (base + k)
            for k, n in enumerate(ids)
        ]
        hits = [jnp.where((n & 15) == wanted, 1, 0) for n in ids]
        for value, hit in zip(values, hits):
            codes[found] = value
            found = found + hit
    for j in range(STEP - 1):
        codes[found + j] = -1

    def several(i, carry):
        code = [codes[i * STEP + j] for j in range(STEP)]
        used = [jnp.where(n >= 0, 1.0, 0.0) for n in code]
        code = [jnp.maximum(n, 0) for n in code]
        ps = [lax.shift_right_logical(n, 4) & 7 for n in code]
        zs = [lax.shift_right_logical(n, 11) for n in code]
        weights = [sm_f[lax.shift_right_logical(n, 7) & 15, n & 15] * u for n, u in zip(code, used)]
        inter = [
            jnp.dot(
                left[pl.ds(pl.multiple_of(p * v, v), v), :],
                q[zq, :nv, :],
                preferred_element_type=jnp.float32,
            ).astype(jnp.bfloat16)
            for p, zq in zip(ps, zs)
        ]
        mid = [
            jnp.dot(a, q[zq, nv:, :], preferred_element_type=jnp.float32).astype(jnp.bfloat16)
            for a, zq in zip(inter, zs)
        ]
        proj = [
            lax.dot_general(m, a, (((1,), (1,)), ((), ())), preferred_element_type=jnp.float32)
            .astype(jnp.bfloat16)
            .astype(jnp.float32)
            for m, a in zip(mid, inter)
        ]
        for weight, p, value in zip(weights, ps, proj):
            acc[p] += weight * value
        return carry

    lax.fori_loop(0, (found + STEP - 1) // STEP, several, 0)
    near[...] = acc[:4].astype(jnp.bfloat16)
    own[...] = acc[4:6]
    far[...] = acc[6:8].astype(jnp.bfloat16)


def settle_kernel(where, local, near, far, own, kept, gone):
    c = where[3]
    for s in range(2):
        gone[s] = local[2 * (1 - c) + s] - near[2 * (1 - c) + s].astype(jnp.float32)
        kept[s] = local[2 * c + s] - near[2 * c + s].astype(jnp.float32) - (
            own[s] + far[s].astype(jnp.float32)
        )


def shards(
    amplitudes,
    coefficients,
    energies,
    pair_shift,
    pno_count,
    coupled_pairs,
    coupling_weight,
    slab_one,
    slab_two,
):
    pairs, v, _ = amplitudes.shape
    nv = coefficients.shape[1]
    nz = lax.axis_size("z")
    where = jnp.stack([lax.axis_index(a) for a in ("z", "x", "y", "c")]).astype(jnp.int32)
    c = where[3]
    smem = pl.BlockSpec(memory_space=pltpu.SMEM)
    vmem = pl.BlockSpec(memory_space=pltpu.VMEM)
    anywhere = pl.BlockSpec(memory_space=pl.ANY)
    bf16, f32, i32 = jnp.bfloat16, jnp.float32, jnp.int32

    small = pltpu.CompilerParams(vmem_limit_bytes=4 * 1024 * 1024)
    half, amp_half = nv // NC, v // NC
    z_full, x_all, x_own = pl.pallas_call(
        prepare_kernel,
        out_shape=(
            jax.ShapeDtypeStruct((nv + v, v), bf16),
            jax.ShapeDtypeStruct((4 * nv + META, v), bf16),
            jax.ShapeDtypeStruct((2 * nv + META, v), bf16),
        ),
        in_specs=[anywhere] * 4,
        out_specs=(vmem,) * 3,
        scratch_shapes=[
            pltpu.VMEM(coupled_pairs.shape, i32),
            pltpu.VMEM(coupling_weight.shape, f32),
            pltpu.SemaphoreType.DMA((12,)),
        ],
        compiler_params=pltpu.CompilerParams(vmem_limit_bytes=62 * 1024 * 1024),
        name="prepare",
    )(coupled_pairs, coupling_weight, coefficients, amplitudes)

    swap = ring(NC, 1)
    z_one = lax.ppermute(z_full, ("z", "c"), opposite(nz, 1))
    z_two = lax.ppermute(z_full, ("z", "c"), opposite(nz, 2))
    x_near = lax.ppermute(x_all, ("x", "c"), opposite(NX, 1))
    x_far = lax.ppermute(x_own, "x", ring(NX, 2))

    exchange = jnp.einsum("pqa,pqb->pab", slab_one, slab_two, preferred_element_type=f32)
    amp_float = amplitudes.astype(f32)
    right = jnp.einsum("pab,pbc->pac", exchange, amp_float, precision=lax.Precision.HIGHEST)
    quadratic = jnp.einsum("pba,pbc->pac", amp_float, right, precision=lax.Precision.HIGHEST)
    local = exchange + quadratic

    z_three = lax.ppermute(z_two, ("z", "c"), opposite(nz, 1))
    z_four = lax.dynamic_slice_in_dim(z_two, c * (half + amp_half), half + amp_half, 0)
    z_four = lax.ppermute(z_four, ("z", "c"), opposite(nz, 2))
    z_mine = [z_one, z_two, z_three, z_four]
    z_other = [lax.ppermute(b, "c", swap) for b in z_mine]

    near, far, own = pl.pallas_call(
        couple_kernel,
        out_shape=(
            jax.ShapeDtypeStruct((4, v, v), bf16),
            jax.ShapeDtypeStruct((2, v, v), bf16),
            jax.ShapeDtypeStruct((2, v, v), f32),
        ),
        in_specs=[smem] + [vmem] * 12,
        out_specs=(vmem, vmem, vmem),
        scratch_shapes=[
            pltpu.VMEM((8 * v, nv), bf16),
            pltpu.VMEM((nz, nv + v, v), bf16),
            pltpu.VMEM((8, v, v), f32),
            pltpu.VMEM((16, v), f32),
            pltpu.VMEM((16, v), i32),
            pltpu.SMEM((16, v), f32),
            pltpu.SMEM((16, v), i32),
            pltpu.SMEM((136,), i32),
            pltpu.SemaphoreType.DMA((2,)),
        ],
        compiler_params=pltpu.CompilerParams(vmem_limit_bytes=8 * 1024 * 1024),
        cost_estimate=pl.CostEstimate(flops=0, bytes_accessed=12_000_000, transcendentals=0),
        name="couple",
    )(where, x_near, x_own, x_far, z_full, *z_mine, *z_other)

    near_back = lax.ppermute(near, ("x", "c"), opposite(NX, NX - 1))
    far_back = lax.ppermute(far, "x", ring(NX, 2))
    kept, gone = pl.pallas_call(
        settle_kernel,
        out_shape=(jax.ShapeDtypeStruct((2, v, v), f32),) * 2,
        in_specs=[smem] + [vmem] * 4,
        out_specs=(vmem, vmem),
        compiler_params=pltpu.CompilerParams(vmem_limit_bytes=4 * 1024 * 1024),
        name="settle",
    )(where, local, near_back, far_back, own)
    share = kept + lax.ppermute(gone, "c", swap)
    share = share + lax.ppermute(share, ("y", "c"), partners(0))
    share = share + lax.ppermute(share, ("y", "c"), partners(1))
    other = lax.ppermute(share, "c", swap)
    total = jnp.where(
        c == 0, jnp.concatenate([share, other], axis=0), jnp.concatenate([other, share], axis=0)
    )
    diagonal = (energies[:, :, None] + energies[:, None, :] - pair_shift[:, None, None]) * amp_float
    inside = jnp.arange(v, dtype=i32)[None, :] < pno_count[:, None]
    return jnp.where(inside[:, :, None] & inside[:, None, :], total + diagonal, f32(0.0))


def solution(mesh):
    owners = mesh.devices.shape[0]
    fine = Mesh(mesh.devices.reshape(owners // NX, NX, NY, NC), ("z", "x", "y", "c"))
    pair, aux = ("z", "x"), ("y", "c")
    placed = (
        P(pair, None, None),
        P(pair, None, None),
        P(pair, None),
        P(pair),
        P(pair),
        P(pair, None),
        P(pair, None),
        P(pair, aux, None),
        P(pair, aux, None),
    )
    return jax.shard_map(
        shards, mesh=fine, in_specs=placed, out_specs=P(pair, None, None), check_vma=False
    )
```

time: 61 us -> 53.9 us (0.88)
  local copies, waits for them, and re-layouts: 3.49 us -> 0.04 us
  Pallas kernels: 8.57 us -> 6.14 us
  waiting for transfers between devices: 14 us -> 11.9 us
  matrix products: 3.81 us -> 4.76 us
    ppermute x1, starting transfers between devices: 6.48 us -> 0.73 us  [shards(): z_one = lax.ppermute(z_full, ('z', 'c'), opposite(nz, 1))]
    ppermute x1, starting transfers between devices: 1.17 us -> 6.93 us  [shards(): z_two = lax.ppermute(z_full, ('z', 'c'), opposite(nz, 2))]
    unnamed x18 -> x12, local copies, waits for them, and re-layouts: 3.49 us -> 0.03 us
    ppermute x1 -> x2, waiting for transfers between devices: 3.03 us -> 0.01 us  [the longest x1 0.01 us: shards(): z_four = lax.ppermute(z_four, ('z', 'c'), opposite(nz, 2))]
    pallas_call x1, Pallas kernels: 5.32 us -> 3.22 us  [shards(): pl.pallas_call(couple_kernel, out_shape=(jax.ShapeDtypeStruct((4, v, v),...]
    ppermute x1, starting transfers between devices: 2.48 us -> 0.86 us  [shards(): x_near = lax.ppermute(x_all, ('x', 'c'), opposite(NX, 1))]
    ppermute x1, starting transfers between devices: 2.28 us -> 3.88 us  [shards(): share = share + lax.ppermute(share, ('y', 'c'), partners(0))]
    ppermute x3 -> x4, waiting for transfers between devices: 0.01 us -> 1.19 us  [shards(): z_other = [lax.ppermute(b, 'c', swap) for b in z_mine]]
  transfers between devices with their start and end apart: 14 -> 16, of which waited for: 7 -> 6; matrix products, arithmetic and copies ran while one was open for 6% -> 9% of each run, Pallas kernels for 1% -> 0%
where the time goes in v3:
time: 53.9 us; the launch traced here: 54.3 us
  starting transfers between devices  30.2 us (56%)
  waiting for transfers between devices  11.9 us (22%)
  Pallas kernels  6.14 us (11%)
  matrix products  4.76 us (9%)
  other arithmetic  1.11 us (2%)
    ppermute x1, starting transfers between devices, shards(): z_two = lax.ppermute(z_full, ('z', 'c'), opposite(nz, 2))  6.93 us
    ppermute x1, starting transfers between devices, shards(): z_four = lax.ppermute(z_four, ('z', 'c'), opposite(nz, 2))  4.25 us
    dot_general x1, matrix products, shards(): jnp.einsum('pqa,pqb->pab', slab_one, slab_two, preferred_element_type=f32)  3.91 us
    ppermute x1, starting transfers between devices, shards(): share = share + lax.ppermute(share, ('y', 'c'), partners(0))  3.88 us
    ppermute x1, waiting for transfers between devices, shards(): share = share + lax.ppermute(share, ('y', 'c'), partners(1))  3.8 us
    pallas_call x1, Pallas kernels, shards(): pl.pallas_call(couple_kernel, out_shape=(jax.ShapeDtypeStruct((4, v, v),...  3.22 us
    ppermute x1, starting transfers between devices, shards(): x_far = lax.ppermute(x_own, 'x', ring(NX, 2))  2.74 us
    ppermute x1, waiting for transfers between devices, shards(): far_back = lax.ppermute(far, 'x', ring(NX, 2))  2.63 us
  transfers between devices with their start and end apart: 16, of which 6 were waited for; matrix products, arithmetic and copies ran while one was open for 9% of the time, Pallas kernels for 0%

profile of v3, /device:TPU:1, one launch (start us, length us, event | category | flops | bytes accessed | tf_op | source)
XLA Modules:
  0.0 54.3 jit_solution(8106619220486739919)
XLA Ops:
  0.0 2.3 %prepare.1 = (bf16[640,128]{1,0:T(8,128)(2,1)}, bf16[2064,128]{1,0:T(8,128)(2,1)}, bf16[1040,128]{1,0:T(8,128)(2,1)}) custom-call(s32[4,16]{1,0:T(4,128)} %pairs.1, f32[4,16]{1,0:T(4,128)} %weights.1, bf16[4,512,128]{2,1,0:T(8,128)(2,1)} %coef.1, bf16[4,128,128]{2,1,0:T(8,128)(2,1)} %amp.1), custom_call_target="tpu_custom_call" | custom-call | tf_op jit(solution)/shard_map/prepare/pallas_call | solution.py:191
  2.3 6.9 %collective-permute-start.3 = (bf16[640,128]{1,0:T(8,128)(2,1)}, bf16[640,128]{1,0:T(8,128)(2,1)S(1)}, u32[]{:S(2)}, u32[]{:S(2)}) collective-permute-start(bf16[640,128]{1,0:T(8,128)(2,1)} %get-tuple-element.15.z_full), channel_id=1, source_target_pairs={{0,64},{32,96},{64,128},{96,160},{128,192},{160,224},{192,0},{224,... | collective-permute-start | bytes 491528 | tf_op jit(solution)/shard_map/ppermute | solution.py:211
  9.3 0.7 %collective-permute-start.2 = (bf16[640,128]{1,0:T(8,128)(2,1)}, bf16[640,128]{1,0:T(8,128)(2,1)S(1)}, u32[]{:S(2)}, u32[]{:S(2)}) collective-permute-start(bf16[640,128]{1,0:T(8,128)(2,1)} %get-tuple-element.15.z_full), channel_id=1, source_target_pairs={{0,32},{32,64},{64,96},{96,128},{128,160},{160,192},{192,224},{224... | collective-permute-start | bytes 491528 | tf_op jit(solution)/shard_map/ppermute | solution.py:210
  10.0 2.7 %collective-permute-start.1 = (bf16[1040,128]{1,0:T(8,128)(2,1)}, bf16[1040,128]{1,0:T(8,128)(2,1)S(1)}, u32[]{:S(2)}, u32[]{:S(2)}) collective-permute-start(bf16[1040,128]{1,0:T(8,128)(2,1)} %get-tuple-element.14.x_own), channel_id=1, source_target_pairs={{0,16},{8,24},{16,0},{24,8},{1,17},{9,25},{17,1},{25,9},{2,18},{10... | collective-permute-start | bytes 798728 | tf_op jit(solution)/shard_map/ppermute | solution.py:213
  12.7 0.9 %collective-permute-start = (bf16[2064,128]{1,0:T(8,128)(2,1)}, bf16[2064,128]{1,0:T(8,128)(2,1)S(1)}, u32[]{:S(2)}, u32[]{:S(2)}) collective-permute-start(bf16[2064,128]{1,0:T(8,128)(2,1)} %get-tuple-element.13), channel_id=1, source_target_pairs={{0,8},{8,16},{16,24},{24,0},{1,25},{9,1},{17,9},{25,17},{2,10},{10... | collective-permute-start | bytes 1585160 | tf_op jit(solution)/shard_map/ppermute | solution.py:212
  13.6 0.0 collective-permute-done.3.refs_1_
  13.6 0.0 copy-start.2
  13.6 0.0 copy-start
  13.7 0.0 copy-start.1
  13.7 4.3 %collective-permute-start.5 = (bf16[320,128]{1,0:T(8,128)(2,1)S(1)}, bf16[320,128]{1,0:T(8,128)(2,1)S(1)}, u32[]{:S(2)}, u32[]{:S(2)}) collective-permute-start(bf16[320,128]{1,0:T(8,128)(2,1)S(1)} %constant_dynamic-slice_fusion), channel_id=1, source_target_pairs={{0,64},{32,96},{64,128},{96,160},{128,192},{160,224},{192,0},{224,... | collective-permute-start | bytes 245768 | tf_op jit(solution)/shard_map/ppermute | solution.py:223
  17.9 0.0 collective-permute-start.4
  17.9 3.9 %fusion.3 = f32[4,128,128]{2,1,0:T(8,128)S(1)} fusion(bf16[4,3072,128]{2,1,0:T(8,128)(2,1)} %param.16, bf16[4,3072,128]{2,1,0:T(8,128)(2,1)} %param.17), kind=kOutput, calls=%fused_computation.8 | convolution fusion | flops 402653184 | bytes 6553600 | tf_op jit(solution)/shard_map/pqa,pqb->pab/dot_general | solution.py:215
  21.8 0.0 copy-start.5
  21.9 0.0 copy-start.3
  21.9 0.0 copy-start.4
  21.9 0.0 collective-permute-done.2.refs_0_
  21.9 0.1 collective-permute-start.7
  22.0 0.0 collective-permute-done.5.refs_3_
  22.0 0.5 collective-permute-start.6
  22.5 0.0 collective-permute-done.4.refs_2_
  22.5 1.2 %collective-permute-start.8 = (bf16[640,128]{1,0:T(8,128)(2,1)S(1)}, bf16[640,128]{1,0:T(8,128)(2,1)S(1)}, u32[]{:S(2)}, u32[]{:S(2)}) collective-permute-start(bf16[640,128]{1,0:T(8,128)(2,1)S(1)} %collective-permute-done.4.refs_2_), channel_id=1, source_target_pairs={{0,1},{1,0},{2,3},{3,2},{4,5},{5,4},{6,7},{7,6},{8,9},{9,8},{10,11... | collective-permute-start | bytes 491528 | tf_op jit(solution)/shard_map/ppermute | solution.py:225
  23.7 0.0 copy-done.2
  23.7 0.4 fusion.4
  24.1 0.0 collective-permute-done.1.x_far
  24.2 0.1 collective-permute-start.9
  24.3 0.1 pad_add_fusion.where
  24.3 1.2 %collective-permute-done.9.refs_7_ = bf16[320,128]{1,0:T(8,128)(2,1)S(1)} collective-permute-done((bf16[320,128]{1,0:T(8,128)(2,1)S(1)}, bf16[320,128]{1,0:T(8,128)(2,1)S(1)}, u32[]{:S(2)}, u32[]{:S(2)}) %collective-permute-start.9) | collective-permute-done | bytes 81952 | tf_op jit(solution)/shard_map/ppermute | solution.py:225
  25.5 0.0 collective-permute-done.7.refs_5_
  25.5 0.0 collective-permute-done.6.refs_4_
  25.5 0.0 collective-permute-done.8.refs_6_
  25.5 0.0 collective-permute-done.x_near
  25.5 0.0 copy-done
  25.6 0.0 copy-done.1
  25.6 3.2 %couple.1 = (bf16[4,128,128]{2,1,0:T(8,128)(2,1)S(1)}, bf16[2,128,128]{2,1,0:T(8,128)(2,1)S(1)}, f32[2,128,128]{2,1,0:T(8,128)S(1)}) custom-call(s32[4]{0:T(128)S(1)} %pad_add_fusion.where, bf16[2064,128]{1,0:T(8,128)(2,1)S(1)} %collective-permute-done.x_near, bf16[1040,128]{1,0:T(8,128)(2,1)S(1)} %copy-done, ...), custom_call_target="tpu_custom_call" | custom-call | bytes 12000000 | tf_op jit(solution)/shard_map/couple/pallas_call | solution.py:227
  28.8 1.8 %collective-permute-start.10 = (bf16[4,128,128]{2,1,0:T(8,128)(2,1)S(1)}, bf16[4,128,128]{2,1,0:T(8,128)(2,1)S(1)}, u32[]{:S(2)}, u32[]{:S(2)}) collective-permute-start(bf16[4,128,128]{2,1,0:T(8,128)(2,1)S(1)} %get-tuple-element.16), channel_id=1, source_target_pairs={{0,24},{8,0},{16,8},{24,16},{1,9},{9,17},{17,25},{25,1},{2,26},{10... | collective-permute-start | bytes 393224 | tf_op jit(solution)/shard_map/ppermute | solution.py:252
  30.6 1.9 %collective-permute-start.11 = (bf16[2,128,128]{2,1,0:T(8,128)(2,1)S(1)}, bf16[2,128,128]{2,1,0:T(8,128)(2,1)S(1)}, u32[]{:S(2)}, u32[]{:S(2)}) collective-permute-start(bf16[2,128,128]{2,1,0:T(8,128)(2,1)S(1)} %get-tuple-element.17), channel_id=1, source_target_pairs={{0,16},{8,24},{16,0},{24,8},{1,17},{9,25},{17,1},{25,9},{2,18},{10... | collective-permute-start | bytes 196616 | tf_op jit(solution)/shard_map/ppermute | solution.py:253
  32.5 0.4 fusion.local
  33.0 2.6 %collective-permute-done.11.far = bf16[2,128,128]{2,1,0:T(8,128)(2,1)S(1)} collective-permute-done((bf16[2,128,128]{2,1,0:T(8,128)(2,1)S(1)}, bf16[2,128,128]{2,1,0:T(8,128)(2,1)S(1)}, u32[]{:S(2)}, u32[]{:S(2)}) %collective-permute-start.11) | collective-permute-done | bytes 65568 | tf_op jit(solution)/shard_map/ppermute | solution.py:253
  35.6 0.0 collective-permute-done.10.near
  35.6 0.6 %settle.1 = (f32[2,128,128]{2,1,0:T(8,128)S(1)}, f32[2,128,128]{2,1,0:T(8,128)S(1)}) custom-call(s32[4]{0:T(128)S(1)} %pad_add_fusion.where, f32[4,128,128]{2,1,0:T(8,128)S(1)} %fusion.local, bf16[4,128,128]{2,1,0:T(8,128)(2,1)S(1)} %collective-permute-done.10.near, bf16[2,128,128]{2,1,0:T(8,128)(2,1)S(1)} %collective-permute-done.11.far, ...), custom_call_target="tpu_custom_call" | custom-call | tf_op jit(solution)/shard_map/settle/pallas_call | solution.py:254
  36.2 2.6 %collective-permute-start.12 = (f32[2,128,128]{2,1,0:T(8,128)S(1)}, f32[2,128,128]{2,1,0:T(8,128)S(1)}, u32[]{:S(2)}, u32[]{:S(2)}) collective-permute-start(f32[2,128,128]{2,1,0:T(8,128)S(1)} %get-tuple-element.20), channel_id=1, source_target_pairs={{0,1},{1,0},{2,3},{3,2},{4,5},{5,4},{6,7},{7,6},{8,9},{9,8},{10,11... | collective-permute-start | bytes 393224 | tf_op jit(solution)/shard_map/ppermute | solution.py:262
  38.8 1.0 %collective-permute-done.12 = f32[2,128,128]{2,1,0:T(8,128)S(1)} collective-permute-done((f32[2,128,128]{2,1,0:T(8,128)S(1)}, f32[2,128,128]{2,1,0:T(8,128)S(1)}, u32[]{:S(2)}, u32[]{:S(2)}) %collective-permute-start.12) | collective-permute-done | bytes 131104 | tf_op jit(solution)/shard_map/ppermute | solution.py:262
  39.8 3.9 %collective-permute-start.13 = (f32[2,128,128]{2,1,0:T(8,128)S(1)}, f32[2,128,128]{2,1,0:T(8,128)S(1)}, u32[]{:S(2)}, u32[]{:S(2)}) collective-permute-start(f32[2,128,128]{2,1,0:T(8,128)S(1)} %add.33), channel_id=1, source_target_pairs={{0,2},{1,7},{2,0},{3,5},{4,6},{5,3},{6,4},{7,1},{8,10},{9,15},{10,... | collective-permute-start | bytes 393224 | tf_op jit(solution)/shard_map/ppermute | solution.py:263
  43.6 2.4 %collective-permute-done.13 = f32[2,128,128]{2,1,0:T(8,128)S(1)} collective-permute-done((f32[2,128,128]{2,1,0:T(8,128)S(1)}, f32[2,128,128]{2,1,0:T(8,128)S(1)}, u32[]{:S(2)}, u32[]{:S(2)}) %collective-permute-start.13) | collective-permute-done | bytes 131104 | tf_op jit(solution)/shard_map/ppermute | solution.py:263
  46.0 0.1 collective-permute-start.14
  46.1 3.8 %collective-permute-done.14 = f32[2,128,128]{2,1,0:T(8,128)S(1)} collective-permute-done((f32[2,128,128]{2,1,0:T(8,128)S(1)}, f32[2,128,128]{2,1,0:T(8,128)S(1)}, u32[]{:S(2)}, u32[]{:S(2)}) %collective-permute-start.14) | collective-permute-done | bytes 131104 | tf_op jit(solution)/shard_map/ppermute | solution.py:264
  49.9 2.5 %collective-permute-start.15 = (f32[2,128,128]{2,1,0:T(8,128)S(1)}, f32[2,128,128]{2,1,0:T(8,128)S(1)}, u32[]{:S(2)}, u32[]{:S(2)}) collective-permute-start(f32[2,128,128]{2,1,0:T(8,128)S(1)} %add.35), channel_id=1, source_target_pairs={{0,1},{1,0},{2,3},{3,2},{4,5},{5,4},{6,7},{7,6},{8,9},{9,8},{10,11... | collective-permute-start | bytes 393224 | tf_op jit(solution)/shard_map/ppermute | solution.py:265
  52.4 0.0 copy-done.5
  52.4 0.1 iota_compare_fusion
  52.5 0.9 %collective-permute-done.15 = f32[2,128,128]{2,1,0:T(8,128)S(1)} collective-permute-done((f32[2,128,128]{2,1,0:T(8,128)S(1)}, f32[2,128,128]{2,1,0:T(8,128)S(1)}, u32[]{:S(2)}, u32[]{:S(2)}) %collective-permute-start.15) | collective-permute-done | bytes 131104 | tf_op jit(solution)/shard_map/ppermute | solution.py:265
  53.4 0.0 copy-done.3
  53.4 0.0 copy-done.4
  53.4 0.9 %fusion.2 = f32[4,128,128]{2,1,0:T(8,128)} fusion(f32[2,128,128]{2,1,0:T(8,128)S(1)} %collective-permute-done.15, f32[2,128,128]{2,1,0:T(8,128)S(1)} %add.35, bf16[4,128,128]{2,1,0:T(8,128)(2,1)S(1)} %copy-done.2, f32[4]{0:T(128)S(1)} %copy-done.4, f32[4,128]{1,0:T(4,128)S(1)} %copy-done.3, pred[]{:T(512)S(6)} %eq.3, pred[4,128]{1,0:T(4,128)(4,1)S(1)} %iota_compare_fusion), kind=kLoop, calls=%fused_computation.4 | loop fusion | flops 655360 | bytes 657937 | tf_op jit(solution)/shard_map/jit(_where)/select_n | solution.py:271
  (4 shorter events, 0.1 us)
Async XLA Ops:
  2.3 11.3 %collective-permute-start.3 = (bf16[640,128]{1,0:T(8,128)(2,1)}, bf16[640,128]{1,0:T(8,128)(2,1)S(1)}, u32[]{:S(2)}, u32[]{:S(2)}) collective-permute-start(bf16[640,128]{1,0:T(8,128)(2,1)} %get-tuple-element.15.z_full), channel_id=1, source_target_pairs={{0,64},{32,96},{64,128},{96,160},{128,192},{160,224},{192,0},{224,... | collective-permute-start | bytes 491528 | tf_op jit(solution)/shard_map/ppermute | solution.py:211
  9.3 12.6 %collective-permute-start.2 = (bf16[640,128]{1,0:T(8,128)(2,1)}, bf16[640,128]{1,0:T(8,128)(2,1)S(1)}, u32[]{:S(2)}, u32[]{:S(2)}) collective-permute-start(bf16[640,128]{1,0:T(8,128)(2,1)} %get-tuple-element.15.z_full), channel_id=1, source_target_pairs={{0,32},{32,64},{64,96},{96,128},{128,160},{160,192},{192,224},{224... | collective-permute-start | bytes 491528 | tf_op jit(solution)/shard_map/ppermute | solution.py:210
  10.0 14.2 %collective-permute-start.1 = (bf16[1040,128]{1,0:T(8,128)(2,1)}, bf16[1040,128]{1,0:T(8,128)(2,1)S(1)}, u32[]{:S(2)}, u32[]{:S(2)}) collective-permute-start(bf16[1040,128]{1,0:T(8,128)(2,1)} %get-tuple-element.14.x_own), channel_id=1, source_target_pairs={{0,16},{8,24},{16,0},{24,8},{1,17},{9,25},{17,1},{25,9},{2,18},{10... | collective-permute-start | bytes 798728 | tf_op jit(solution)/shard_map/ppermute | solution.py:213
  12.7 12.8 %collective-permute-start = (bf16[2064,128]{1,0:T(8,128)(2,1)}, bf16[2064,128]{1,0:T(8,128)(2,1)S(1)}, u32[]{:S(2)}, u32[]{:S(2)}) collective-permute-start(bf16[2064,128]{1,0:T(8,128)(2,1)} %get-tuple-element.13), channel_id=1, source_target_pairs={{0,8},{8,16},{16,24},{24,0},{1,25},{9,1},{17,9},{25,17},{2,10},{10... | collective-permute-start | bytes 1585160 | tf_op jit(solution)/shard_map/ppermute | solution.py:212
  13.6 10.1 %copy-start.2 = (bf16[4,128,128]{2,1,0:T(8,128)(2,1)S(1)}, bf16[4,128,128]{2,1,0:T(8,128)(2,1)}, u32[]{:S(2)}) copy-start(bf16[4,128,128]{2,1,0:T(8,128)(2,1)} %amp.1) | copy-start | bytes 393220
  13.6 11.9 %copy-start = (bf16[1040,128]{1,0:T(8,128)(2,1)S(1)}, bf16[1040,128]{1,0:T(8,128)(2,1)}, u32[]{:S(2)}) copy-start(bf16[1040,128]{1,0:T(8,128)(2,1)} %get-tuple-element.14.x_own) | copy-start | bytes 798724
  13.7 11.9 %copy-start.1 = (bf16[640,128]{1,0:T(8,128)(2,1)S(1)}, bf16[640,128]{1,0:T(8,128)(2,1)}, u32[]{:S(2)}) copy-start(bf16[640,128]{1,0:T(8,128)(2,1)} %get-tuple-element.15.z_full) | copy-start | bytes 491524
  13.7 8.3 %collective-permute-start.5 = (bf16[320,128]{1,0:T(8,128)(2,1)S(1)}, bf16[320,128]{1,0:T(8,128)(2,1)S(1)}, u32[]{:S(2)}, u32[]{:S(2)}) collective-permute-start(bf16[320,128]{1,0:T(8,128)(2,1)S(1)} %constant_dynamic-slice_fusion), channel_id=1, source_target_pairs={{0,64},{32,96},{64,128},{96,160},{128,192},{160,224},{192,0},{224,... | collective-permute-start | bytes 245768 | tf_op jit(solution)/shard_map/ppermute | solution.py:223
  17.9 4.6 %collective-permute-start.4 = (bf16[640,128]{1,0:T(8,128)(2,1)S(1)}, bf16[640,128]{1,0:T(8,128)(2,1)S(1)}, u32[]{:S(2)}, u32[]{:S(2)}) collective-permute-start(bf16[640,128]{1,0:T(8,128)(2,1)S(1)} %collective-permute-done.3.refs_1_), channel_id=1, source_target_pairs={{0,32},{32,64},{64,96},{96,128},{128,160},{160,192},{192,224},{224... | collective-permute-start | bytes 491528 | tf_op jit(solution)/shard_map/ppermute | solution.py:221
  21.8 30.6 %copy-start.5 = (s32[4]{0:T(128)S(1)}, s32[4]{0:T(128)}, u32[]{:S(2)}) copy-start(s32[4]{0:T(128)} %param.13) | copy-start | bytes 52
  21.9 31.5 %copy-start.3 = (f32[4,128]{1,0:T(4,128)S(1)}, f32[4,128]{1,0:T(4,128)}, u32[]{:S(2)}) copy-start(f32[4,128]{1,0:T(4,128)} %param.11) | copy-start | bytes 6148
  21.9 31.5 %copy-start.4 = (f32[4]{0:T(128)S(1)}, f32[4]{0:T(128)}, u32[]{:S(2)}) copy-start(f32[4]{0:T(128)} %param.12) | copy-start | bytes 52
  21.9 3.6 %collective-permute-start.7 = (bf16[640,128]{1,0:T(8,128)(2,1)S(1)}, bf16[640,128]{1,0:T(8,128)(2,1)S(1)}, u32[]{:S(2)}, u32[]{:S(2)}) collective-permute-start(bf16[640,128]{1,0:T(8,128)(2,1)S(1)} %collective-permute-done.3.refs_1_), channel_id=1, source_target_pairs={{0,1},{1,0},{2,3},{3,2},{4,5},{5,4},{6,7},{7,6},{8,9},{9,8},{10,11... | collective-permute-start | bytes 491528 | tf_op jit(solution)/shard_map/ppermute | solution.py:225
  22.0 3.5 %collective-permute-start.6 = (bf16[640,128]{1,0:T(8,128)(2,1)S(1)}, bf16[640,128]{1,0:T(8,128)(2,1)S(1)}, u32[]{:S(2)}, u32[]{:S(2)}) collective-permute-start(bf16[640,128]{1,0:T(8,128)(2,1)S(1)} %collective-permute-done.2.refs_0_), channel_id=1, source_target_pairs={{0,1},{1,0},{2,3},{3,2},{4,5},{5,4},{6,7},{7,6},{8,9},{9,8},{10,11... | collective-permute-start | bytes 491528 | tf_op jit(solution)/shard_map/ppermute | solution.py:225
  22.5 3.0 %collective-permute-start.8 = (bf16[640,128]{1,0:T(8,128)(2,1)S(1)}, bf16[640,128]{1,0:T(8,128)(2,1)S(1)}, u32[]{:S(2)}, u32[]{:S(2)}) collective-permute-start(bf16[640,128]{1,0:T(8,128)(2,1)S(1)} %collective-permute-done.4.refs_2_), channel_id=1, source_target_pairs={{0,1},{1,0},{2,3},{3,2},{4,5},{5,4},{6,7},{7,6},{8,9},{9,8},{10,11... | collective-permute-start | bytes 491528 | tf_op jit(solution)/shard_map/ppermute | solution.py:225
  24.2 1.4 %collective-permute-start.9 = (bf16[320,128]{1,0:T(8,128)(2,1)S(1)}, bf16[320,128]{1,0:T(8,128)(2,1)S(1)}, u32[]{:S(2)}, u32[]{:S(2)}) collective-permute-start(bf16[320,128]{1,0:T(8,128)(2,1)S(1)} %collective-permute-done.5.refs_3_), channel_id=1, source_target_pairs={{0,1},{1,0},{2,3},{3,2},{4,5},{5,4},{6,7},{7,6},{8,9},{9,8},{10,11... | collective-permute-start | bytes 245768 | tf_op jit(solution)/shard_map/ppermute | solution.py:225
  28.8 6.8 %collective-permute-start.10 = (bf16[4,128,128]{2,1,0:T(8,128)(2,1)S(1)}, bf16[4,128,128]{2,1,0:T(8,128)(2,1)S(1)}, u32[]{:S(2)}, u32[]{:S(2)}) collective-permute-start(bf16[4,128,128]{2,1,0:T(8,128)(2,1)S(1)} %get-tuple-element.16), channel_id=1, source_target_pairs={{0,24},{8,0},{16,8},{24,16},{1,9},{9,17},{17,25},{25,1},{2,26},{10... | collective-permute-start | bytes 393224 | tf_op jit(solution)/shard_map/ppermute | solution.py:252
  30.6 5.0 %collective-permute-start.11 = (bf16[2,128,128]{2,1,0:T(8,128)(2,1)S(1)}, bf16[2,128,128]{2,1,0:T(8,128)(2,1)S(1)}, u32[]{:S(2)}, u32[]{:S(2)}) collective-permute-start(bf16[2,128,128]{2,1,0:T(8,128)(2,1)S(1)} %get-tuple-element.17), channel_id=1, source_target_pairs={{0,16},{8,24},{16,0},{24,8},{1,17},{9,25},{17,1},{25,9},{2,18},{10... | collective-permute-start | bytes 196616 | tf_op jit(solution)/shard_map/ppermute | solution.py:253
  36.2 3.6 %collective-permute-start.12 = (f32[2,128,128]{2,1,0:T(8,128)S(1)}, f32[2,128,128]{2,1,0:T(8,128)S(1)}, u32[]{:S(2)}, u32[]{:S(2)}) collective-permute-start(f32[2,128,128]{2,1,0:T(8,128)S(1)} %get-tuple-element.20), channel_id=1, source_target_pairs={{0,1},{1,0},{2,3},{3,2},{4,5},{5,4},{6,7},{7,6},{8,9},{9,8},{10,11... | collective-permute-start | bytes 393224 | tf_op jit(solution)/shard_map/ppermute | solution.py:262
  39.8 6.2 %collective-permute-start.13 = (f32[2,128,128]{2,1,0:T(8,128)S(1)}, f32[2,128,128]{2,1,0:T(8,128)S(1)}, u32[]{:S(2)}, u32[]{:S(2)}) collective-permute-start(f32[2,128,128]{2,1,0:T(8,128)S(1)} %add.33), channel_id=1, source_target_pairs={{0,2},{1,7},{2,0},{3,5},{4,6},{5,3},{6,4},{7,1},{8,10},{9,15},{10,... | collective-permute-start | bytes 393224 | tf_op jit(solution)/shard_map/ppermute | solution.py:263
  46.0 3.9 %collective-permute-start.14 = (f32[2,128,128]{2,1,0:T(8,128)S(1)}, f32[2,128,128]{2,1,0:T(8,128)S(1)}, u32[]{:S(2)}, u32[]{:S(2)}) collective-permute-start(f32[2,128,128]{2,1,0:T(8,128)S(1)} %add.34), channel_id=1, source_target_pairs={{0,6},{1,3},{2,4},{3,1},{4,2},{5,7},{6,0},{7,5},{8,14},{9,11},{10,... | collective-permute-start | bytes 393224 | tf_op jit(solution)/shard_map/ppermute | solution.py:264
  49.9 3.5 %collective-permute-start.15 = (f32[2,128,128]{2,1,0:T(8,128)S(1)}, f32[2,128,128]{2,1,0:T(8,128)S(1)}, u32[]{:S(2)}, u32[]{:S(2)}) collective-permute-start(f32[2,128,128]{2,1,0:T(8,128)S(1)} %add.35), channel_id=1, source_target_pairs={{0,1},{1,0},{2,3},{3,2},{4,5},{5,4},{6,7},{7,6},{8,9},{9,8},{10,11... | collective-permute-start | bytes 393224 | tf_op jit(solution)/shard_map/ppermute | solution.py:265

commit v4 on v3

--- a/solution.py
+++ b/solution.py
@@ -212,6 +212,7 @@
     x_near = lax.ppermute(x_all, ("x", "c"), opposite(NX, 1))
     x_far = lax.ppermute(x_own, "x", ring(NX, 2))
 
+    slab_one, slab_two, _ = lax.optimization_barrier((slab_one, slab_two, z_two))
     exchange = jnp.einsum("pqa,pqb->pab", slab_one, slab_two, preferred_element_type=f32)
     amp_float = amplitudes.astype(f32)
     right = jnp.einsum("pab,pbc->pac", exchange, amp_float, precision=lax.Precision.HIGHEST)

time: 53.9 us -> 52.8 us (0.980); the launches traced: 54.3 us -> 52.4 us
  waiting for transfers between devices: 11.9 us -> 11.2 us
  starting transfers between devices: 30.2 us -> 29.5 us
    ppermute x1, starting transfers between devices: 3.88 us -> 2.83 us  [shards(): share = share + lax.ppermute(share, ('y', 'c'), partners(0))]
    ppermute x1, starting transfers between devices: 0.09 us -> 0.77 us  [shards(): share = share + lax.ppermute(share, ('y', 'c'), partners(1))]
    ppermute x1, waiting for transfers between devices: 3.8 us -> 3.14 us  [shards(): share = share + lax.ppermute(share, ('y', 'c'), partners(1))]
    ppermute x1, starting transfers between devices: 2.58 us -> 1.96 us  [shards(): share = kept + lax.ppermute(gone, 'c', swap)]
    ppermute x1, waiting for transfers between devices: 0.01 us -> 0.61 us  [shards(): x_near = lax.ppermute(x_all, ('x', 'c'), opposite(NX, 1))]
    ppermute x4, waiting for transfers between devices: 1.19 us -> 0.58 us  [shards(): z_other = [lax.ppermute(b, 'c', swap) for b in z_mine]]
  transfers between devices with their start and end apart: 16 -> 16, of which waited for: 6 -> 7; matrix products, arithmetic and copies ran while one was open for 9% -> 9% of each run, Pallas kernels for 0% -> 0%
where the time goes in v4:
time: 52.8 us; the launch traced here: 52.4 us
  starting transfers between devices  29.5 us (56%)
  waiting for transfers between devices  11.2 us (21%)
  Pallas kernels  5.61 us (11%)
  matrix products  4.76 us (9%)
  other arithmetic  1.11 us (2%)
    ppermute x1, starting transfers between devices, shards(): z_two = lax.ppermute(z_full, ('z', 'c'), opposite(nz, 2))  6.93 us
    ppermute x1, starting transfers between devices, shards(): z_four = lax.ppermute(z_four, ('z', 'c'), opposite(nz, 2))  4.19 us
    dot_general x1, matrix products, shards(): jnp.einsum('pqa,pqb->pab', slab_one, slab_two, preferred_element_type=f32)  3.91 us
    ppermute x1, waiting for transfers between devices, shards(): share = share + lax.ppermute(share, ('y', 'c'), partners(1))  3.14 us
    ppermute x1, starting transfers between devices, shards(): share = share + lax.ppermute(share, ('y', 'c'), partners(0))  2.83 us
    ppermute x1, starting transfers between devices, shards(): x_far = lax.ppermute(x_own, 'x', ring(NX, 2))  2.74 us
    pallas_call x1, Pallas kernels, shards(): pl.pallas_call(couple_kernel, out_shape=(jax.ShapeDtypeStruct((4, v, v),...  2.69 us
    ppermute x1, starting transfers between devices, shards(): other = lax.ppermute(share, 'c', swap)  2.68 us
  transfers between devices with their start and end apart: 16, of which 7 were waited for; matrix products, arithmetic and copies ran while one was open for 9% of the time, Pallas kernels for 0%

profile of v4, /device:TPU:1, one launch (start us, length us, event | category | flops | bytes accessed | tf_op | source)
XLA Modules:
  0.0 52.4 jit_solution(9196648977398201168)
XLA Ops:
  0.0 2.3 %prepare.1 = (bf16[640,128]{1,0:T(8,128)(2,1)}, bf16[2064,128]{1,0:T(8,128)(2,1)}, bf16[1040,128]{1,0:T(8,128)(2,1)}) custom-call(s32[4,16]{1,0:T(4,128)} %pairs.1, f32[4,16]{1,0:T(4,128)} %weights.1, bf16[4,512,128]{2,1,0:T(8,128)(2,1)} %coef.1, bf16[4,128,128]{2,1,0:T(8,128)(2,1)} %amp.1), custom_call_target="tpu_custom_call" | custom-call | tf_op jit(solution)/shard_map/prepare/pallas_call | solution.py:191
  2.3 6.9 %collective-permute-start = (bf16[640,128]{1,0:T(8,128)(2,1)}, bf16[640,128]{1,0:T(8,128)(2,1)S(1)}, u32[]{:S(2)}, u32[]{:S(2)}) collective-permute-start(bf16[640,128]{1,0:T(8,128)(2,1)} %get-tuple-element.15.z_full), channel_id=1, source_target_pairs={{0,64},{32,96},{64,128},{96,160},{128,192},{160,224},{192,0},{224,... | collective-permute-start | bytes 491528 | tf_op jit(solution)/shard_map/ppermute | solution.py:211
  9.3 0.7 %collective-permute-start.3 = (bf16[640,128]{1,0:T(8,128)(2,1)}, bf16[640,128]{1,0:T(8,128)(2,1)S(1)}, u32[]{:S(2)}, u32[]{:S(2)}) collective-permute-start(bf16[640,128]{1,0:T(8,128)(2,1)} %get-tuple-element.15.z_full), channel_id=1, source_target_pairs={{0,32},{32,64},{64,96},{96,128},{128,160},{160,192},{192,224},{224... | collective-permute-start | bytes 491528 | tf_op jit(solution)/shard_map/ppermute | solution.py:210
  10.0 2.7 %collective-permute-start.2 = (bf16[1040,128]{1,0:T(8,128)(2,1)}, bf16[1040,128]{1,0:T(8,128)(2,1)S(1)}, u32[]{:S(2)}, u32[]{:S(2)}) collective-permute-start(bf16[1040,128]{1,0:T(8,128)(2,1)} %get-tuple-element.19.x_own), channel_id=1, source_target_pairs={{0,16},{8,24},{16,0},{24,8},{1,17},{9,25},{17,1},{25,9},{2,18},{10... | collective-permute-start | bytes 798728 | tf_op jit(solution)/shard_map/ppermute | solution.py:213
  12.7 0.9 %collective-permute-start.1 = (bf16[2064,128]{1,0:T(8,128)(2,1)}, bf16[2064,128]{1,0:T(8,128)(2,1)S(1)}, u32[]{:S(2)}, u32[]{:S(2)}) collective-permute-start(bf16[2064,128]{1,0:T(8,128)(2,1)} %get-tuple-element.18), channel_id=1, source_target_pairs={{0,8},{8,16},{16,24},{24,0},{1,25},{9,1},{17,9},{25,17},{2,10},{10... | collective-permute-start | bytes 1585160 | tf_op jit(solution)/shard_map/ppermute | solution.py:212
  13.6 0.1 pad_add_fusion.where
  13.7 0.0 collective-permute-done.refs_1_
  13.7 0.0 copy-start.2
  13.7 0.0 copy-start
  13.7 0.0 copy-start.1
  13.7 4.2 %collective-permute-start.5 = (bf16[320,128]{1,0:T(8,128)(2,1)S(1)}, bf16[320,128]{1,0:T(8,128)(2,1)S(1)}, u32[]{:S(2)}, u32[]{:S(2)}) collective-permute-start(bf16[320,128]{1,0:T(8,128)(2,1)S(1)} %constant_dynamic-slice_fusion), channel_id=1, source_target_pairs={{0,64},{32,96},{64,128},{96,160},{128,192},{160,224},{192,0},{224,... | collective-permute-start | bytes 245768 | tf_op jit(solution)/shard_map/ppermute | solution.py:224
  17.9 0.0 collective-permute-start.4
  17.9 3.9 %fusion.3 = f32[4,128,128]{2,1,0:T(8,128)S(1)} fusion(bf16[4,3072,128]{2,1,0:T(8,128)(2,1)} %param.16, bf16[4,3072,128]{2,1,0:T(8,128)(2,1)} %param.17), kind=kOutput, calls=%fused_computation.8 | convolution fusion | flops 402653184 | bytes 6553600 | tf_op jit(solution)/shard_map/pqa,pqb->pab/dot_general | solution.py:216
  21.8 0.0 copy-start.5
  21.9 0.0 copy-start.3
  21.9 0.0 copy-start.4
  21.9 0.0 collective-permute-done.3.refs_0_
  21.9 0.1 collective-permute-start.7
  22.0 0.0 collective-permute-done.5.refs_3_
  22.0 0.5 collective-permute-start.6
  22.5 0.0 collective-permute-done.2.x_far
  22.5 0.1 collective-permute-start.9
  22.6 0.0 collective-permute-done.4.refs_2_
  22.6 1.1 %collective-permute-start.8 = (bf16[640,128]{1,0:T(8,128)(2,1)S(1)}, bf16[640,128]{1,0:T(8,128)(2,1)S(1)}, u32[]{:S(2)}, u32[]{:S(2)}) collective-permute-start(bf16[640,128]{1,0:T(8,128)(2,1)S(1)} %collective-permute-done.4.refs_2_), channel_id=1, source_target_pairs={{0,1},{1,0},{2,3},{3,2},{4,5},{5,4},{6,7},{7,6},{8,9},{9,8},{10,11... | collective-permute-start | bytes 491528 | tf_op jit(solution)/shard_map/ppermute | solution.py:226
  23.7 0.0 copy-done.2
  23.7 0.4 fusion.4
  24.1 0.0 collective-permute-done.9.refs_7_
  24.1 0.0 collective-permute-done.7.refs_5_
  24.2 0.0 collective-permute-done.6.refs_4_
  24.2 0.6 %collective-permute-done.8.refs_6_ = bf16[640,128]{1,0:T(8,128)(2,1)S(1)} collective-permute-done((bf16[640,128]{1,0:T(8,128)(2,1)S(1)}, bf16[640,128]{1,0:T(8,128)(2,1)S(1)}, u32[]{:S(2)}, u32[]{:S(2)}) %collective-permute-start.8) | collective-permute-done | bytes 163872 | tf_op jit(solution)/shard_map/ppermute | solution.py:226
  24.7 0.6 %collective-permute-done.1.x_near = bf16[2064,128]{1,0:T(8,128)(2,1)S(1)} collective-permute-done((bf16[2064,128]{1,0:T(8,128)(2,1)}, bf16[2064,128]{1,0:T(8,128)(2,1)S(1)}, u32[]{:S(2)}, u32[]{:S(2)}) %collective-permute-start.1) | collective-permute-done | bytes 528416 | tf_op jit(solution)/shard_map/ppermute | solution.py:212
  25.4 0.0 copy-done
  25.4 0.0 copy-done.1
  25.4 2.7 %couple.1 = (bf16[4,128,128]{2,1,0:T(8,128)(2,1)S(1)}, bf16[2,128,128]{2,1,0:T(8,128)(2,1)S(1)}, f32[2,128,128]{2,1,0:T(8,128)S(1)}) custom-call(s32[4]{0:T(128)S(1)} %pad_add_fusion.where, bf16[2064,128]{1,0:T(8,128)(2,1)S(1)} %collective-permute-done.1.x_near, bf16[1040,128]{1,0:T(8,128)(2,1)S(1)} %copy-done, ...), custom_call_target="tpu_custom_call" | custom-call | bytes 12000000 | tf_op jit(solution)/shard_map/couple/pallas_call | solution.py:228
  28.1 1.8 %collective-permute-start.10 = (bf16[4,128,128]{2,1,0:T(8,128)(2,1)S(1)}, bf16[4,128,128]{2,1,0:T(8,128)(2,1)S(1)}, u32[]{:S(2)}, u32[]{:S(2)}) collective-permute-start(bf16[4,128,128]{2,1,0:T(8,128)(2,1)S(1)} %get-tuple-element.20), channel_id=1, source_target_pairs={{0,24},{8,0},{16,8},{24,16},{1,9},{9,17},{17,25},{25,1},{2,26},{10... | collective-permute-start | bytes 393224 | tf_op jit(solution)/shard_map/ppermute | solution.py:253
  29.9 2.2 %collective-permute-start.11 = (bf16[2,128,128]{2,1,0:T(8,128)(2,1)S(1)}, bf16[2,128,128]{2,1,0:T(8,128)(2,1)S(1)}, u32[]{:S(2)}, u32[]{:S(2)}) collective-permute-start(bf16[2,128,128]{2,1,0:T(8,128)(2,1)S(1)} %get-tuple-element.21), channel_id=1, source_target_pairs={{0,16},{8,24},{16,0},{24,8},{1,17},{9,25},{17,1},{25,9},{2,18},{10... | collective-permute-start | bytes 196616 | tf_op jit(solution)/shard_map/ppermute | solution.py:254
  32.0 0.4 fusion.local
  32.5 2.6 %collective-permute-done.11.far = bf16[2,128,128]{2,1,0:T(8,128)(2,1)S(1)} collective-permute-done((bf16[2,128,128]{2,1,0:T(8,128)(2,1)S(1)}, bf16[2,128,128]{2,1,0:T(8,128)(2,1)S(1)}, u32[]{:S(2)}, u32[]{:S(2)}) %collective-permute-start.11) | collective-permute-done | bytes 65568 | tf_op jit(solution)/shard_map/ppermute | solution.py:254
  35.1 0.0 collective-permute-done.10.near
  35.1 0.6 %settle.1 = (f32[2,128,128]{2,1,0:T(8,128)S(1)}, f32[2,128,128]{2,1,0:T(8,128)S(1)}) custom-call(s32[4]{0:T(128)S(1)} %pad_add_fusion.where, f32[4,128,128]{2,1,0:T(8,128)S(1)} %fusion.local, bf16[4,128,128]{2,1,0:T(8,128)(2,1)S(1)} %collective-permute-done.10.near, bf16[2,128,128]{2,1,0:T(8,128)(2,1)S(1)} %collective-permute-done.11.far, ...), custom_call_target="tpu_custom_call" | custom-call | tf_op jit(solution)/shard_map/settle/pallas_call | solution.py:255
  35.7 2.0 %collective-permute-start.12 = (f32[2,128,128]{2,1,0:T(8,128)S(1)}, f32[2,128,128]{2,1,0:T(8,128)S(1)}, u32[]{:S(2)}, u32[]{:S(2)}) collective-permute-start(f32[2,128,128]{2,1,0:T(8,128)S(1)} %get-tuple-element.24), channel_id=1, source_target_pairs={{0,1},{1,0},{2,3},{3,2},{4,5},{5,4},{6,7},{7,6},{8,9},{9,8},{10,11... | collective-permute-start | bytes 393224 | tf_op jit(solution)/shard_map/ppermute | solution.py:263
  37.6 1.0 %collective-permute-done.12 = f32[2,128,128]{2,1,0:T(8,128)S(1)} collective-permute-done((f32[2,128,128]{2,1,0:T(8,128)S(1)}, f32[2,128,128]{2,1,0:T(8,128)S(1)}, u32[]{:S(2)}, u32[]{:S(2)}) %collective-permute-start.12) | collective-permute-done | bytes 131104 | tf_op jit(solution)/shard_map/ppermute | solution.py:263
  38.6 2.8 %collective-permute-start.13 = (f32[2,128,128]{2,1,0:T(8,128)S(1)}, f32[2,128,128]{2,1,0:T(8,128)S(1)}, u32[]{:S(2)}, u32[]{:S(2)}) collective-permute-start(f32[2,128,128]{2,1,0:T(8,128)S(1)} %add.33), channel_id=1, source_target_pairs={{0,2},{1,7},{2,0},{3,5},{4,6},{5,3},{6,4},{7,1},{8,10},{9,15},{10,... | collective-permute-start | bytes 393224 | tf_op jit(solution)/shard_map/ppermute | solution.py:264
  41.5 2.4 %collective-permute-done.13 = f32[2,128,128]{2,1,0:T(8,128)S(1)} collective-permute-done((f32[2,128,128]{2,1,0:T(8,128)S(1)}, f32[2,128,128]{2,1,0:T(8,128)S(1)}, u32[]{:S(2)}, u32[]{:S(2)}) %collective-permute-start.13) | collective-permute-done | bytes 131104 | tf_op jit(solution)/shard_map/ppermute | solution.py:264
  43.8 0.8 %collective-permute-start.14 = (f32[2,128,128]{2,1,0:T(8,128)S(1)}, f32[2,128,128]{2,1,0:T(8,128)S(1)}, u32[]{:S(2)}, u32[]{:S(2)}) collective-permute-start(f32[2,128,128]{2,1,0:T(8,128)S(1)} %add.34), channel_id=1, source_target_pairs={{0,6},{1,3},{2,4},{3,1},{4,2},{5,7},{6,0},{7,5},{8,14},{9,11},{10,... | collective-permute-start | bytes 393224 | tf_op jit(solution)/shard_map/ppermute | solution.py:265
  44.6 3.1 %collective-permute-done.14 = f32[2,128,128]{2,1,0:T(8,128)S(1)} collective-permute-done((f32[2,128,128]{2,1,0:T(8,128)S(1)}, f32[2,128,128]{2,1,0:T(8,128)S(1)}, u32[]{:S(2)}, u32[]{:S(2)}) %collective-permute-start.14) | collective-permute-done | bytes 131104 | tf_op jit(solution)/shard_map/ppermute | solution.py:265
  47.8 2.7 %collective-permute-start.15 = (f32[2,128,128]{2,1,0:T(8,128)S(1)}, f32[2,128,128]{2,1,0:T(8,128)S(1)}, u32[]{:S(2)}, u32[]{:S(2)}) collective-permute-start(f32[2,128,128]{2,1,0:T(8,128)S(1)} %add.35), channel_id=1, source_target_pairs={{0,1},{1,0},{2,3},{3,2},{4,5},{5,4},{6,7},{7,6},{8,9},{9,8},{10,11... | collective-permute-start | bytes 393224 | tf_op jit(solution)/shard_map/ppermute | solution.py:266
  50.4 0.0 copy-done.5
  50.5 0.1 iota_compare_fusion
  50.5 0.9 %collective-permute-done.15 = f32[2,128,128]{2,1,0:T(8,128)S(1)} collective-permute-done((f32[2,128,128]{2,1,0:T(8,128)S(1)}, f32[2,128,128]{2,1,0:T(8,128)S(1)}, u32[]{:S(2)}, u32[]{:S(2)}) %collective-permute-start.15) | collective-permute-done | bytes 131104 | tf_op jit(solution)/shard_map/ppermute | solution.py:266
  51.4 0.0 copy-done.3
  51.4 0.0 copy-done.4
  51.4 0.9 %fusion.2 = f32[4,128,128]{2,1,0:T(8,128)} fusion(f32[2,128,128]{2,1,0:T(8,128)S(1)} %collective-permute-done.15, f32[2,128,128]{2,1,0:T(8,128)S(1)} %add.35, bf16[4,128,128]{2,1,0:T(8,128)(2,1)S(1)} %copy-done.2, f32[4]{0:T(128)S(1)} %copy-done.4, f32[4,128]{1,0:T(4,128)S(1)} %copy-done.3, pred[]{:T(512)S(6)} %eq.3, pred[4,128]{1,0:T(4,128)(4,1)S(1)} %iota_compare_fusion), kind=kLoop, calls=%fused_computation.4 | loop fusion | flops 655360 | bytes 657937 | tf_op jit(solution)/shard_map/jit(_where)/select_n | solution.py:272
  (4 shorter events, 0.1 us)
Async XLA Ops:
  2.3 11.3 %collective-permute-start = (bf16[640,128]{1,0:T(8,128)(2,1)}, bf16[640,128]{1,0:T(8,128)(2,1)S(1)}, u32[]{:S(2)}, u32[]{:S(2)}) collective-permute-start(bf16[640,128]{1,0:T(8,128)(2,1)} %get-tuple-element.15.z_full), channel_id=1, source_target_pairs={{0,64},{32,96},{64,128},{96,160},{128,192},{160,224},{192,0},{224,... | collective-permute-start | bytes 491528 | tf_op jit(solution)/shard_map/ppermute | solution.py:211
  9.3 12.6 %collective-permute-start.3 = (bf16[640,128]{1,0:T(8,128)(2,1)}, bf16[640,128]{1,0:T(8,128)(2,1)S(1)}, u32[]{:S(2)}, u32[]{:S(2)}) collective-permute-start(bf16[640,128]{1,0:T(8,128)(2,1)} %get-tuple-element.15.z_full), channel_id=1, source_target_pairs={{0,32},{32,64},{64,96},{96,128},{128,160},{160,192},{192,224},{224... | collective-permute-start | bytes 491528 | tf_op jit(solution)/shard_map/ppermute | solution.py:210
  10.0 12.5 %collective-permute-start.2 = (bf16[1040,128]{1,0:T(8,128)(2,1)}, bf16[1040,128]{1,0:T(8,128)(2,1)S(1)}, u32[]{:S(2)}, u32[]{:S(2)}) collective-permute-start(bf16[1040,128]{1,0:T(8,128)(2,1)} %get-tuple-element.19.x_own), channel_id=1, source_target_pairs={{0,16},{8,24},{16,0},{24,8},{1,17},{9,25},{17,1},{25,9},{2,18},{10... | collective-permute-start | bytes 798728 | tf_op jit(solution)/shard_map/ppermute | solution.py:213
  12.7 12.6 %collective-permute-start.1 = (bf16[2064,128]{1,0:T(8,128)(2,1)}, bf16[2064,128]{1,0:T(8,128)(2,1)S(1)}, u32[]{:S(2)}, u32[]{:S(2)}) collective-permute-start(bf16[2064,128]{1,0:T(8,128)(2,1)} %get-tuple-element.18), channel_id=1, source_target_pairs={{0,8},{8,16},{16,24},{24,0},{1,25},{9,1},{17,9},{25,17},{2,10},{10... | collective-permute-start | bytes 1585160 | tf_op jit(solution)/shard_map/ppermute | solution.py:212
  13.7 10.0 %copy-start.2 = (bf16[4,128,128]{2,1,0:T(8,128)(2,1)S(1)}, bf16[4,128,128]{2,1,0:T(8,128)(2,1)}, u32[]{:S(2)}) copy-start(bf16[4,128,128]{2,1,0:T(8,128)(2,1)} %amp.1) | copy-start | bytes 393220
  13.7 11.7 %copy-start = (bf16[1040,128]{1,0:T(8,128)(2,1)S(1)}, bf16[1040,128]{1,0:T(8,128)(2,1)}, u32[]{:S(2)}) copy-start(bf16[1040,128]{1,0:T(8,128)(2,1)} %get-tuple-element.19.x_own) | copy-start | bytes 798724
  13.7 11.7 %copy-start.1 = (bf16[640,128]{1,0:T(8,128)(2,1)S(1)}, bf16[640,128]{1,0:T(8,128)(2,1)}, u32[]{:S(2)}) copy-start(bf16[640,128]{1,0:T(8,128)(2,1)} %get-tuple-element.15.z_full) | copy-start | bytes 491524
  13.7 8.3 %collective-permute-start.5 = (bf16[320,128]{1,0:T(8,128)(2,1)S(1)}, bf16[320,128]{1,0:T(8,128)(2,1)S(1)}, u32[]{:S(2)}, u32[]{:S(2)}) collective-permute-start(bf16[320,128]{1,0:T(8,128)(2,1)S(1)} %constant_dynamic-slice_fusion), channel_id=1, source_target_pairs={{0,64},{32,96},{64,128},{96,160},{128,192},{160,224},{192,0},{224,... | collective-permute-start | bytes 245768 | tf_op jit(solution)/shard_map/ppermute | solution.py:224
  17.9 4.7 %collective-permute-start.4 = (bf16[640,128]{1,0:T(8,128)(2,1)S(1)}, bf16[640,128]{1,0:T(8,128)(2,1)S(1)}, u32[]{:S(2)}, u32[]{:S(2)}) collective-permute-start(bf16[640,128]{1,0:T(8,128)(2,1)S(1)} %collective-permute-done.refs_1_), channel_id=1, source_target_pairs={{0,32},{32,64},{64,96},{96,128},{128,160},{160,192},{192,224},{224... | collective-permute-start | bytes 491528 | tf_op jit(solution)/shard_map/ppermute | solution.py:222
  21.8 28.6 %copy-start.5 = (s32[4]{0:T(128)S(1)}, s32[4]{0:T(128)}, u32[]{:S(2)}) copy-start(s32[4]{0:T(128)} %param.13) | copy-start | bytes 52
  21.9 29.6 %copy-start.3 = (f32[4,128]{1,0:T(4,128)S(1)}, f32[4,128]{1,0:T(4,128)}, u32[]{:S(2)}) copy-start(f32[4,128]{1,0:T(4,128)} %param.11) | copy-start | bytes 6148
  21.9 29.6 %copy-start.4 = (f32[4]{0:T(128)S(1)}, f32[4]{0:T(128)}, u32[]{:S(2)}) copy-start(f32[4]{0:T(128)} %param.12) | copy-start | bytes 52
  21.9 2.3 %collective-permute-start.7 = (bf16[640,128]{1,0:T(8,128)(2,1)S(1)}, bf16[640,128]{1,0:T(8,128)(2,1)S(1)}, u32[]{:S(2)}, u32[]{:S(2)}) collective-permute-start(bf16[640,128]{1,0:T(8,128)(2,1)S(1)} %collective-permute-done.refs_1_), channel_id=1, source_target_pairs={{0,1},{1,0},{2,3},{3,2},{4,5},{5,4},{6,7},{7,6},{8,9},{9,8},{10,11... | collective-permute-start | bytes 491528 | tf_op jit(solution)/shard_map/ppermute | solution.py:226
  22.0 2.2 %collective-permute-start.6 = (bf16[640,128]{1,0:T(8,128)(2,1)S(1)}, bf16[640,128]{1,0:T(8,128)(2,1)S(1)}, u32[]{:S(2)}, u32[]{:S(2)}) collective-permute-start(bf16[640,128]{1,0:T(8,128)(2,1)S(1)} %collective-permute-done.3.refs_0_), channel_id=1, source_target_pairs={{0,1},{1,0},{2,3},{3,2},{4,5},{5,4},{6,7},{7,6},{8,9},{9,8},{10,11... | collective-permute-start | bytes 491528 | tf_op jit(solution)/shard_map/ppermute | solution.py:226
  22.5 1.7 %collective-permute-start.9 = (bf16[320,128]{1,0:T(8,128)(2,1)S(1)}, bf16[320,128]{1,0:T(8,128)(2,1)S(1)}, u32[]{:S(2)}, u32[]{:S(2)}) collective-permute-start(bf16[320,128]{1,0:T(8,128)(2,1)S(1)} %collective-permute-done.5.refs_3_), channel_id=1, source_target_pairs={{0,1},{1,0},{2,3},{3,2},{4,5},{5,4},{6,7},{7,6},{8,9},{9,8},{10,11... | collective-permute-start | bytes 245768 | tf_op jit(solution)/shard_map/ppermute | solution.py:226
  22.6 2.1 %collective-permute-start.8 = (bf16[640,128]{1,0:T(8,128)(2,1)S(1)}, bf16[640,128]{1,0:T(8,128)(2,1)S(1)}, u32[]{:S(2)}, u32[]{:S(2)}) collective-permute-start(bf16[640,128]{1,0:T(8,128)(2,1)S(1)} %collective-permute-done.4.refs_2_), channel_id=1, source_target_pairs={{0,1},{1,0},{2,3},{3,2},{4,5},{5,4},{6,7},{7,6},{8,9},{9,8},{10,11... | collective-permute-start | bytes 491528 | tf_op jit(solution)/shard_map/ppermute | solution.py:226
  28.1 7.0 %collective-permute-start.10 = (bf16[4,128,128]{2,1,0:T(8,128)(2,1)S(1)}, bf16[4,128,128]{2,1,0:T(8,128)(2,1)S(1)}, u32[]{:S(2)}, u32[]{:S(2)}) collective-permute-start(bf16[4,128,128]{2,1,0:T(8,128)(2,1)S(1)} %get-tuple-element.20), channel_id=1, source_target_pairs={{0,24},{8,0},{16,8},{24,16},{1,9},{9,17},{17,25},{25,1},{2,26},{10... | collective-permute-start | bytes 393224 | tf_op jit(solution)/shard_map/ppermute | solution.py:253
  29.9 5.2 %collective-permute-start.11 = (bf16[2,128,128]{2,1,0:T(8,128)(2,1)S(1)}, bf16[2,128,128]{2,1,0:T(8,128)(2,1)S(1)}, u32[]{:S(2)}, u32[]{:S(2)}) collective-permute-start(bf16[2,128,128]{2,1,0:T(8,128)(2,1)S(1)} %get-tuple-element.21), channel_id=1, source_target_pairs={{0,16},{8,24},{16,0},{24,8},{1,17},{9,25},{17,1},{25,9},{2,18},{10... | collective-permute-start | bytes 196616 | tf_op jit(solution)/shard_map/ppermute | solution.py:254
  35.7 2.9 %collective-permute-start.12 = (f32[2,128,128]{2,1,0:T(8,128)S(1)}, f32[2,128,128]{2,1,0:T(8,128)S(1)}, u32[]{:S(2)}, u32[]{:S(2)}) collective-permute-start(f32[2,128,128]{2,1,0:T(8,128)S(1)} %get-tuple-element.24), channel_id=1, source_target_pairs={{0,1},{1,0},{2,3},{3,2},{4,5},{5,4},{6,7},{7,6},{8,9},{9,8},{10,11... | collective-permute-start | bytes 393224 | tf_op jit(solution)/shard_map/ppermute | solution.py:263
  38.6 5.2 %collective-permute-start.13 = (f32[2,128,128]{2,1,0:T(8,128)S(1)}, f32[2,128,128]{2,1,0:T(8,128)S(1)}, u32[]{:S(2)}, u32[]{:S(2)}) collective-permute-start(f32[2,128,128]{2,1,0:T(8,128)S(1)} %add.33), channel_id=1, source_target_pairs={{0,2},{1,7},{2,0},{3,5},{4,6},{5,3},{6,4},{7,1},{8,10},{9,15},{10,... | collective-permute-start | bytes 393224 | tf_op jit(solution)/shard_map/ppermute | solution.py:264
  43.8 3.9 %collective-permute-start.14 = (f32[2,128,128]{2,1,0:T(8,128)S(1)}, f32[2,128,128]{2,1,0:T(8,128)S(1)}, u32[]{:S(2)}, u32[]{:S(2)}) collective-permute-start(f32[2,128,128]{2,1,0:T(8,128)S(1)} %add.34), channel_id=1, source_target_pairs={{0,6},{1,3},{2,4},{3,1},{4,2},{5,7},{6,0},{7,5},{8,14},{9,11},{10,... | collective-permute-start | bytes 393224 | tf_op jit(solution)/shard_map/ppermute | solution.py:265
  47.8 3.7 %collective-permute-start.15 = (f32[2,128,128]{2,1,0:T(8,128)S(1)}, f32[2,128,128]{2,1,0:T(8,128)S(1)}, u32[]{:S(2)}, u32[]{:S(2)}) collective-permute-start(f32[2,128,128]{2,1,0:T(8,128)S(1)} %add.35), channel_id=1, source_target_pairs={{0,1},{1,0},{2,3},{3,2},{4,5},{5,4},{6,7},{7,6},{8,9},{9,8},{10,11... | collective-permute-start | bytes 393224 | tf_op jit(solution)/shard_map/ppermute | solution.py:266

commit v5 on v3

--- a/solution.py
+++ b/solution.py
@@ -40,15 +40,13 @@
 
     fetch(pairs, pairs_v)
     fetch(weights, weights_v)
-    at = 0
+    half, amp_half = nv // NC, v // NC
+    step = half + amp_half
     for part in range(NC):
-        for ref, size in ((coef, nv // NC), (amp, v // NC)):
-            fetch(ref.at[y, pl.ds(part * size, size)], z_full.at[pl.ds(at, size)])
-            at += size
+        src = amp.at[y, pl.ds(part * amp_half, amp_half)]
+        fetch(src, z_full.at[pl.ds(part * step + half, amp_half)])
     for s in range(4):
         fetch(coef.at[s], x_all.at[pl.ds(s * nv, nv)])
-    for s in range(2):
-        fetch(coef.at[2 * c + s], x_own.at[pl.ds(s * nv, nv)])
     copies[0].wait()
     copies[1].wait()
     weight = weights_v[...]
@@ -62,6 +60,10 @@
         ref[start : start + META, : meta.shape[1]] = meta
     for copy in copies[2:]:
         copy.wait()
+    for part in range(NC):
+        start = pl.multiple_of(y * nv + part * half, half)
+        z_full[part * step : part * step + half, :] = x_all[pl.ds(start, half), :]
+    x_own[: 2 * nv, :] = x_all[pl.ds(pl.multiple_of(2 * c * nv, nv), 2 * nv), :]
 
 
 def couple_kernel(where, x_near, x_own, x_far, z_full, *refs):

time: 53.9 us -> 53.1 us (0.985)
  starting transfers between devices: 30.2 us -> 29.4 us
where the time goes in v5:
time: 53.1 us
  starting transfers between devices  29.4 us (55%)
  waiting for transfers between devices  11.6 us (22%)
  Pallas kernels  6.02 us (11%)
  matrix products  4.76 us (9%)
  other arithmetic  1.11 us (2%)
    ppermute x1, starting transfers between devices, shards(): z_two = lax.ppermute(z_full, ('z', 'c'), opposite(nz, 2))  6.93 us
    ppermute x1, starting transfers between devices, shards(): z_four = lax.ppermute(z_four, ('z', 'c'), opposite(nz, 2))  4.25 us
    dot_general x1, matrix products, shards(): jnp.einsum('pqa,pqb->pab', slab_one, slab_two, preferred_element_type=f32)  3.91 us
    ppermute x1, waiting for transfers between devices, shards(): share = share + lax.ppermute(share, ('y', 'c'), partners(1))  3.51 us
    ppermute x1, starting transfers between devices, shards(): share = share + lax.ppermute(share, ('y', 'c'), partners(0))  3.35 us
    pallas_call x1, Pallas kernels, shards(): pl.pallas_call(couple_kernel, out_shape=(jax.ShapeDtypeStruct((4, v, v),...  3.22 us
    ppermute x1, starting transfers between devices, shards(): x_far = lax.ppermute(x_own, 'x', ring(NX, 2))  2.74 us
    ppermute x1, waiting for transfers between devices, shards(): far_back = lax.ppermute(far, 'x', ring(NX, 2))  2.63 us
  transfers between devices with their start and end apart: 16, of which 6 were waited for; matrix products, arithmetic and copies ran while one was open for 9% of the time, Pallas kernels for 0%

profile of v5, /device:TPU:1, one launch (start us, length us, event | category | flops | bytes accessed | tf_op | source)
XLA Modules:
  0.0 53.1 jit_solution(2736827599065961027)
XLA Ops:
  0.0 2.2 %prepare.1 = (bf16[640,128]{1,0:T(8,128)(2,1)}, bf16[2064,128]{1,0:T(8,128)(2,1)}, bf16[1040,128]{1,0:T(8,128)(2,1)}) custom-call(s32[4,16]{1,0:T(4,128)} %pairs.1, f32[4,16]{1,0:T(4,128)} %weights.1, bf16[4,512,128]{2,1,0:T(8,128)(2,1)} %coef.1, bf16[4,128,128]{2,1,0:T(8,128)(2,1)} %amp.1), custom_call_target="tpu_custom_call" | custom-call | tf_op jit(solution)/shard_map/prepare/pallas_call | solution.py:193
  2.2 6.9 %collective-permute-start.3 = (bf16[640,128]{1,0:T(8,128)(2,1)}, bf16[640,128]{1,0:T(8,128)(2,1)S(1)}, u32[]{:S(2)}, u32[]{:S(2)}) collective-permute-start(bf16[640,128]{1,0:T(8,128)(2,1)} %get-tuple-element.15.z_full), channel_id=1, source_target_pairs={{0,64},{32,96},{64,128},{96,160},{128,192},{160,224},{192,0},{224,... | collective-permute-start | bytes 491528 | tf_op jit(solution)/shard_map/ppermute | solution.py:213
  9.1 0.7 %collective-permute-start.2 = (bf16[640,128]{1,0:T(8,128)(2,1)}, bf16[640,128]{1,0:T(8,128)(2,1)S(1)}, u32[]{:S(2)}, u32[]{:S(2)}) collective-permute-start(bf16[640,128]{1,0:T(8,128)(2,1)} %get-tuple-element.15.z_full), channel_id=1, source_target_pairs={{0,32},{32,64},{64,96},{96,128},{128,160},{160,192},{192,224},{224... | collective-permute-start | bytes 491528 | tf_op jit(solution)/shard_map/ppermute | solution.py:212
  9.9 2.7 %collective-permute-start.1 = (bf16[1040,128]{1,0:T(8,128)(2,1)}, bf16[1040,128]{1,0:T(8,128)(2,1)S(1)}, u32[]{:S(2)}, u32[]{:S(2)}) collective-permute-start(bf16[1040,128]{1,0:T(8,128)(2,1)} %get-tuple-element.14.x_own), channel_id=1, source_target_pairs={{0,16},{8,24},{16,0},{24,8},{1,17},{9,25},{17,1},{25,9},{2,18},{10... | collective-permute-start | bytes 798728 | tf_op jit(solution)/shard_map/ppermute | solution.py:215
  12.6 0.9 %collective-permute-start = (bf16[2064,128]{1,0:T(8,128)(2,1)}, bf16[2064,128]{1,0:T(8,128)(2,1)S(1)}, u32[]{:S(2)}, u32[]{:S(2)}) collective-permute-start(bf16[2064,128]{1,0:T(8,128)(2,1)} %get-tuple-element.13), channel_id=1, source_target_pairs={{0,8},{8,16},{16,24},{24,0},{1,25},{9,1},{17,9},{25,17},{2,10},{10... | collective-permute-start | bytes 1585160 | tf_op jit(solution)/shard_map/ppermute | solution.py:214
  13.5 0.0 collective-permute-done.3.refs_1_
  13.5 0.0 copy-start.2
  13.5 0.0 copy-start
  13.5 0.0 copy-start.1
  13.5 4.3 %collective-permute-start.5 = (bf16[320,128]{1,0:T(8,128)(2,1)S(1)}, bf16[320,128]{1,0:T(8,128)(2,1)S(1)}, u32[]{:S(2)}, u32[]{:S(2)}) collective-permute-start(bf16[320,128]{1,0:T(8,128)(2,1)S(1)} %constant_dynamic-slice_fusion), channel_id=1, source_target_pairs={{0,64},{32,96},{64,128},{96,160},{128,192},{160,224},{192,0},{224,... | collective-permute-start | bytes 245768 | tf_op jit(solution)/shard_map/ppermute | solution.py:225
  17.8 0.0 collective-permute-start.4
  17.8 3.9 %fusion.3 = f32[4,128,128]{2,1,0:T(8,128)S(1)} fusion(bf16[4,3072,128]{2,1,0:T(8,128)(2,1)} %param.16, bf16[4,3072,128]{2,1,0:T(8,128)(2,1)} %param.17), kind=kOutput, calls=%fused_computation.8 | convolution fusion | flops 402653184 | bytes 6553600 | tf_op jit(solution)/shard_map/pqa,pqb->pab/dot_general | solution.py:217
  21.7 0.0 copy-start.5
  21.7 0.0 copy-start.3
  21.7 0.0 copy-start.4
  21.8 0.0 collective-permute-done.2.refs_0_
  21.8 0.1 collective-permute-start.7
  21.9 0.0 collective-permute-done.5.refs_3_
  21.9 0.5 collective-permute-start.6
  22.4 0.0 collective-permute-done.4.refs_2_
  22.4 1.2 %collective-permute-start.8 = (bf16[640,128]{1,0:T(8,128)(2,1)S(1)}, bf16[640,128]{1,0:T(8,128)(2,1)S(1)}, u32[]{:S(2)}, u32[]{:S(2)}) collective-permute-start(bf16[640,128]{1,0:T(8,128)(2,1)S(1)} %collective-permute-done.4.refs_2_), channel_id=1, source_target_pairs={{0,1},{1,0},{2,3},{3,2},{4,5},{5,4},{6,7},{7,6},{8,9},{9,8},{10,11... | collective-permute-start | bytes 491528 | tf_op jit(solution)/shard_map/ppermute | solution.py:227
  23.6 0.0 copy-done.2
  23.6 0.4 fusion.4
  24.0 0.0 collective-permute-done.1.x_far
  24.0 0.1 collective-permute-start.9
  24.1 0.1 pad_add_fusion.where
  24.2 1.2 %collective-permute-done.9.refs_7_ = bf16[320,128]{1,0:T(8,128)(2,1)S(1)} collective-permute-done((bf16[320,128]{1,0:T(8,128)(2,1)S(1)}, bf16[320,128]{1,0:T(8,128)(2,1)S(1)}, u32[]{:S(2)}, u32[]{:S(2)}) %collective-permute-start.9) | collective-permute-done | bytes 81952 | tf_op jit(solution)/shard_map/ppermute | solution.py:227
  25.4 0.0 collective-permute-done.7.refs_5_
  25.4 0.0 collective-permute-done.6.refs_4_
  25.4 0.0 collective-permute-done.8.refs_6_
  25.4 0.0 collective-permute-done.x_near
  25.4 0.0 copy-done
  25.4 0.0 copy-done.1
  25.4 3.2 %couple.1 = (bf16[4,128,128]{2,1,0:T(8,128)(2,1)S(1)}, bf16[2,128,128]{2,1,0:T(8,128)(2,1)S(1)}, f32[2,128,128]{2,1,0:T(8,128)S(1)}) custom-call(s32[4]{0:T(128)S(1)} %pad_add_fusion.where, bf16[2064,128]{1,0:T(8,128)(2,1)S(1)} %collective-permute-done.x_near, bf16[1040,128]{1,0:T(8,128)(2,1)S(1)} %copy-done, ...), custom_call_target="tpu_custom_call" | custom-call | bytes 12000000 | tf_op jit(solution)/shard_map/couple/pallas_call | solution.py:229
  28.7 1.3 %collective-permute-start.10 = (bf16[4,128,128]{2,1,0:T(8,128)(2,1)S(1)}, bf16[4,128,128]{2,1,0:T(8,128)(2,1)S(1)}, u32[]{:S(2)}, u32[]{:S(2)}) collective-permute-start(bf16[4,128,128]{2,1,0:T(8,128)(2,1)S(1)} %get-tuple-element.16), channel_id=1, source_target_pairs={{0,24},{8,0},{16,8},{24,16},{1,9},{9,17},{17,25},{25,1},{2,26},{10... | collective-permute-start | bytes 393224 | tf_op jit(solution)/shard_map/ppermute | solution.py:254
  30.0 2.5 %collective-permute-start.11 = (bf16[2,128,128]{2,1,0:T(8,128)(2,1)S(1)}, bf16[2,128,128]{2,1,0:T(8,128)(2,1)S(1)}, u32[]{:S(2)}, u32[]{:S(2)}) collective-permute-start(bf16[2,128,128]{2,1,0:T(8,128)(2,1)S(1)} %get-tuple-element.17), channel_id=1, source_target_pairs={{0,16},{8,24},{16,0},{24,8},{1,17},{9,25},{17,1},{25,9},{2,18},{10... | collective-permute-start | bytes 196616 | tf_op jit(solution)/shard_map/ppermute | solution.py:255
  32.4 0.4 fusion.local
  32.8 2.6 %collective-permute-done.11.far = bf16[2,128,128]{2,1,0:T(8,128)(2,1)S(1)} collective-permute-done((bf16[2,128,128]{2,1,0:T(8,128)(2,1)S(1)}, bf16[2,128,128]{2,1,0:T(8,128)(2,1)S(1)}, u32[]{:S(2)}, u32[]{:S(2)}) %collective-permute-start.11) | collective-permute-done | bytes 65568 | tf_op jit(solution)/shard_map/ppermute | solution.py:255
  35.5 0.0 collective-permute-done.10.near
  35.5 0.6 %settle.1 = (f32[2,128,128]{2,1,0:T(8,128)S(1)}, f32[2,128,128]{2,1,0:T(8,128)S(1)}) custom-call(s32[4]{0:T(128)S(1)} %pad_add_fusion.where, f32[4,128,128]{2,1,0:T(8,128)S(1)} %fusion.local, bf16[4,128,128]{2,1,0:T(8,128)(2,1)S(1)} %collective-permute-done.10.near, bf16[2,128,128]{2,1,0:T(8,128)(2,1)S(1)} %collective-permute-done.11.far, ...), custom_call_target="tpu_custom_call" | custom-call | tf_op jit(solution)/shard_map/settle/pallas_call | solution.py:256
  36.1 2.1 %collective-permute-start.12 = (f32[2,128,128]{2,1,0:T(8,128)S(1)}, f32[2,128,128]{2,1,0:T(8,128)S(1)}, u32[]{:S(2)}, u32[]{:S(2)}) collective-permute-start(f32[2,128,128]{2,1,0:T(8,128)S(1)} %get-tuple-element.20), channel_id=1, source_target_pairs={{0,1},{1,0},{2,3},{3,2},{4,5},{5,4},{6,7},{7,6},{8,9},{9,8},{10,11... | collective-permute-start | bytes 393224 | tf_op jit(solution)/shard_map/ppermute | solution.py:264
  38.1 1.0 %collective-permute-done.12 = f32[2,128,128]{2,1,0:T(8,128)S(1)} collective-permute-done((f32[2,128,128]{2,1,0:T(8,128)S(1)}, f32[2,128,128]{2,1,0:T(8,128)S(1)}, u32[]{:S(2)}, u32[]{:S(2)}) %collective-permute-start.12) | collective-permute-done | bytes 131104 | tf_op jit(solution)/shard_map/ppermute | solution.py:264
  39.1 3.4 %collective-permute-start.13 = (f32[2,128,128]{2,1,0:T(8,128)S(1)}, f32[2,128,128]{2,1,0:T(8,128)S(1)}, u32[]{:S(2)}, u32[]{:S(2)}) collective-permute-start(f32[2,128,128]{2,1,0:T(8,128)S(1)} %add.33), channel_id=1, source_target_pairs={{0,2},{1,7},{2,0},{3,5},{4,6},{5,3},{6,4},{7,1},{8,10},{9,15},{10,... | collective-permute-start | bytes 393224 | tf_op jit(solution)/shard_map/ppermute | solution.py:265
  42.5 2.4 %collective-permute-done.13 = f32[2,128,128]{2,1,0:T(8,128)S(1)} collective-permute-done((f32[2,128,128]{2,1,0:T(8,128)S(1)}, f32[2,128,128]{2,1,0:T(8,128)S(1)}, u32[]{:S(2)}, u32[]{:S(2)}) %collective-permute-start.13) | collective-permute-done | bytes 131104 | tf_op jit(solution)/shard_map/ppermute | solution.py:265
  44.8 0.4 collective-permute-start.14
  45.2 3.5 %collective-permute-done.14 = f32[2,128,128]{2,1,0:T(8,128)S(1)} collective-permute-done((f32[2,128,128]{2,1,0:T(8,128)S(1)}, f32[2,128,128]{2,1,0:T(8,128)S(1)}, u32[]{:S(2)}, u32[]{:S(2)}) %collective-permute-start.14) | collective-permute-done | bytes 131104 | tf_op jit(solution)/shard_map/ppermute | solution.py:266
  48.8 2.5 %collective-permute-start.15 = (f32[2,128,128]{2,1,0:T(8,128)S(1)}, f32[2,128,128]{2,1,0:T(8,128)S(1)}, u32[]{:S(2)}, u32[]{:S(2)}) collective-permute-start(f32[2,128,128]{2,1,0:T(8,128)S(1)} %add.35), channel_id=1, source_target_pairs={{0,1},{1,0},{2,3},{3,2},{4,5},{5,4},{6,7},{7,6},{8,9},{9,8},{10,11... | collective-permute-start | bytes 393224 | tf_op jit(solution)/shard_map/ppermute | solution.py:267
  51.2 0.0 copy-done.5
  51.2 0.1 iota_compare_fusion
  51.3 0.9 %collective-permute-done.15 = f32[2,128,128]{2,1,0:T(8,128)S(1)} collective-permute-done((f32[2,128,128]{2,1,0:T(8,128)S(1)}, f32[2,128,128]{2,1,0:T(8,128)S(1)}, u32[]{:S(2)}, u32[]{:S(2)}) %collective-permute-start.15) | collective-permute-done | bytes 131104 | tf_op jit(solution)/shard_map/ppermute | solution.py:267
  52.2 0.0 copy-done.3
  52.2 0.0 copy-done.4
  52.2 0.9 %fusion.2 = f32[4,128,128]{2,1,0:T(8,128)} fusion(f32[2,128,128]{2,1,0:T(8,128)S(1)} %collective-permute-done.15, f32[2,128,128]{2,1,0:T(8,128)S(1)} %add.35, bf16[4,128,128]{2,1,0:T(8,128)(2,1)S(1)} %copy-done.2, f32[4]{0:T(128)S(1)} %copy-done.4, f32[4,128]{1,0:T(4,128)S(1)} %copy-done.3, pred[]{:T(512)S(6)} %eq.3, pred[4,128]{1,0:T(4,128)(4,1)S(1)} %iota_compare_fusion), kind=kLoop, calls=%fused_computation.4 | loop fusion | flops 655360 | bytes 657937 | tf_op jit(solution)/shard_map/jit(_where)/select_n | solution.py:273
  (4 shorter events, 0.1 us)
Async XLA Ops:
  2.2 11.3 %collective-permute-start.3 = (bf16[640,128]{1,0:T(8,128)(2,1)}, bf16[640,128]{1,0:T(8,128)(2,1)S(1)}, u32[]{:S(2)}, u32[]{:S(2)}) collective-permute-start(bf16[640,128]{1,0:T(8,128)(2,1)} %get-tuple-element.15.z_full), channel_id=1, source_target_pairs={{0,64},{32,96},{64,128},{96,160},{128,192},{160,224},{192,0},{224,... | collective-permute-start | bytes 491528 | tf_op jit(solution)/shard_map/ppermute | solution.py:213
  9.1 12.6 %collective-permute-start.2 = (bf16[640,128]{1,0:T(8,128)(2,1)}, bf16[640,128]{1,0:T(8,128)(2,1)S(1)}, u32[]{:S(2)}, u32[]{:S(2)}) collective-permute-start(bf16[640,128]{1,0:T(8,128)(2,1)} %get-tuple-element.15.z_full), channel_id=1, source_target_pairs={{0,32},{32,64},{64,96},{96,128},{128,160},{160,192},{192,224},{224... | collective-permute-start | bytes 491528 | tf_op jit(solution)/shard_map/ppermute | solution.py:212
  9.9 14.2 %collective-permute-start.1 = (bf16[1040,128]{1,0:T(8,128)(2,1)}, bf16[1040,128]{1,0:T(8,128)(2,1)S(1)}, u32[]{:S(2)}, u32[]{:S(2)}) collective-permute-start(bf16[1040,128]{1,0:T(8,128)(2,1)} %get-tuple-element.14.x_own), channel_id=1, source_target_pairs={{0,16},{8,24},{16,0},{24,8},{1,17},{9,25},{17,1},{25,9},{2,18},{10... | collective-permute-start | bytes 798728 | tf_op jit(solution)/shard_map/ppermute | solution.py:215
  12.6 12.8 %collective-permute-start = (bf16[2064,128]{1,0:T(8,128)(2,1)}, bf16[2064,128]{1,0:T(8,128)(2,1)S(1)}, u32[]{:S(2)}, u32[]{:S(2)}) collective-permute-start(bf16[2064,128]{1,0:T(8,128)(2,1)} %get-tuple-element.13), channel_id=1, source_target_pairs={{0,8},{8,16},{16,24},{24,0},{1,25},{9,1},{17,9},{25,17},{2,10},{10... | collective-permute-start | bytes 1585160 | tf_op jit(solution)/shard_map/ppermute | solution.py:214
  13.5 10.1 %copy-start.2 = (bf16[4,128,128]{2,1,0:T(8,128)(2,1)S(1)}, bf16[4,128,128]{2,1,0:T(8,128)(2,1)}, u32[]{:S(2)}) copy-start(bf16[4,128,128]{2,1,0:T(8,128)(2,1)} %amp.1) | copy-start | bytes 393220
  13.5 11.9 %copy-start = (bf16[1040,128]{1,0:T(8,128)(2,1)S(1)}, bf16[1040,128]{1,0:T(8,128)(2,1)}, u32[]{:S(2)}) copy-start(bf16[1040,128]{1,0:T(8,128)(2,1)} %get-tuple-element.14.x_own) | copy-start | bytes 798724
  13.5 11.9 %copy-start.1 = (bf16[640,128]{1,0:T(8,128)(2,1)S(1)}, bf16[640,128]{1,0:T(8,128)(2,1)}, u32[]{:S(2)}) copy-start(bf16[640,128]{1,0:T(8,128)(2,1)} %get-tuple-element.15.z_full) | copy-start | bytes 491524
  13.5 8.3 %collective-permute-start.5 = (bf16[320,128]{1,0:T(8,128)(2,1)S(1)}, bf16[320,128]{1,0:T(8,128)(2,1)S(1)}, u32[]{:S(2)}, u32[]{:S(2)}) collective-permute-start(bf16[320,128]{1,0:T(8,128)(2,1)S(1)} %constant_dynamic-slice_fusion), channel_id=1, source_target_pairs={{0,64},{32,96},{64,128},{96,160},{128,192},{160,224},{192,0},{224,... | collective-permute-start | bytes 245768 | tf_op jit(solution)/shard_map/ppermute | solution.py:225
  17.8 4.6 %collective-permute-start.4 = (bf16[640,128]{1,0:T(8,128)(2,1)S(1)}, bf16[640,128]{1,0:T(8,128)(2,1)S(1)}, u32[]{:S(2)}, u32[]{:S(2)}) collective-permute-start(bf16[640,128]{1,0:T(8,128)(2,1)S(1)} %collective-permute-done.3.refs_1_), channel_id=1, source_target_pairs={{0,32},{32,64},{64,96},{96,128},{128,160},{160,192},{192,224},{224... | collective-permute-start | bytes 491528 | tf_op jit(solution)/shard_map/ppermute | solution.py:223
  21.7 29.5 %copy-start.5 = (s32[4]{0:T(128)S(1)}, s32[4]{0:T(128)}, u32[]{:S(2)}) copy-start(s32[4]{0:T(128)} %param.13) | copy-start | bytes 52
  21.7 30.5 %copy-start.3 = (f32[4,128]{1,0:T(4,128)S(1)}, f32[4,128]{1,0:T(4,128)}, u32[]{:S(2)}) copy-start(f32[4,128]{1,0:T(4,128)} %param.11) | copy-start | bytes 6148
  21.7 30.5 %copy-start.4 = (f32[4]{0:T(128)S(1)}, f32[4]{0:T(128)}, u32[]{:S(2)}) copy-start(f32[4]{0:T(128)} %param.12) | copy-start | bytes 52
  21.8 3.6 %collective-permute-start.7 = (bf16[640,128]{1,0:T(8,128)(2,1)S(1)}, bf16[640,128]{1,0:T(8,128)(2,1)S(1)}, u32[]{:S(2)}, u32[]{:S(2)}) collective-permute-start(bf16[640,128]{1,0:T(8,128)(2,1)S(1)} %collective-permute-done.3.refs_1_), channel_id=1, source_target_pairs={{0,1},{1,0},{2,3},{3,2},{4,5},{5,4},{6,7},{7,6},{8,9},{9,8},{10,11... | collective-permute-start | bytes 491528 | tf_op jit(solution)/shard_map/ppermute | solution.py:227
  21.9 3.5 %collective-permute-start.6 = (bf16[640,128]{1,0:T(8,128)(2,1)S(1)}, bf16[640,128]{1,0:T(8,128)(2,1)S(1)}, u32[]{:S(2)}, u32[]{:S(2)}) collective-permute-start(bf16[640,128]{1,0:T(8,128)(2,1)S(1)} %collective-permute-done.2.refs_0_), channel_id=1, source_target_pairs={{0,1},{1,0},{2,3},{3,2},{4,5},{5,4},{6,7},{7,6},{8,9},{9,8},{10,11... | collective-permute-start | bytes 491528 | tf_op jit(solution)/shard_map/ppermute | solution.py:227
  22.4 3.0 %collective-permute-start.8 = (bf16[640,128]{1,0:T(8,128)(2,1)S(1)}, bf16[640,128]{1,0:T(8,128)(2,1)S(1)}, u32[]{:S(2)}, u32[]{:S(2)}) collective-permute-start(bf16[640,128]{1,0:T(8,128)(2,1)S(1)} %collective-permute-done.4.refs_2_), channel_id=1, source_target_pairs={{0,1},{1,0},{2,3},{3,2},{4,5},{5,4},{6,7},{7,6},{8,9},{9,8},{10,11... | collective-permute-start | bytes 491528 | tf_op jit(solution)/shard_map/ppermute | solution.py:227
  24.0 1.4 %collective-permute-start.9 = (bf16[320,128]{1,0:T(8,128)(2,1)S(1)}, bf16[320,128]{1,0:T(8,128)(2,1)S(1)}, u32[]{:S(2)}, u32[]{:S(2)}) collective-permute-start(bf16[320,128]{1,0:T(8,128)(2,1)S(1)} %collective-permute-done.5.refs_3_), channel_id=1, source_target_pairs={{0,1},{1,0},{2,3},{3,2},{4,5},{5,4},{6,7},{7,6},{8,9},{9,8},{10,11... | collective-permute-start | bytes 245768 | tf_op jit(solution)/shard_map/ppermute | solution.py:227
  28.7 6.8 %collective-permute-start.10 = (bf16[4,128,128]{2,1,0:T(8,128)(2,1)S(1)}, bf16[4,128,128]{2,1,0:T(8,128)(2,1)S(1)}, u32[]{:S(2)}, u32[]{:S(2)}) collective-permute-start(bf16[4,128,128]{2,1,0:T(8,128)(2,1)S(1)} %get-tuple-element.16), channel_id=1, source_target_pairs={{0,24},{8,0},{16,8},{24,16},{1,9},{9,17},{17,25},{25,1},{2,26},{10... | collective-permute-start | bytes 393224 | tf_op jit(solution)/shard_map/ppermute | solution.py:254
  30.0 5.5 %collective-permute-start.11 = (bf16[2,128,128]{2,1,0:T(8,128)(2,1)S(1)}, bf16[2,128,128]{2,1,0:T(8,128)(2,1)S(1)}, u32[]{:S(2)}, u32[]{:S(2)}) collective-permute-start(bf16[2,128,128]{2,1,0:T(8,128)(2,1)S(1)} %get-tuple-element.17), channel_id=1, source_target_pairs={{0,16},{8,24},{16,0},{24,8},{1,17},{9,25},{17,1},{25,9},{2,18},{10... | collective-permute-start | bytes 196616 | tf_op jit(solution)/shard_map/ppermute | solution.py:255
  36.1 3.0 %collective-permute-start.12 = (f32[2,128,128]{2,1,0:T(8,128)S(1)}, f32[2,128,128]{2,1,0:T(8,128)S(1)}, u32[]{:S(2)}, u32[]{:S(2)}) collective-permute-start(f32[2,128,128]{2,1,0:T(8,128)S(1)} %get-tuple-element.20), channel_id=1, source_target_pairs={{0,1},{1,0},{2,3},{3,2},{4,5},{5,4},{6,7},{7,6},{8,9},{9,8},{10,11... | collective-permute-start | bytes 393224 | tf_op jit(solution)/shard_map/ppermute | solution.py:264
  39.1 5.7 %collective-permute-start.13 = (f32[2,128,128]{2,1,0:T(8,128)S(1)}, f32[2,128,128]{2,1,0:T(8,128)S(1)}, u32[]{:S(2)}, u32[]{:S(2)}) collective-permute-start(f32[2,128,128]{2,1,0:T(8,128)S(1)} %add.33), channel_id=1, source_target_pairs={{0,2},{1,7},{2,0},{3,5},{4,6},{5,3},{6,4},{7,1},{8,10},{9,15},{10,... | collective-permute-start | bytes 393224 | tf_op jit(solution)/shard_map/ppermute | solution.py:265
  44.8 3.9 %collective-permute-start.14 = (f32[2,128,128]{2,1,0:T(8,128)S(1)}, f32[2,128,128]{2,1,0:T(8,128)S(1)}, u32[]{:S(2)}, u32[]{:S(2)}) collective-permute-start(f32[2,128,128]{2,1,0:T(8,128)S(1)} %add.34), channel_id=1, source_target_pairs={{0,6},{1,3},{2,4},{3,1},{4,2},{5,7},{6,0},{7,5},{8,14},{9,11},{10,... | collective-permute-start | bytes 393224 | tf_op jit(solution)/shard_map/ppermute | solution.py:266
  48.8 3.5 %collective-permute-start.15 = (f32[2,128,128]{2,1,0:T(8,128)S(1)}, f32[2,128,128]{2,1,0:T(8,128)S(1)}, u32[]{:S(2)}, u32[]{:S(2)}) collective-permute-start(f32[2,128,128]{2,1,0:T(8,128)S(1)} %add.35), channel_id=1, source_target_pairs={{0,1},{1,0},{2,3},{3,2},{4,5},{5,4},{6,7},{7,6},{8,9},{9,8},{10,11... | collective-permute-start | bytes 393224 | tf_op jit(solution)/shard_map/ppermute | solution.py:267
